TPU v7x, 128 devices: a whole 4x4x4 slice. The times are simulated.
128 devices in a mesh: seq: 32 (over x, z, core), dp: 4 (over y).
Axes of the slice: x: 4, y: 4, z: 4, core: 2. Of those that a mesh axis runs over, the one named last changes fastest.
Arguments:
- tokens: bfloat16 [4, 6144, 640], P('dp', 'seq'), may hold values from -6 to 6
- lengths: int32 [4, 2], P('dp'), may hold values from 2048 to 4096, as said below
- w_query: bfloat16 [640, 1024], replicated, may hold values from -0.25 to 0.25
- w_key: bfloat16 [640, 256], replicated, may hold values from -0.25 to 0.25
- w_value: bfloat16 [640, 256], replicated, may hold values from -0.25 to 0.25
- w_output: bfloat16 [1024, 640], replicated, may hold values from -1.5 to 1.5
- w_gate: bfloat16 [640, 2048], replicated, may hold values from -0.25 to 0.25
- w_up: bfloat16 [640, 2048], replicated, may hold values from -0.25 to 0.25
- w_down: bfloat16 [2048, 640], replicated, may hold values from -0.125 to 0.125
- gain_attn: float32 [640], replicated, may hold values from 0.1 to 1.9
- gain_mlp: float32 [640], replicated, may hold values from 0.1 to 1.9
- out_grad: bfloat16 [4, 6144, 640], P('dp', 'seq'), may hold values from -6 to 6
Outputs:
- block_out: bfloat16 [4, 6144, 640], P('dp', 'seq')
- shared_kv: bfloat16 [4, 6144, 512], P('dp', 'seq')
- input_grad: float32 [4, 6144, 640], P('dp', 'seq')
- grad_query: float32 [640, 1024], replicated
- grad_key: float32 [640, 256], replicated
- grad_value: float32 [640, 256], replicated
- grad_proj: float32 [1024, 640], replicated
- grad_gate: float32 [640, 2048], replicated
- grad_up: float32 [640, 2048], replicated
- grad_down: float32 [2048, 640], replicated
- grad_gain_attn: float32 [640], replicated
- grad_gain_mlp: float32 [640], replicated
Inputs may be any that keep to these rules, and one draw needn't show every extreme that they name: `lengths`: in each row, 1 entries are 2048 and 1 are 4096, in an order drawn for each row.
All inputs are finite; a program needn't handle non-finite values.
Results may differ from a plain program's by a relative error of at most 0.015.
Values may be sent and summed in bfloat16 or wider, within the bound.
No kernel may reach another device: no remote copies, remote signals or barrier semaphores. Data moves between devices by JAX's collectives and lax.ppermute only.
A program may use at most 128 MiB of HBM per device.

v0:
```python
import jax
import jax.numpy as jnp
from jax import lax
from jax.sharding import PartitionSpec as P

WINDOW = 1024
SHORT_LEN = 2048
PAIRS = 1


epsilon = 1e-06
theta_base = 10000.0
masked_score = -1e30


def passed_along(array, axis, by):
    length = lax.axis_size(axis)
    pairs = [(i, i + by) for i in range(length) if 0 <= i + by < length]
    return lax.ppermute(array, axis, pairs)


def matmul(left, right):
    return jnp.dot(left, right, preferred_element_type=jnp.float32)


def outer_sum(left, right):
    return lax.dot_general(
        left, right, (((0,), (0,)), ((), ())), preferred_element_type=jnp.float32
    )


def times_transpose(left, right):
    return lax.dot_general(
        left, right, (((1,), (1,)), ((), ())), preferred_element_type=jnp.float32
    )


def rms_scale(values):
    return lax.rsqrt(jnp.mean(values * values, axis=-1, keepdims=True) + epsilon)


def rotary_tables(positions, head_dim):
    half_dim = head_dim // 2
    frequency = theta_base ** (-(jnp.arange(half_dim, dtype=jnp.float32) * 2.0 / head_dim))
    angles = positions.astype(jnp.float32)[:, None] * frequency[None, :]
    cosine_half = jnp.cos(angles)
    sine_half = jnp.sin(angles)
    return (
        jnp.concatenate([cosine_half, cosine_half], axis=1),
        jnp.concatenate([sine_half, sine_half], axis=1),
    )


def rotate(values, cosine_table, sine_table):
    half_dim = values.shape[-1] // 2
    turned = jnp.concatenate([-values[..., half_dim:], values[..., :half_dim]], axis=-1)
    return values * cosine_table + turned * sine_table


def rotate_back(grads, cosine_table, sine_table):
    half_dim = grads.shape[-1] // 2
    sined = grads * sine_table
    turned = jnp.concatenate([sined[..., half_dim:], -sined[..., :half_dim]], axis=-1)
    return grads * cosine_table + turned


def token_layout(seq_lengths, device, seq_count, slot_count):
    pieces = seq_lengths // seq_count
    offsets = jnp.cumsum(pieces) - pieces
    slot_index = jnp.arange(slot_count, dtype=jnp.int32)
    member = jnp.sum((slot_index[:, None] >= offsets[None, :]).astype(jnp.int32), axis=1) - 1
    onehot = (member[:, None] == jnp.arange(seq_lengths.shape[0], dtype=jnp.int32)[None, :]).astype(
        jnp.int32
    )
    own_piece = jnp.sum(onehot * pieces[None, :], axis=1)
    own_offset = jnp.sum(onehot * offsets[None, :], axis=1)
    return (offsets, device * own_piece + slot_index - own_offset)


def kind_offsets(flags, offsets, count):
    ranks = jnp.cumsum(flags.astype(jnp.int32)) - 1
    chosen = flags[None, :] & (ranks[None, :] == jnp.arange(count, dtype=jnp.int32)[:, None])
    return jnp.sum(chosen.astype(jnp.int32) * offsets[None, :], axis=1)


def take_members(stack, starts, first, width):
    rows = stack.shape[0] - first
    return jnp.stack(
        [lax.dynamic_slice(stack, (first, starts[0], 0), (rows, width, stack.shape[2]))]
    )


def take_rows(values, starts, width):
    return jnp.stack([lax.dynamic_slice_in_dim(values, starts[0], width, 0)])


def put_rows(target, pieces, starts):
    index = (starts[0],) + (0,) * (target.ndim - 1)
    target = lax.dynamic_update_slice(target, pieces[0], index)
    return target


def put_window(target, pieces, starts, first):
    target = lax.dynamic_update_slice(target, pieces[0], (first, starts[0], 0))
    return target


def shards(
    tokens,
    lengths,
    w_query,
    w_key,
    w_value,
    w_output,
    w_gate,
    w_up,
    w_down,
    gain_attn,
    gain_mlp,
    out_grad,
):
    seq_count = lax.axis_size("seq")
    seq_index = lax.axis_index("seq")
    slot_count = tokens.shape[1]
    head_dim = w_key.shape[1]
    head_count = w_query.shape[1] // head_dim
    piece_short = slot_count // (3 * PAIRS)
    piece_long = 2 * piece_short
    reach = WINDOW // piece_short
    half_reach = reach // 2
    score_scale = head_dim ** (-0.5)
    seq_lengths = lengths[0]
    offsets, position = token_layout(seq_lengths, seq_index, seq_count, slot_count)
    is_short = seq_lengths == SHORT_LEN
    short_starts = kind_offsets(is_short, offsets, PAIRS)
    long_starts = kind_offsets(jnp.logical_not(is_short), offsets, PAIRS)
    cosine_table, sine_table = rotary_tables(position, head_dim)
    tokens_wide = tokens[0].astype(jnp.float32)
    scale_first = rms_scale(tokens_wide)
    unit_first = tokens_wide * scale_first
    normed = (unit_first * gain_attn).astype(jnp.bfloat16)
    query_raw = matmul(normed, w_query)
    key_raw = matmul(normed, w_key)
    value_raw = matmul(normed, w_value)
    queries = rotate(
        query_raw.reshape(slot_count, head_count, head_dim),
        cosine_table[:, None, :],
        sine_table[:, None, :],
    ).astype(jnp.bfloat16)
    key_rows = rotate(key_raw, cosine_table, sine_table).astype(jnp.bfloat16)
    own_kv = jnp.concatenate([key_rows, value_raw.astype(jnp.bfloat16)], axis=1)

    def hop_forward(carry, unused):
        moved = passed_along(carry, "seq", 1)
        return (moved, moved)

    unused_last, behind = lax.scan(hop_forward, own_kv, None, length=reach)
    window_stack = jnp.concatenate([behind[::-1], own_kv[None]], axis=0)
    short_kv = take_members(window_stack, short_starts, 0, piece_short)
    long_kv = take_members(window_stack, long_starts, reach - half_reach, piece_long)

    def kind_mask(width, piece_count):
        query_position = seq_index * width + jnp.arange(width, dtype=jnp.int32)
        key_position = (seq_index - piece_count + 1) * width + jnp.arange(
            piece_count * width, dtype=jnp.int32
        )
        distance = query_position[:, None] - key_position[None, :]
        return (key_position[None, :] >= 0) & (distance >= 0) & (distance < WINDOW)

    def kind_scores(query_kind, key_kind, allowed):
        raw_scores = (
            jnp.einsum("pqhd,pkd->phqk", query_kind, key_kind, preferred_element_type=jnp.float32)
            * score_scale
        )
        return jnp.where(allowed[None, None], raw_scores, masked_score)

    def split_kind(kv_kind):
        flat = kv_kind.reshape(PAIRS, -1, 2 * head_dim)
        return (flat[:, :, :head_dim], flat[:, :, head_dim:])

    def attend_kind(query_kind, kv_kind, allowed):
        key_kind, value_kind = split_kind(kv_kind)
        scores = kind_scores(query_kind, key_kind, allowed)
        row_max = jnp.max(scores, axis=-1, keepdims=True)
        exponent = jnp.exp(scores - row_max)
        row_total = jnp.sum(exponent, axis=-1, keepdims=True)
        attn_probs = exponent / row_total
        mixed_kind = jnp.einsum(
            "phqk,pkd->pqhd",
            attn_probs.astype(jnp.bfloat16),
            value_kind,
            preferred_element_type=jnp.float32,
        )
        return (mixed_kind, row_max, row_total)

    short_allowed = kind_mask(piece_short, reach + 1)
    long_allowed = kind_mask(piece_long, half_reach + 1)
    short_queries = take_rows(queries, short_starts, piece_short)
    long_queries = take_rows(queries, long_starts, piece_long)
    short_mixed, short_max, short_total = attend_kind(short_queries, short_kv, short_allowed)
    long_mixed, long_max, long_total = attend_kind(long_queries, long_kv, long_allowed)
    mixed = jnp.zeros((slot_count, head_count, head_dim), jnp.float32)
    mixed = put_rows(mixed, short_mixed, short_starts)
    mixed = put_rows(mixed, long_mixed, long_starts)
    mixed = mixed.reshape(slot_count, head_count * head_dim).astype(jnp.bfloat16)
    resid = tokens_wide + matmul(mixed, w_output)
    scale_second = rms_scale(resid)
    unit_second = resid * scale_second
    normed_mlp = (unit_second * gain_mlp).astype(jnp.bfloat16)
    gate = matmul(normed_mlp, w_gate)
    upward = matmul(normed_mlp, w_up)
    sigmoid_gate = jax.nn.sigmoid(gate)
    silu_gate = gate * sigmoid_gate
    act = (silu_gate * upward).astype(jnp.bfloat16)
    block_out = resid + matmul(act, w_down)
    grad_out = out_grad[0]
    grad_down = outer_sum(act, grad_out)
    grad_act = times_transpose(grad_out, w_down)
    grad_gate_in = (grad_act * upward * sigmoid_gate * (1.0 + gate * (1.0 - sigmoid_gate))).astype(
        jnp.bfloat16
    )
    grad_up_in = (grad_act * silu_gate).astype(jnp.bfloat16)
    grad_gatemat = outer_sum(normed_mlp, grad_gate_in)
    grad_upmat = outer_sum(normed_mlp, grad_up_in)
    grad_normed_mlp = times_transpose(grad_gate_in, w_gate) + times_transpose(grad_up_in, w_up)
    grad_gain_mlp = jnp.sum(grad_normed_mlp * unit_second, axis=0)
    scaled_second = grad_normed_mlp * gain_mlp
    grad_resid = grad_out.astype(jnp.float32) + scale_second * (
        scaled_second - unit_second * jnp.mean(scaled_second * unit_second, axis=-1, keepdims=True)
    )
    grad_branch = grad_resid.astype(jnp.bfloat16)
    grad_projmat = outer_sum(mixed, grad_branch)
    grad_mixed = times_transpose(grad_branch, w_output).astype(jnp.bfloat16)
    grad_mixed_heads = grad_mixed.reshape(slot_count, head_count, head_dim)

    def attend_kind_back(query_kind, kv_kind, allowed, max_kind, total_kind, grad_kind, width):
        key_kind, value_kind = split_kind(kv_kind)
        scores = kind_scores(query_kind, key_kind, allowed)
        attn_probs = jnp.exp(scores - max_kind) / total_kind
        probs_low = attn_probs.astype(jnp.bfloat16)
        grad_probs = jnp.einsum(
            "pqhd,pkd->phqk", grad_kind, value_kind, preferred_element_type=jnp.float32
        )
        grad_value_kind = jnp.einsum(
            "phqk,pqhd->pkd", probs_low, grad_kind, preferred_element_type=jnp.float32
        )
        inner = jnp.sum(attn_probs * grad_probs, axis=-1, keepdims=True)
        grad_scores = (attn_probs * (grad_probs - inner)).astype(jnp.bfloat16)
        grad_query_kind = (
            jnp.einsum("phqk,pkd->pqhd", grad_scores, key_kind, preferred_element_type=jnp.float32)
            * score_scale
        )
        grad_key_kind = (
            jnp.einsum(
                "phqk,pqhd->pkd", grad_scores, query_kind, preferred_element_type=jnp.float32
            )
            * score_scale
        )
        grad_kv_kind = jnp.concatenate([grad_key_kind, grad_value_kind], axis=2)
        return (grad_query_kind, grad_kv_kind.reshape(PAIRS, -1, width, 2 * head_dim))

    grad_short_queries, grad_short_kv = attend_kind_back(
        short_queries,
        short_kv,
        short_allowed,
        short_max,
        short_total,
        take_rows(grad_mixed_heads, short_starts, piece_short),
        piece_short,
    )
    grad_long_queries, grad_long_kv = attend_kind_back(
        long_queries,
        long_kv,
        long_allowed,
        long_max,
        long_total,
        take_rows(grad_mixed_heads, long_starts, piece_long),
        piece_long,
    )
    grad_queries = jnp.zeros((slot_count, head_count, head_dim), jnp.float32)
    grad_queries = put_rows(grad_queries, grad_short_queries, short_starts)
    grad_queries = put_rows(grad_queries, grad_long_queries, long_starts)
    grad_window = jnp.zeros((reach + 1, slot_count, 2 * head_dim), jnp.float32)
    grad_window = put_window(grad_window, grad_short_kv, short_starts, 0)
    grad_window = put_window(grad_window, grad_long_kv, long_starts, reach - half_reach)

    def hop_back(carry, incoming):
        moved = passed_along((carry + incoming).astype(jnp.bfloat16), "seq", -1).astype(jnp.float32)
        return (moved, None)

    returned_sum, unused_out = lax.scan(
        hop_back, jnp.zeros_like(grad_window[0]), grad_window[:reach]
    )
    grad_own = grad_window[reach] + returned_sum
    grad_key_raw = rotate_back(grad_own[:, :head_dim], cosine_table, sine_table).astype(
        jnp.bfloat16
    )
    grad_value_raw = grad_own[:, head_dim:].astype(jnp.bfloat16)
    grad_query_raw = rotate_back(grad_queries, cosine_table[:, None, :], sine_table[:, None, :])
    grad_query_raw = grad_query_raw.reshape(slot_count, head_count * head_dim).astype(jnp.bfloat16)
    grad_querymat = outer_sum(normed, grad_query_raw)
    grad_keymat = outer_sum(normed, grad_key_raw)
    grad_valuemat = outer_sum(normed, grad_value_raw)
    grad_normed = (
        times_transpose(grad_query_raw, w_query)
        + times_transpose(grad_key_raw, w_key)
        + times_transpose(grad_value_raw, w_value)
    )
    grad_gain_attn = jnp.sum(grad_normed * unit_first, axis=0)
    scaled_first = grad_normed * gain_attn
    input_grad = grad_resid + scale_first * (
        scaled_first - unit_first * jnp.mean(scaled_first * unit_first, axis=-1, keepdims=True)
    )
    totals = lax.psum(
        (
            grad_querymat,
            grad_keymat,
            grad_valuemat,
            grad_projmat,
            grad_gatemat,
            grad_upmat,
            grad_down,
            grad_gain_attn,
            grad_gain_mlp,
        ),
        ("seq", "dp"),
    )
    return (
        block_out.astype(jnp.bfloat16)[None],
        own_kv[None],
        input_grad[None],
        totals[0],
        totals[1],
        totals[2],
        totals[3],
        totals[4],
        totals[5],
        totals[6],
        totals[7],
        totals[8],
    )


def solution(mesh):
    in_specs = (
        P("dp", "seq", None),
        P("dp", None),
        P(),
        P(),
        P(),
        P(),
        P(),
        P(),
        P(),
        P(),
        P(),
        P("dp", "seq", None),
    )
    out_specs = (
        P("dp", "seq", None),
        P("dp", "seq", None),
        P("dp", "seq", None),
        P(),
        P(),
        P(),
        P(),
        P(),
        P(),
        P(),
        P(),
        P(),
    )
    return jax.shard_map(shards, mesh=mesh, in_specs=in_specs, out_specs=out_specs, check_vma=False)
```

profile of v0, /device:TPU:3, one launch (start us, length us, event | category | flops | bytes accessed | tf_op | source)
XLA Modules:
  0.0 755.5 jit_solution(13575206503907776974)
XLA Ops:
  19.1 2.0 convolution_convert_fusion.1
  22.6 2.4 copy.53
  30.1 165.0 %while.23 = (s32[]{:T(128)}, bf16[192,512]{1,0:T(8,128)(2,1)}, bf16[16,192,512]{2,1,0:T(8,128)(2,1)}, s32[]{:T(128)}) while((s32[]{:T(128)}, bf16[192,512]{1,0:T(8,128)(2,1)}, bf16[16,192,512]{2,1,0:T(8,128)(2,1)}, s32[]{:T(128)}) %tuple.65), condition=%wide.region_6.7_spmd, body=%wide.region_5.6_spmd.sunk | while | flops 2 | bytes 1572969 | solution.py:157
  30.1 4.1 collective-permute-start
  34.2 2.9 collective-permute-done
  38.4 4.3 collective-permute-start
  42.7 2.9 collective-permute-done
  47.0 4.3 collective-permute-start
  51.3 3.8 collective-permute-done
  56.5 3.4 collective-permute-start
  59.8 5.9 collective-permute-done
  69.0 7.4 collective-permute-done
  79.7 7.4 collective-permute-done
  90.4 7.4 collective-permute-done
  101.0 7.4 collective-permute-done
  111.7 7.4 collective-permute-done
  122.4 7.4 collective-permute-done
  133.0 7.4 collective-permute-done
  143.7 7.4 collective-permute-done
  154.4 7.4 collective-permute-done
  165.0 7.4 collective-permute-done
  175.7 7.4 collective-permute-done
  186.3 7.4 collective-permute-done
  195.1 3.9 rev.3
  214.1 3.0 dynamic_update_slice.23
  223.4 2.3 multiply_convert_fusion.1
  244.8 2.1 fusion.66
  246.9 3.2 fusion.103
  250.2 3.2 fusion.102
  254.9 2.2 copy.48
  263.0 3.6 broadcast_in_dim.55
  266.6 12.2 %dynamic_update_slice.26 = f32[17,192,512]{2,1,0:T(8,128)} dynamic-update-slice(f32[17,192,512]{2,1,0:T(8,128)} %broadcast_in_dim.55, f32[17,64,512]{2,1,0:T(8,128)} %pad_maximum_fusion.1, s32[]{:T(128)} %constant.40.clone.1, s32[]{:T(128)S(6)} %select_n.42, s32[]{:T(128)} %constant.40.clone.1) | dynamic-update-slice | bytes 4456452 | tf_op jit(solution)/shard_map/dynamic_update_slice | solution.py:104
  278.8 11.6 %dynamic_update_slice.27 = f32[17,192,512]{2,1,0:T(8,128)} dynamic-update-slice(f32[17,192,512]{2,1,0:T(8,128)} %dynamic_update_slice.26, f32[9,128,512]{2,1,0:T(8,128)} %pad_maximum_fusion, s32[]{:T(128)} %constant.109.clone.1, s32[]{:T(128)S(6)} %select_n.44, s32[]{:T(128)} %constant.40.clone.1) | dynamic-update-slice | bytes 4718596 | tf_op jit(solution)/shard_map/dynamic_update_slice | solution.py:104
  290.4 6.5 slice.80
  296.9 176.1 %while.24 = (s32[]{:T(128)}, f32[192,512]{1,0:T(8,128)S(1)}, f32[16,192,512]{2,1,0:T(8,128)}, s32[]{:T(128)}, s32[]{:T(128)}) while((s32[]{:T(128)}, f32[192,512]{1,0:T(8,128)S(1)}, f32[16,192,512]{2,1,0:T(8,128)}, s32[]{:T(128)}, s32[]{:T(128)}) %tuple.68), condition=%wide.region_20.21_spmd.clone, body=%wide.region_19.20_spmd.clone.sunk | while | flops 393219 | bytes 2359411 | solution.py:291
  297.9 8.2 %collective-permute-start.1 = (bf16[192,512]{1,0:T(8,128)(2,1)S(1)}, bf16[192,512]{1,0:T(8,128)(2,1)}, u32[]{:S(2)}, u32[]{:S(2)}) collective-permute-start(bf16[192,512]{1,0:T(8,128)(2,1)S(1)} %fusion.142), channel_id=1, source_target_pairs={{4,0},{8,4},{12,8},{16,12},{20,16},{24,20},{28,24},{32,28},{36,32}... | collective-permute-start | bytes 589832 | tf_op jit(solution)/shard_map/while/body/eval_jaxpr/ppermute | solution.py:19
  309.3 3.9 collective-permute-start.1
  313.2 3.2 collective-permute-done.1
  318.5 6.0 collective-permute-start.1
  327.7 8.0 %collective-permute-start.1 = (bf16[192,512]{1,0:T(8,128)(2,1)S(1)}, bf16[192,512]{1,0:T(8,128)(2,1)}, u32[]{:S(2)}, u32[]{:S(2)}) collective-permute-start(bf16[192,512]{1,0:T(8,128)(2,1)S(1)} %fusion.142), channel_id=1, source_target_pairs={{4,0},{8,4},{12,8},{16,12},{20,16},{24,20},{28,24},{32,28},{36,32}... | collective-permute-start | bytes 589832 | tf_op jit(solution)/shard_map/while/body/eval_jaxpr/ppermute | solution.py:19
  339.0 8.0 %collective-permute-start.1 = (bf16[192,512]{1,0:T(8,128)(2,1)S(1)}, bf16[192,512]{1,0:T(8,128)(2,1)}, u32[]{:S(2)}, u32[]{:S(2)}) collective-permute-start(bf16[192,512]{1,0:T(8,128)(2,1)S(1)} %fusion.142), channel_id=1, source_target_pairs={{4,0},{8,4},{12,8},{16,12},{20,16},{24,20},{28,24},{32,28},{36,32}... | collective-permute-start | bytes 589832 | tf_op jit(solution)/shard_map/while/body/eval_jaxpr/ppermute | solution.py:19
  350.2 8.0 %collective-permute-start.1 = (bf16[192,512]{1,0:T(8,128)(2,1)S(1)}, bf16[192,512]{1,0:T(8,128)(2,1)}, u32[]{:S(2)}, u32[]{:S(2)}) collective-permute-start(bf16[192,512]{1,0:T(8,128)(2,1)S(1)} %fusion.142), channel_id=1, source_target_pairs={{4,0},{8,4},{12,8},{16,12},{20,16},{24,20},{28,24},{32,28},{36,32}... | collective-permute-start | bytes 589832 | tf_op jit(solution)/shard_map/while/body/eval_jaxpr/ppermute | solution.py:19
  361.5 8.0 %collective-permute-start.1 = (bf16[192,512]{1,0:T(8,128)(2,1)S(1)}, bf16[192,512]{1,0:T(8,128)(2,1)}, u32[]{:S(2)}, u32[]{:S(2)}) collective-permute-start(bf16[192,512]{1,0:T(8,128)(2,1)S(1)} %fusion.142), channel_id=1, source_target_pairs={{4,0},{8,4},{12,8},{16,12},{20,16},{24,20},{28,24},{32,28},{36,32}... | collective-permute-start | bytes 589832 | tf_op jit(solution)/shard_map/while/body/eval_jaxpr/ppermute | solution.py:19
  372.8 8.0 %collective-permute-start.1 = (bf16[192,512]{1,0:T(8,128)(2,1)S(1)}, bf16[192,512]{1,0:T(8,128)(2,1)}, u32[]{:S(2)}, u32[]{:S(2)}) collective-permute-start(bf16[192,512]{1,0:T(8,128)(2,1)S(1)} %fusion.142), channel_id=1, source_target_pairs={{4,0},{8,4},{12,8},{16,12},{20,16},{24,20},{28,24},{32,28},{36,32}... | collective-permute-start | bytes 589832 | tf_op jit(solution)/shard_map/while/body/eval_jaxpr/ppermute | solution.py:19
  384.0 8.0 %collective-permute-start.1 = (bf16[192,512]{1,0:T(8,128)(2,1)S(1)}, bf16[192,512]{1,0:T(8,128)(2,1)}, u32[]{:S(2)}, u32[]{:S(2)}) collective-permute-start(bf16[192,512]{1,0:T(8,128)(2,1)S(1)} %fusion.142), channel_id=1, source_target_pairs={{4,0},{8,4},{12,8},{16,12},{20,16},{24,20},{28,24},{32,28},{36,32}... | collective-permute-start | bytes 589832 | tf_op jit(solution)/shard_map/while/body/eval_jaxpr/ppermute | solution.py:19
  395.3 8.0 %collective-permute-start.1 = (bf16[192,512]{1,0:T(8,128)(2,1)S(1)}, bf16[192,512]{1,0:T(8,128)(2,1)}, u32[]{:S(2)}, u32[]{:S(2)}) collective-permute-start(bf16[192,512]{1,0:T(8,128)(2,1)S(1)} %fusion.142), channel_id=1, source_target_pairs={{4,0},{8,4},{12,8},{16,12},{20,16},{24,20},{28,24},{32,28},{36,32}... | collective-permute-start | bytes 589832 | tf_op jit(solution)/shard_map/while/body/eval_jaxpr/ppermute | solution.py:19
  406.5 8.0 %collective-permute-start.1 = (bf16[192,512]{1,0:T(8,128)(2,1)S(1)}, bf16[192,512]{1,0:T(8,128)(2,1)}, u32[]{:S(2)}, u32[]{:S(2)}) collective-permute-start(bf16[192,512]{1,0:T(8,128)(2,1)S(1)} %fusion.142), channel_id=1, source_target_pairs={{4,0},{8,4},{12,8},{16,12},{20,16},{24,20},{28,24},{32,28},{36,32}... | collective-permute-start | bytes 589832 | tf_op jit(solution)/shard_map/while/body/eval_jaxpr/ppermute | solution.py:19
  417.8 8.0 %collective-permute-start.1 = (bf16[192,512]{1,0:T(8,128)(2,1)S(1)}, bf16[192,512]{1,0:T(8,128)(2,1)}, u32[]{:S(2)}, u32[]{:S(2)}) collective-permute-start(bf16[192,512]{1,0:T(8,128)(2,1)S(1)} %fusion.142), channel_id=1, source_target_pairs={{4,0},{8,4},{12,8},{16,12},{20,16},{24,20},{28,24},{32,28},{36,32}... | collective-permute-start | bytes 589832 | tf_op jit(solution)/shard_map/while/body/eval_jaxpr/ppermute | solution.py:19
  429.0 8.0 %collective-permute-start.1 = (bf16[192,512]{1,0:T(8,128)(2,1)S(1)}, bf16[192,512]{1,0:T(8,128)(2,1)}, u32[]{:S(2)}, u32[]{:S(2)}) collective-permute-start(bf16[192,512]{1,0:T(8,128)(2,1)S(1)} %fusion.142), channel_id=1, source_target_pairs={{4,0},{8,4},{12,8},{16,12},{20,16},{24,20},{28,24},{32,28},{36,32}... | collective-permute-start | bytes 589832 | tf_op jit(solution)/shard_map/while/body/eval_jaxpr/ppermute | solution.py:19
  440.3 8.0 %collective-permute-start.1 = (bf16[192,512]{1,0:T(8,128)(2,1)S(1)}, bf16[192,512]{1,0:T(8,128)(2,1)}, u32[]{:S(2)}, u32[]{:S(2)}) collective-permute-start(bf16[192,512]{1,0:T(8,128)(2,1)S(1)} %fusion.142), channel_id=1, source_target_pairs={{4,0},{8,4},{12,8},{16,12},{20,16},{24,20},{28,24},{32,28},{36,32}... | collective-permute-start | bytes 589832 | tf_op jit(solution)/shard_map/while/body/eval_jaxpr/ppermute | solution.py:19
  451.5 8.0 %collective-permute-start.1 = (bf16[192,512]{1,0:T(8,128)(2,1)S(1)}, bf16[192,512]{1,0:T(8,128)(2,1)}, u32[]{:S(2)}, u32[]{:S(2)}) collective-permute-start(bf16[192,512]{1,0:T(8,128)(2,1)S(1)} %fusion.142), channel_id=1, source_target_pairs={{4,0},{8,4},{12,8},{16,12},{20,16},{24,20},{28,24},{32,28},{36,32}... | collective-permute-start | bytes 589832 | tf_op jit(solution)/shard_map/while/body/eval_jaxpr/ppermute | solution.py:19
  462.8 8.0 %collective-permute-start.1 = (bf16[192,512]{1,0:T(8,128)(2,1)S(1)}, bf16[192,512]{1,0:T(8,128)(2,1)}, u32[]{:S(2)}, u32[]{:S(2)}) collective-permute-start(bf16[192,512]{1,0:T(8,128)(2,1)S(1)} %fusion.142), channel_id=1, source_target_pairs={{4,0},{8,4},{12,8},{16,12},{20,16},{24,20},{28,24},{32,28},{36,32}... | collective-permute-start | bytes 589832 | tf_op jit(solution)/shard_map/while/body/eval_jaxpr/ppermute | solution.py:19
  479.3 3.0 dynamic_update_slice.25
  484.3 2.1 fusion.56
  486.5 3.4 fusion.50
  495.4 74.2 %all-reduce = (f32[640]{0:T(1024)}, f32[640]{0:T(1024)}) all-reduce(f32[640]{0:T(1024)S(1)} %get-tuple-element.62, f32[640]{0:T(1024)S(1)} %copy-done.64), channel_id=1, replica_groups=mesh['seq'=32,'dp'=4] {'seq','dp'}, use_global_device_ids=true, to_apply=%region_30.31 | all-reduce | flops 1280 | bytes 10240 | tf_op jit(solution)/shard_map/psum | solution.py:314
  569.6 2.3 fusion.39
  571.9 2.5 fusion.17
  574.4 156.2 %all-reduce.4.cloned.1.call-done = (f32[640,1024]{1,0:T(8,128)}, f32[640,256]{1,0:T(8,128)}, f32[640,256]{1,0:T(8,128)}, f32[1024,640]{1,0:T(8,128)}, f32[640,20...) async-done(((f32[640,1024]{1,0:T(8,128)}, f32[640,256]{1,0:T(8,128)}, f32[640,256]{1,0:T(8,128)}, f32[1024,640]{1,0:T(8,128)}, f32[640,2048]{1,0:T(8,128)}, ...) | async-done | bytes 22282256 | tf_op jit(solution)/shard_map/psum | solution.py:314
  730.6 3.7 copy.103
  736.3 2.1 copy.105
  739.9 2.7 copy.107
  742.6 2.7 copy.108
  746.3 2.4 copy.109
  (330 shorter events, 174.7 us)
Async XLA Ops:
  7.2 216.1 %copy-start = (bf16[2048,640]{1,0:T(8,128)(2,1)S(1)}, bf16[2048,640]{1,0:T(8,128)(2,1)}, u32[]{:S(2)}) copy-start(bf16[2048,640]{1,0:T(8,128)(2,1)} %param.24) | copy-start | bytes 7864324
  7.2 723.5 %all-reduce.4.cloned.1.call-start = ((), (), s32[]{:S(2)}) async-start(), calls=%async_computation | async-start | bytes 44564480 | tf_op jit(solution)/shard_map/psum | solution.py:314
  19.0 6.0 copy-start.57
  21.1 3.9 copy-start.4
  21.2 3.9 copy-start.52
  25.0 3.0 copy-start.69
  27.0 2.3 copy-start.13
  27.0 2.3 copy-start.56
  30.1 7.0 collective-permute-start
  38.4 7.2 collective-permute-start
  47.0 8.1 %collective-permute-start = (bf16[192,512]{1,0:T(8,128)(2,1)}, bf16[192,512]{1,0:T(8,128)(2,1)S(1)}, u32[]{:S(2)}, u32[]{:S(2)}) collective-permute-start(bf16[192,512]{1,0:T(8,128)(2,1)} %get-tuple-element.169), channel_id=1, source_target_pairs={{0,4},{4,8},{8,12},{12,16},{16,20},{20,24},{24,28},{28,32},{32,36}... | collective-permute-start | bytes 589832 | tf_op jit(solution)/shard_map/while/body/eval_jaxpr/ppermute | solution.py:19
  56.5 9.3 %collective-permute-start = (bf16[192,512]{1,0:T(8,128)(2,1)}, bf16[192,512]{1,0:T(8,128)(2,1)S(1)}, u32[]{:S(2)}, u32[]{:S(2)}) collective-permute-start(bf16[192,512]{1,0:T(8,128)(2,1)} %get-tuple-element.169), channel_id=1, source_target_pairs={{0,4},{4,8},{8,12},{12,16},{16,20},{20,24},{24,28},{28,32},{32,36}... | collective-permute-start | bytes 589832 | tf_op jit(solution)/shard_map/while/body/eval_jaxpr/ppermute | solution.py:19
  67.1 9.3 %collective-permute-start = (bf16[192,512]{1,0:T(8,128)(2,1)}, bf16[192,512]{1,0:T(8,128)(2,1)S(1)}, u32[]{:S(2)}, u32[]{:S(2)}) collective-permute-start(bf16[192,512]{1,0:T(8,128)(2,1)} %get-tuple-element.169), channel_id=1, source_target_pairs={{0,4},{4,8},{8,12},{12,16},{16,20},{20,24},{24,28},{28,32},{32,36}... | collective-permute-start | bytes 589832 | tf_op jit(solution)/shard_map/while/body/eval_jaxpr/ppermute | solution.py:19
  77.8 9.3 %collective-permute-start = (bf16[192,512]{1,0:T(8,128)(2,1)}, bf16[192,512]{1,0:T(8,128)(2,1)S(1)}, u32[]{:S(2)}, u32[]{:S(2)}) collective-permute-start(bf16[192,512]{1,0:T(8,128)(2,1)} %get-tuple-element.169), channel_id=1, source_target_pairs={{0,4},{4,8},{8,12},{12,16},{16,20},{20,24},{24,28},{28,32},{32,36}... | collective-permute-start | bytes 589832 | tf_op jit(solution)/shard_map/while/body/eval_jaxpr/ppermute | solution.py:19
  88.5 9.3 %collective-permute-start = (bf16[192,512]{1,0:T(8,128)(2,1)}, bf16[192,512]{1,0:T(8,128)(2,1)S(1)}, u32[]{:S(2)}, u32[]{:S(2)}) collective-permute-start(bf16[192,512]{1,0:T(8,128)(2,1)} %get-tuple-element.169), channel_id=1, source_target_pairs={{0,4},{4,8},{8,12},{12,16},{16,20},{20,24},{24,28},{28,32},{32,36}... | collective-permute-start | bytes 589832 | tf_op jit(solution)/shard_map/while/body/eval_jaxpr/ppermute | solution.py:19
  99.1 9.3 %collective-permute-start = (bf16[192,512]{1,0:T(8,128)(2,1)}, bf16[192,512]{1,0:T(8,128)(2,1)S(1)}, u32[]{:S(2)}, u32[]{:S(2)}) collective-permute-start(bf16[192,512]{1,0:T(8,128)(2,1)} %get-tuple-element.169), channel_id=1, source_target_pairs={{0,4},{4,8},{8,12},{12,16},{16,20},{20,24},{24,28},{28,32},{32,36}... | collective-permute-start | bytes 589832 | tf_op jit(solution)/shard_map/while/body/eval_jaxpr/ppermute | solution.py:19
  109.8 9.3 %collective-permute-start = (bf16[192,512]{1,0:T(8,128)(2,1)}, bf16[192,512]{1,0:T(8,128)(2,1)S(1)}, u32[]{:S(2)}, u32[]{:S(2)}) collective-permute-start(bf16[192,512]{1,0:T(8,128)(2,1)} %get-tuple-element.169), channel_id=1, source_target_pairs={{0,4},{4,8},{8,12},{12,16},{16,20},{20,24},{24,28},{28,32},{32,36}... | collective-permute-start | bytes 589832 | tf_op jit(solution)/shard_map/while/body/eval_jaxpr/ppermute | solution.py:19
  120.5 9.3 %collective-permute-start = (bf16[192,512]{1,0:T(8,128)(2,1)}, bf16[192,512]{1,0:T(8,128)(2,1)S(1)}, u32[]{:S(2)}, u32[]{:S(2)}) collective-permute-start(bf16[192,512]{1,0:T(8,128)(2,1)} %get-tuple-element.169), channel_id=1, source_target_pairs={{0,4},{4,8},{8,12},{12,16},{16,20},{20,24},{24,28},{28,32},{32,36}... | collective-permute-start | bytes 589832 | tf_op jit(solution)/shard_map/while/body/eval_jaxpr/ppermute | solution.py:19
  131.1 9.3 %collective-permute-start = (bf16[192,512]{1,0:T(8,128)(2,1)}, bf16[192,512]{1,0:T(8,128)(2,1)S(1)}, u32[]{:S(2)}, u32[]{:S(2)}) collective-permute-start(bf16[192,512]{1,0:T(8,128)(2,1)} %get-tuple-element.169), channel_id=1, source_target_pairs={{0,4},{4,8},{8,12},{12,16},{16,20},{20,24},{24,28},{28,32},{32,36}... | collective-permute-start | bytes 589832 | tf_op jit(solution)/shard_map/while/body/eval_jaxpr/ppermute | solution.py:19
  141.8 9.3 %collective-permute-start = (bf16[192,512]{1,0:T(8,128)(2,1)}, bf16[192,512]{1,0:T(8,128)(2,1)S(1)}, u32[]{:S(2)}, u32[]{:S(2)}) collective-permute-start(bf16[192,512]{1,0:T(8,128)(2,1)} %get-tuple-element.169), channel_id=1, source_target_pairs={{0,4},{4,8},{8,12},{12,16},{16,20},{20,24},{24,28},{28,32},{32,36}... | collective-permute-start | bytes 589832 | tf_op jit(solution)/shard_map/while/body/eval_jaxpr/ppermute | solution.py:19
  152.4 9.3 %collective-permute-start = (bf16[192,512]{1,0:T(8,128)(2,1)}, bf16[192,512]{1,0:T(8,128)(2,1)S(1)}, u32[]{:S(2)}, u32[]{:S(2)}) collective-permute-start(bf16[192,512]{1,0:T(8,128)(2,1)} %get-tuple-element.169), channel_id=1, source_target_pairs={{0,4},{4,8},{8,12},{12,16},{16,20},{20,24},{24,28},{28,32},{32,36}... | collective-permute-start | bytes 589832 | tf_op jit(solution)/shard_map/while/body/eval_jaxpr/ppermute | solution.py:19
  163.1 9.3 %collective-permute-start = (bf16[192,512]{1,0:T(8,128)(2,1)}, bf16[192,512]{1,0:T(8,128)(2,1)S(1)}, u32[]{:S(2)}, u32[]{:S(2)}) collective-permute-start(bf16[192,512]{1,0:T(8,128)(2,1)} %get-tuple-element.169), channel_id=1, source_target_pairs={{0,4},{4,8},{8,12},{12,16},{16,20},{20,24},{24,28},{28,32},{32,36}... | collective-permute-start | bytes 589832 | tf_op jit(solution)/shard_map/while/body/eval_jaxpr/ppermute | solution.py:19
  173.8 9.3 %collective-permute-start = (bf16[192,512]{1,0:T(8,128)(2,1)}, bf16[192,512]{1,0:T(8,128)(2,1)S(1)}, u32[]{:S(2)}, u32[]{:S(2)}) collective-permute-start(bf16[192,512]{1,0:T(8,128)(2,1)} %get-tuple-element.169), channel_id=1, source_target_pairs={{0,4},{4,8},{8,12},{12,16},{16,20},{20,24},{24,28},{28,32},{32,36}... | collective-permute-start | bytes 589832 | tf_op jit(solution)/shard_map/while/body/eval_jaxpr/ppermute | solution.py:19
  184.4 9.3 %collective-permute-start = (bf16[192,512]{1,0:T(8,128)(2,1)}, bf16[192,512]{1,0:T(8,128)(2,1)S(1)}, u32[]{:S(2)}, u32[]{:S(2)}) collective-permute-start(bf16[192,512]{1,0:T(8,128)(2,1)} %get-tuple-element.169), channel_id=1, source_target_pairs={{0,4},{4,8},{8,12},{12,16},{16,20},{20,24},{24,28},{28,32},{32,36}... | collective-permute-start | bytes 589832 | tf_op jit(solution)/shard_map/while/body/eval_jaxpr/ppermute | solution.py:19
  195.1 5.2 copy-start.36
  202.6 3.3 copy-start.47
  202.6 2.3 copy-start.42
  203.3 5.9 copy-start.45
  205.1 2.9 copy-start.43
  219.3 9.3 %copy-start.9 = (f32[192,640]{1,0:T(8,128)}, f32[192,640]{1,0:T(8,128)S(1)}, u32[]{:S(2)}) copy-start(f32[192,640]{1,0:T(8,128)S(1)} %get-tuple-element.117) | copy-start | bytes 1474564
  237.0 2.3 copy-start.44
  237.0 3.6 copy-start.46
  238.3 2.4 copy-start.3
  246.9 3.2 copy-start.30
  250.2 3.2 copy-start.19
  258.9 2.4 copy-start.23
  297.9 9.4 %collective-permute-start.1 = (bf16[192,512]{1,0:T(8,128)(2,1)S(1)}, bf16[192,512]{1,0:T(8,128)(2,1)}, u32[]{:S(2)}, u32[]{:S(2)}) collective-permute-start(bf16[192,512]{1,0:T(8,128)(2,1)S(1)} %fusion.142), channel_id=1, source_target_pairs={{4,0},{8,4},{12,8},{16,12},{20,16},{24,20},{28,24},{32,28},{36,32}... | collective-permute-start | bytes 589832 | tf_op jit(solution)/shard_map/while/body/eval_jaxpr/ppermute | solution.py:19
  309.3 7.1 collective-permute-start.1
  318.5 7.2 collective-permute-start.1
  327.7 9.2 %collective-permute-start.1 = (bf16[192,512]{1,0:T(8,128)(2,1)S(1)}, bf16[192,512]{1,0:T(8,128)(2,1)}, u32[]{:S(2)}, u32[]{:S(2)}) collective-permute-start(bf16[192,512]{1,0:T(8,128)(2,1)S(1)} %fusion.142), channel_id=1, source_target_pairs={{4,0},{8,4},{12,8},{16,12},{20,16},{24,20},{28,24},{32,28},{36,32}... | collective-permute-start | bytes 589832 | tf_op jit(solution)/shard_map/while/body/eval_jaxpr/ppermute | solution.py:19
  339.0 9.2 %collective-permute-start.1 = (bf16[192,512]{1,0:T(8,128)(2,1)S(1)}, bf16[192,512]{1,0:T(8,128)(2,1)}, u32[]{:S(2)}, u32[]{:S(2)}) collective-permute-start(bf16[192,512]{1,0:T(8,128)(2,1)S(1)} %fusion.142), channel_id=1, source_target_pairs={{4,0},{8,4},{12,8},{16,12},{20,16},{24,20},{28,24},{32,28},{36,32}... | collective-permute-start | bytes 589832 | tf_op jit(solution)/shard_map/while/body/eval_jaxpr/ppermute | solution.py:19
  350.2 9.2 %collective-permute-start.1 = (bf16[192,512]{1,0:T(8,128)(2,1)S(1)}, bf16[192,512]{1,0:T(8,128)(2,1)}, u32[]{:S(2)}, u32[]{:S(2)}) collective-permute-start(bf16[192,512]{1,0:T(8,128)(2,1)S(1)} %fusion.142), channel_id=1, source_target_pairs={{4,0},{8,4},{12,8},{16,12},{20,16},{24,20},{28,24},{32,28},{36,32}... | collective-permute-start | bytes 589832 | tf_op jit(solution)/shard_map/while/body/eval_jaxpr/ppermute | solution.py:19
  361.5 9.2 %collective-permute-start.1 = (bf16[192,512]{1,0:T(8,128)(2,1)S(1)}, bf16[192,512]{1,0:T(8,128)(2,1)}, u32[]{:S(2)}, u32[]{:S(2)}) collective-permute-start(bf16[192,512]{1,0:T(8,128)(2,1)S(1)} %fusion.142), channel_id=1, source_target_pairs={{4,0},{8,4},{12,8},{16,12},{20,16},{24,20},{28,24},{32,28},{36,32}... | collective-permute-start | bytes 589832 | tf_op jit(solution)/shard_map/while/body/eval_jaxpr/ppermute | solution.py:19
  372.8 9.2 %collective-permute-start.1 = (bf16[192,512]{1,0:T(8,128)(2,1)S(1)}, bf16[192,512]{1,0:T(8,128)(2,1)}, u32[]{:S(2)}, u32[]{:S(2)}) collective-permute-start(bf16[192,512]{1,0:T(8,128)(2,1)S(1)} %fusion.142), channel_id=1, source_target_pairs={{4,0},{8,4},{12,8},{16,12},{20,16},{24,20},{28,24},{32,28},{36,32}... | collective-permute-start | bytes 589832 | tf_op jit(solution)/shard_map/while/body/eval_jaxpr/ppermute | solution.py:19
  384.0 9.2 %collective-permute-start.1 = (bf16[192,512]{1,0:T(8,128)(2,1)S(1)}, bf16[192,512]{1,0:T(8,128)(2,1)}, u32[]{:S(2)}, u32[]{:S(2)}) collective-permute-start(bf16[192,512]{1,0:T(8,128)(2,1)S(1)} %fusion.142), channel_id=1, source_target_pairs={{4,0},{8,4},{12,8},{16,12},{20,16},{24,20},{28,24},{32,28},{36,32}... | collective-permute-start | bytes 589832 | tf_op jit(solution)/shard_map/while/body/eval_jaxpr/ppermute | solution.py:19
  395.3 9.2 %collective-permute-start.1 = (bf16[192,512]{1,0:T(8,128)(2,1)S(1)}, bf16[192,512]{1,0:T(8,128)(2,1)}, u32[]{:S(2)}, u32[]{:S(2)}) collective-permute-start(bf16[192,512]{1,0:T(8,128)(2,1)S(1)} %fusion.142), channel_id=1, source_target_pairs={{4,0},{8,4},{12,8},{16,12},{20,16},{24,20},{28,24},{32,28},{36,32}... | collective-permute-start | bytes 589832 | tf_op jit(solution)/shard_map/while/body/eval_jaxpr/ppermute | solution.py:19
  406.5 9.2 %collective-permute-start.1 = (bf16[192,512]{1,0:T(8,128)(2,1)S(1)}, bf16[192,512]{1,0:T(8,128)(2,1)}, u32[]{:S(2)}, u32[]{:S(2)}) collective-permute-start(bf16[192,512]{1,0:T(8,128)(2,1)S(1)} %fusion.142), channel_id=1, source_target_pairs={{4,0},{8,4},{12,8},{16,12},{20,16},{24,20},{28,24},{32,28},{36,32}... | collective-permute-start | bytes 589832 | tf_op jit(solution)/shard_map/while/body/eval_jaxpr/ppermute | solution.py:19
  417.8 9.2 %collective-permute-start.1 = (bf16[192,512]{1,0:T(8,128)(2,1)S(1)}, bf16[192,512]{1,0:T(8,128)(2,1)}, u32[]{:S(2)}, u32[]{:S(2)}) collective-permute-start(bf16[192,512]{1,0:T(8,128)(2,1)S(1)} %fusion.142), channel_id=1, source_target_pairs={{4,0},{8,4},{12,8},{16,12},{20,16},{24,20},{28,24},{32,28},{36,32}... | collective-permute-start | bytes 589832 | tf_op jit(solution)/shard_map/while/body/eval_jaxpr/ppermute | solution.py:19
  429.0 9.2 %collective-permute-start.1 = (bf16[192,512]{1,0:T(8,128)(2,1)S(1)}, bf16[192,512]{1,0:T(8,128)(2,1)}, u32[]{:S(2)}, u32[]{:S(2)}) collective-permute-start(bf16[192,512]{1,0:T(8,128)(2,1)S(1)} %fusion.142), channel_id=1, source_target_pairs={{4,0},{8,4},{12,8},{16,12},{20,16},{24,20},{28,24},{32,28},{36,32}... | collective-permute-start | bytes 589832 | tf_op jit(solution)/shard_map/while/body/eval_jaxpr/ppermute | solution.py:19
  440.3 9.2 %collective-permute-start.1 = (bf16[192,512]{1,0:T(8,128)(2,1)S(1)}, bf16[192,512]{1,0:T(8,128)(2,1)}, u32[]{:S(2)}, u32[]{:S(2)}) collective-permute-start(bf16[192,512]{1,0:T(8,128)(2,1)S(1)} %fusion.142), channel_id=1, source_target_pairs={{4,0},{8,4},{12,8},{16,12},{20,16},{24,20},{28,24},{32,28},{36,32}... | collective-permute-start | bytes 589832 | tf_op jit(solution)/shard_map/while/body/eval_jaxpr/ppermute | solution.py:19
  451.5 9.2 %collective-permute-start.1 = (bf16[192,512]{1,0:T(8,128)(2,1)S(1)}, bf16[192,512]{1,0:T(8,128)(2,1)}, u32[]{:S(2)}, u32[]{:S(2)}) collective-permute-start(bf16[192,512]{1,0:T(8,128)(2,1)S(1)} %fusion.142), channel_id=1, source_target_pairs={{4,0},{8,4},{12,8},{16,12},{20,16},{24,20},{28,24},{32,28},{36,32}... | collective-permute-start | bytes 589832 | tf_op jit(solution)/shard_map/while/body/eval_jaxpr/ppermute | solution.py:19
  462.8 9.2 %collective-permute-start.1 = (bf16[192,512]{1,0:T(8,128)(2,1)S(1)}, bf16[192,512]{1,0:T(8,128)(2,1)}, u32[]{:S(2)}, u32[]{:S(2)}) collective-permute-start(bf16[192,512]{1,0:T(8,128)(2,1)S(1)} %fusion.142), channel_id=1, source_target_pairs={{4,0},{8,4},{12,8},{16,12},{20,16},{24,20},{28,24},{32,28},{36,32}... | collective-permute-start | bytes 589832 | tf_op jit(solution)/shard_map/while/body/eval_jaxpr/ppermute | solution.py:19
  475.2 7.1 copy-start.40
  486.5 3.4 copy-start.26
  491.2 2.7 copy-start.16
  491.2 2.7 copy-start.55
  491.2 2.7 copy-start.60
  569.6 2.3 copy-start.35
  730.6 7.8 %copy-start.33 = (f32[1024,640]{1,0:T(8,128)S(1)}, f32[1024,640]{1,0:T(8,128)}, u32[]{:S(2)}) copy-start(f32[1024,640]{1,0:T(8,128)} %get-tuple-element.197) | copy-start | bytes 7864324
  730.6 12.0 %slice-start.2 = ((s8[5242880]{0:T(1024)(128)(4,1)}), s8[4194304]{0:T(1024)(128)(4,1)S(1)}, s32[]{:S(2)}) async-start(s8[5242880]{0:T(1024)(128)(4,1)} %bitcast.236), calls=%async_computation.3 | async-start | bytes 8388608
  736.3 3.6 copy-start.15
  738.4 4.2 slice-start.3
  739.9 5.3 slice-start
  742.6 3.7 slice-start.1
  (43 other events, 61.1 us)
Sparse Core Ops, SparseCore 0:
  491.3 239.2 all-reduce.3
where the time goes:
time: 761 us; the launch traced here: 756 us
  waiting for transfers between devices  281 us (37%)
  starting transfers between devices  161 us (21%)
  local copies, waits for them, and re-layouts  106 us (14%)
  blocking collectives  74.2 us (10%)
  other arithmetic  61.6 us (8%)
  matrix products  51.9 us (7%)
  between operations  18.9 us (2%)
    ppermute x32, starting transfers between devices, passed_along(): return lax.ppermute(array, axis, pairs)  161 us
    psum x1, waiting for transfers between devices, shards(): lax.psum((grad_querymat, grad_keymat, grad_valuemat, grad_projmat, grad_g...  156 us
    ppermute x32, waiting for transfers between devices, passed_along(): return lax.ppermute(array, axis, pairs)  125 us
    psum x1, blocking collectives, shards(): lax.psum((grad_querymat, grad_keymat, grad_valuemat, grad_projmat, grad_g...  74.2 us
    unnamed x155, local copies, waits for them, and re-layouts  25.7 us
    dynamic_update_slice x2, local copies, waits for them, and re-layouts, put_window(): target = lax.dynamic_update_slice(target, pieces[0], (first, starts[0], 0))  23.8 us
    convert_element_type x16, other arithmetic, hop_back(): (carry + incoming).astype(jnp.bfloat16)  17 us
    dot_general x7, matrix products, outer_sum(): lax.dot_general(left, right, (((0,), (0,)), ((), ())), preferred_element_...  16.6 us
  transfers between devices with their start and end apart: 33, of which 33 were waited for; matrix products, arithmetic and copies ran while one was open for 1% of the time, Pallas kernels for 0%

commit v1 on v0

v1 whole, which is shorter than its diff:
```python
import jax
import jax.numpy as jnp
from jax import lax
from jax.experimental import pallas as pl
from jax.experimental.pallas import tpu as pltpu
from jax.sharding import Mesh, PartitionSpec as P

WINDOW = 1024
SHORT_LEN = 2048
D = 640
HEADS = 4
HD = 256
HALF = 128
FF = 2048
TOK = 192
SHORT = 64
LONG = 128
CHIPS = 16
NEAR = 4
FAR = 8
SIDE = (NEAR + 1) * TOK + (FAR - NEAR) * SHORT
GROUPS = SIDE // SHORT
KEYS_SHORT = 2 * (FAR + 1) * SHORT
KEYS_LONG = 2 * (NEAR + 1) * LONG
KEYS = KEYS_SHORT + KEYS_LONG
FF_CHUNK = 512

epsilon = 1e-06
theta_base = 10000.0
masked_score = -1e30

SEQ = ("x", "z", "core")
CHIP = ("x", "z")
RING = ("x", "z", "dp")
ALL = ("x", "z", "core", "dp")
B_ROWS = 8192

bf16 = jnp.bfloat16
f32 = jnp.float32


def mm(left, right):
    return jnp.dot(left, right, preferred_element_type=f32)


def mm_tn(left, right):
    return lax.dot_general(left, right, (((0,), (0,)), ((), ())), preferred_element_type=f32)


def mm_nt(left, right):
    return lax.dot_general(left, right, (((1,), (1,)), ((), ())), preferred_element_type=f32)


def window_groups():
    groups = []
    for behind in range(NEAR + 1):
        groups += [(behind, "short", 0), (behind, "long", 0), (behind, "long", 1)]
    groups += [(behind, "short", 0) for behind in range(NEAR + 1, FAR + 1)]
    return groups


def key_row(side, group):
    behind, kind, part = group
    if kind == "short":
        return side * (KEYS_SHORT // 2) + behind * SHORT
    return KEYS_SHORT + side * (KEYS_LONG // 2) + behind * LONG + part * SHORT


def mask_bias(kind, chip, core):
    rows, width, first_key = (SHORT, KEYS_SHORT, 0) if kind == "short" else (LONG, KEYS_LONG, 0)
    half = width // 2
    column = lax.broadcasted_iota(jnp.int32, (1, width), 1)
    other = (column >= half).astype(jnp.int32)
    inner = column - other * half
    shift = 6 if kind == "short" else 7
    behind = lax.shift_right_logical(inner, shift)
    rest = inner & (rows - 1)
    key_core = core + other * (1 - 2 * core)
    key_position = (2 * (chip - behind) + key_core) * rows + rest
    query_position = (2 * chip + core) * rows + lax.broadcasted_iota(jnp.int32, (rows, 1), 0)
    distance = query_position - key_position
    allowed = (key_position >= 0) & (distance >= 0) & (distance < WINDOW)
    return jnp.where(allowed, 0.0, masked_score).astype(f32)


def group_tables(cosb, sinb, cosr, sinr, index):
    cb, sb = cosb[index : index + 1, :], sinb[index : index + 1, :]
    cr, sr = cosr[...], sinr[...]
    return cb * cr - sb * sr, sb * cr + cb * sr


KINDS = (
    ("short", SHORT, 0, KEYS_SHORT, 0, 0),
    ("long", LONG, KEYS_SHORT, KEYS_LONG, HEADS * SHORT, SHORT),
)


def forward_kernel(
    info, cosb, sinb, cosr, sinr, ga, gm, win_h, og_h, wq_h, wk_h, wv_h, wo_h, wg_h, wu_h, wd_h,
    q_o, k_o, v_o, gmix_o, norm_o, gres_o, ggain_o, bo_h, skv_h, gg_h, gu_h, gd_h, gp_h,
    win, og, wq, wk, wv, wo, wg, wu, wd, kv, mixed, bo, skv, gg, gu, gd, gp, bias_s, bias_l, sems,
):
    chip, core, short_at, long_at = info[0], info[1], info[2], info[3]
    short_at = pl.multiple_of(short_at, SHORT)
    long_at = pl.multiple_of(long_at, SHORT)
    loads = {}
    for number, (name, source, target) in enumerate((
        ("win", win_h, win), ("wk", wk_h, wk), ("wv", wv_h, wv), ("wq", wq_h, wq), ("wo", wo_h, wo),
        ("ogs", og_h.at[pl.ds(short_at, SHORT)], og.at[pl.ds(0, SHORT)]),
        ("ogl", og_h.at[pl.ds(long_at, LONG)], og.at[pl.ds(SHORT, LONG)]),
        ("wg", wg_h, wg), ("wu", wu_h, wu), ("wd", wd_h, wd),
    )):
        loads[name] = pltpu.make_async_copy(source, target, sems.at[number])
        loads[name].start()
    stores = []

    def store(source, target):
        copy = pltpu.make_async_copy(source, target, sems.at[10 + len(stores)])
        copy.start()
        stores.append(copy)

    bias_s[...] = mask_bias("short", chip, core)
    bias_l[...] = mask_bias("long", chip, core)
    gain_a = ga[...]
    gain_m = gm[...]
    loads["win"].wait()

    def normalise(step, carry):
        rows = pl.ds(pl.multiple_of(step * SHORT, SHORT), SHORT)
        x = win[rows, :].astype(f32)
        scale = lax.rsqrt(jnp.mean(x * x, axis=-1, keepdims=True) + epsilon)
        norm_o[rows, :] = (x * scale * gain_a).astype(bf16)
        return carry

    lax.fori_loop(0, 2 * GROUPS, normalise, 0)
    loads["wk"].wait()
    loads["wv"].wait()
    for side in range(2):
        normed = norm_o[side * SIDE : (side + 1) * SIDE, :]
        kv[:, :HD] = mm(normed, wk[...])
        kv[:, HD:] = mm(normed, wv[...])
        for number, group in enumerate(window_groups()):
            rows = slice(number * SHORT, (number + 1) * SHORT)
            cos, sin = group_tables(cosb, sinb, cosr, sinr, side * GROUPS + number)
            low_half, high_half = kv[rows, :HALF], kv[rows, HALF:HD]
            at = key_row(side, group)
            k_o[at : at + SHORT, :HALF] = (low_half * cos - high_half * sin).astype(bf16)
            k_o[at : at + SHORT, HALF:] = (high_half * cos + low_half * sin).astype(bf16)
            v_o[at : at + SHORT, :] = kv[rows, HD:].astype(bf16)
            if side == 0 and number < 3:
                skv[rows, :HD] = k_o[at : at + SHORT, :]
                skv[rows, HD:] = v_o[at : at + SHORT, :]
    store(skv.at[pl.ds(0, SHORT)], skv_h.at[pl.ds(short_at, SHORT)])
    store(skv.at[pl.ds(SHORT, LONG)], skv_h.at[pl.ds(long_at, LONG)])

    loads["wq"].wait()
    query_raw = mm(norm_o[:TOK, :], wq[...])
    for number in range(3):
        rows = slice(number * SHORT, (number + 1) * SHORT)
        cos, sin = group_tables(cosb, sinb, cosr, sinr, number)
        for head in range(HEADS):
            low_half = query_raw[rows, head * HD : head * HD + HALF]
            high_half = query_raw[rows, head * HD + HALF : (head + 1) * HD]
            at = head * SHORT if number == 0 else HEADS * SHORT + head * LONG + (number - 1) * SHORT
            turned_low = (low_half * cos - high_half * sin).astype(bf16) * bf16(HD**-0.5)
            turned_high = (high_half * cos + low_half * sin).astype(bf16) * bf16(HD**-0.5)
            q_o[at : at + SHORT, :HALF] = turned_low
            q_o[at : at + SHORT, HALF:] = turned_high

    for kind, rows, key_at, width, query_at, row_at in KINDS:
        bias = bias_s if kind == "short" else bias_l
        for head in range(HEADS):
            queries = q_o[query_at + head * rows : query_at + (head + 1) * rows, :]
            scores = mm_nt(queries, k_o[key_at : key_at + width, :]) + bias[...]
            exponent = jnp.exp(scores - jnp.max(scores, axis=-1, keepdims=True))
            total = jnp.sum(exponent, axis=-1, keepdims=True)
            probs_low = (exponent / total).astype(bf16)
            mixed[row_at : row_at + rows, head * HD : (head + 1) * HD] = mm(
                probs_low, v_o[key_at : key_at + width, :]
            ).astype(bf16)

    loads["wo"].wait()
    resid = win[:TOK, :].astype(f32) + mm(mixed[...], wo[...])
    scale = lax.rsqrt(jnp.mean(resid * resid, axis=-1, keepdims=True) + epsilon)
    unit = resid * scale
    normed_mlp = (unit * gain_m).astype(bf16)
    for name in ("ogs", "ogl", "wg", "wu", "wd"):
        loads[name].wait()
    grad_out = og[...]
    block_out = resid
    grad_normed = jnp.zeros((TOK, D), f32)
    for chunk in range(FF // FF_CHUNK):
        cols = slice(chunk * FF_CHUNK, (chunk + 1) * FF_CHUNK)
        gate = mm(normed_mlp, wg[:, cols])
        up = mm(normed_mlp, wu[:, cols])
        sig = jax.nn.sigmoid(gate)
        silu = gate * sig
        act = (silu * up).astype(bf16)
        grad_act = mm_nt(grad_out, wd[cols, :])
        grad_gate = (grad_act * up * sig * (1.0 + gate * (1.0 - sig))).astype(bf16)
        grad_up = (grad_act * silu).astype(bf16)
        block_out = block_out + mm(act, wd[cols, :])
        grad_normed = grad_normed + mm_nt(grad_gate, wg[:, cols]) + mm_nt(grad_up, wu[:, cols])
        gd[cols, :] = mm_tn(act, grad_out).astype(bf16)
        gg[:, cols] = mm_tn(normed_mlp, grad_gate).astype(bf16)
        gu[:, cols] = mm_tn(normed_mlp, grad_up).astype(bf16)
        store(gd.at[pl.ds(chunk * FF_CHUNK, FF_CHUNK)], gd_h.at[pl.ds(chunk * FF_CHUNK, FF_CHUNK)])
    store(gg, gg_h)
    store(gu, gu_h)
    bo[...] = block_out.astype(bf16)
    store(bo.at[pl.ds(0, SHORT)], bo_h.at[pl.ds(short_at, SHORT)])
    store(bo.at[pl.ds(SHORT, LONG)], bo_h.at[pl.ds(long_at, LONG)])
    ggain_o[...] = jnp.sum(grad_normed * unit, axis=0, keepdims=True)
    scaled = grad_normed * gain_m
    grad_resid = grad_out.astype(f32) + scale * (
        scaled - unit * jnp.mean(scaled * unit, axis=-1, keepdims=True)
    )
    gres_o[...] = grad_resid
    grad_branch = grad_resid.astype(bf16)
    gp[...] = mm_tn(mixed[...], grad_branch).astype(bf16)
    store(gp, gp_h)
    grad_mixed = mm_nt(grad_branch, wo[...]).astype(bf16)
    for head in range(HEADS):
        cols = slice(head * HD, (head + 1) * HD)
        gmix_o[head * SHORT : (head + 1) * SHORT, :] = grad_mixed[:SHORT, cols]
        at = HEADS * SHORT + head * LONG
        gmix_o[at : at + LONG, :] = grad_mixed[SHORT:, cols]
    for copy in stores:
        copy.wait()


def backward_kernel(
    info, cosb, sinb, cosr, sinr, ggain, q, k, v, gmix, norm, wq,
    b_o, ret_o, gnq_o,
    probs_s, probs_l, gs_s, gs_l, bias_s, bias_l, gq,
):
    chip, core = info[0], info[1]
    bias_s[...] = mask_bias("short", chip, core)
    bias_l[...] = mask_bias("long", chip, core)
    for kind, rows, key_at, width, query_at, row_at in KINDS:
        bias, probs_all, gs_all = (bias_s, probs_s, gs_s) if kind == "short" else (bias_l, probs_l, gs_l)
        keys = k[key_at : key_at + width, :]
        values = v[key_at : key_at + width, :]
        for head in range(HEADS):
            here = slice(query_at + head * rows, query_at + (head + 1) * rows)
            scores = mm_nt(q[here, :], keys) + bias[...]
            exponent = jnp.exp(scores - jnp.max(scores, axis=-1, keepdims=True))
            probs = exponent / jnp.sum(exponent, axis=-1, keepdims=True)
            probs_all[head * rows : (head + 1) * rows, :] = probs.astype(bf16)
            grad_probs = mm_nt(gmix[here, :], values)
            inner = jnp.sum(probs * grad_probs, axis=-1, keepdims=True)
            grad_scores = (probs * (grad_probs - inner)).astype(bf16)
            gs_all[head * rows : (head + 1) * rows, :] = grad_scores
            grad_queries = mm(grad_scores, keys) * (HD**-0.5)
            for part in range(rows // SHORT):
                number = 0 if kind == "short" else 1 + part
                cos, sin = group_tables(cosb, sinb, cosr, sinr, number)
                low_half = grad_queries[part * SHORT : (part + 1) * SHORT, :HALF]
                high_half = grad_queries[part * SHORT : (part + 1) * SHORT, HALF:]
                at = row_at + part * SHORT
                gq[at : at + SHORT, head * HD : head * HD + HALF] = (
                    low_half * cos + high_half * sin
                ).astype(bf16)
                gq[at : at + SHORT, head * HD + HALF : (head + 1) * HD] = (
                    high_half * cos - low_half * sin
                ).astype(bf16)
        stack = slice(query_at, query_at + HEADS * rows)
        grad_keys = mm_tn(gs_all[...], q[stack, :])
        grad_values = mm_tn(probs_all[...], gmix[stack, :])
        for side in range(2):
            for number, group in enumerate(window_groups()):
                if group[1] != kind:
                    continue
                at = key_row(side, group) - key_at
                cos, sin = group_tables(cosb, sinb, cosr, sinr, side * GROUPS + number)
                low_half = grad_keys[at : at + SHORT, :HALF]
                high_half = grad_keys[at : at + SHORT, HALF:]
                to = side * SIDE + number * SHORT
                ret_o[to : to + SHORT, :HALF] = (low_half * cos + high_half * sin).astype(bf16)
                ret_o[to : to + SHORT, HALF:HD] = (high_half * cos - low_half * sin).astype(bf16)
                ret_o[to : to + SHORT, HD:] = grad_values[at : at + SHORT, :].astype(bf16)
    gnq_o[...] = mm_nt(gq[...], wq[...])
    for chunk in range(HEADS):
        grad_wq = mm_tn(norm[:TOK, :], gq[:, chunk * HD : (chunk + 1) * HD]).astype(bf16)
        for part in range(2):
            at = (2 * chunk + part) * D
            b_o[at : at + D, :] = grad_wq[:, part * HALF : (part + 1) * HALF]
    for chunk in range(2):
        grad_wkv = mm_tn(norm[...], ret_o[:, chunk * HD : (chunk + 1) * HD]).astype(bf16)
        for part in range(2):
            at = (8 + 2 * chunk + part) * D
            b_o[at : at + D, :] = grad_wkv[:, part * HALF : (part + 1) * HALF]
    b_o[12 * D :, :] = jnp.zeros((B_ROWS - 12 * D, HALF), bf16)
    for part in range(D // HALF):
        b_o[12 * D + 16 * part : 12 * D + 16 * part + 16, :] = jnp.broadcast_to(
            ggain[:, part * HALF : (part + 1) * HALF], (16, HALF)
        ).astype(bf16)


VMEM = pl.BlockSpec(memory_space=pltpu.VMEM)
SMEM = pl.BlockSpec(memory_space=pltpu.SMEM)
ANY = pl.BlockSpec(memory_space=pl.ANY)


def shape(dims, kind=bf16):
    return jax.ShapeDtypeStruct(dims, kind)


def run_forward(*operands):
    return pl.pallas_call(
        forward_kernel,
        in_specs=[SMEM] + [VMEM] * 6 + [ANY] * 9,
        out_specs=[VMEM] * 7 + [ANY] * 6,
        out_shape=[
            shape((HEADS * TOK, HD)), shape((KEYS, HD)), shape((KEYS, HD)), shape((HEADS * TOK, HD)),
            shape((2 * SIDE, D)), shape((TOK, D), f32), shape((1, D), f32),
            shape((TOK, D)), shape((TOK, 2 * HD)),
            shape((D, FF)), shape((D, FF)), shape((FF, D)), shape((HEADS * HD, D)),
        ],
        scratch_shapes=[
            pltpu.VMEM((2 * SIDE, D), bf16), pltpu.VMEM((TOK, D), bf16),
            pltpu.VMEM((D, HEADS * HD), bf16), pltpu.VMEM((D, HD), bf16), pltpu.VMEM((D, HD), bf16),
            pltpu.VMEM((HEADS * HD, D), bf16), pltpu.VMEM((D, FF), bf16), pltpu.VMEM((D, FF), bf16),
            pltpu.VMEM((FF, D), bf16),
            pltpu.VMEM((SIDE, 2 * HD), f32), pltpu.VMEM((TOK, HEADS * HD), bf16),
            pltpu.VMEM((TOK, D), bf16), pltpu.VMEM((TOK, 2 * HD), bf16),
            pltpu.VMEM((D, FF), bf16), pltpu.VMEM((D, FF), bf16), pltpu.VMEM((FF, D), bf16),
            pltpu.VMEM((HEADS * HD, D), bf16),
            pltpu.VMEM((SHORT, KEYS_SHORT), f32), pltpu.VMEM((LONG, KEYS_LONG), f32),
            pltpu.SemaphoreType.DMA((24,)),
        ],
        compiler_params=pltpu.CompilerParams(vmem_limit_bytes=58 * 2**20),
        cost_estimate=pl.CostEstimate(flops=10**10, bytes_accessed=4 * 10**7, transcendentals=10**6),
        name="forward",
    )(*operands)


def run_backward(*operands):
    return pl.pallas_call(
        backward_kernel,
        in_specs=[SMEM] + [VMEM] * 11,
        out_specs=[VMEM] * 3,
        out_shape=[shape((B_ROWS, HALF)), shape((2 * SIDE, 2 * HD)), shape((TOK, D), f32)],
        scratch_shapes=[
            pltpu.VMEM((HEADS * SHORT, KEYS_SHORT), bf16), pltpu.VMEM((HEADS * LONG, KEYS_LONG), bf16),
            pltpu.VMEM((HEADS * SHORT, KEYS_SHORT), bf16), pltpu.VMEM((HEADS * LONG, KEYS_LONG), bf16),
            pltpu.VMEM((SHORT, KEYS_SHORT), f32), pltpu.VMEM((LONG, KEYS_LONG), f32),
            pltpu.VMEM((TOK, HEADS * HD), bf16),
        ],
        compiler_params=pltpu.CompilerParams(vmem_limit_bytes=58 * 2**20),
        cost_estimate=pl.CostEstimate(flops=8 * 10**9, bytes_accessed=2 * 10**7, transcendentals=10**6),
        name="backward",
    )(*operands)


def shift_chips(array, by):
    pairs = [(i, i + by) for i in range(CHIPS) if 0 <= i + by < CHIPS]
    return lax.ppermute(array, CHIP, pairs)


def swap_cores(array):
    return lax.ppermute(array, "core", [(0, 1), (1, 0)])


def exchange(array, axes, count):
    parts = array.reshape((count, array.shape[0] // count) + array.shape[1:])
    return lax.all_to_all(parts, axes, 0, 0, tiled=True)


def spread(array, axes, count):
    copies = jnp.broadcast_to(array[None], (count,) + array.shape)
    got = lax.all_to_all(copies, axes, 0, 0, tiled=True)
    return got.reshape((count * array.shape[0],) + array.shape[1:])


def total_of(parts):
    return jnp.sum(parts.astype(f32), axis=0).astype(bf16)


def base_tables(chip, core):
    frequency = theta_base ** (-(jnp.arange(HALF, dtype=f32) * 2.0 / HD))
    positions = []
    for side in range(2):
        key_core = core if side == 0 else 1 - core
        for behind, kind, part in window_groups():
            piece = 2 * (chip - behind) + key_core
            positions.append(piece * SHORT if kind == "short" else piece * LONG + part * SHORT)
    base = jnp.stack(positions).astype(f32)[:, None] * frequency[None, :]
    rest = jnp.arange(SHORT, dtype=f32)[:, None] * frequency[None, :]
    return jnp.cos(base), jnp.sin(base), jnp.cos(rest), jnp.sin(rest)


def shards(
    tokens, lengths, w_query, w_key, w_value, w_output, w_gate, w_up, w_down, gain_attn, gain_mlp, out_grad
):
    core = lax.axis_index("core")
    chip = lax.axis_index(CHIP)
    short_first = lengths[0, 0] == SHORT_LEN
    short_at = jnp.where(short_first, 0, LONG).astype(jnp.int32)
    long_at = jnp.where(short_first, SHORT, 0).astype(jnp.int32)
    info = jnp.stack([chip, core, short_at, long_at]).astype(jnp.int32)

    def to_slots(rows):
        return jnp.where(
            short_first, rows, jnp.concatenate([rows[SHORT:], rows[:SHORT]], axis=0)
        )

    own = jnp.where(
        short_first, tokens[0], jnp.concatenate([tokens[0, LONG:], tokens[0, :LONG]], axis=0)
    )
    own_short = own[:SHORT]
    pieces = [own]
    for behind in range(1, FAR + 1):
        pieces.append(shift_chips(own if behind <= NEAR else own_short, behind))
    side_own = jnp.concatenate(pieces, axis=0)
    side_other = swap_cores(side_own)
    window = jnp.concatenate([side_own, side_other], axis=0)
    cosb, sinb, cosr, sinr = base_tables(chip, core)
    (
        q, k, v, gmix, norm, grad_resid, grad_gain_mlp,
        block_out, shared_kv, g_gate, g_up, g_down, g_proj,
    ) = run_forward(
        info, cosb, sinb, cosr, sinr, gain_attn[None], gain_mlp[None], window, out_grad[0],
        w_query, w_key, w_value, w_output, w_gate, w_up, w_down,
    )
    totals = lax.psum((g_gate, g_up, g_down, g_proj), ALL)

    packed, returned, grad_normed_q = run_backward(
        info, cosb, sinb, cosr, sinr, grad_gain_mlp, q, k, v, gmix, norm, w_query
    )
    part = total_of(exchange(packed, "core", 2))
    part = total_of(exchange(part, RING, 64))
    whole = spread(spread(part, RING, 64), "core", 2).astype(f32)
    blocks = [whole[i * D : (i + 1) * D] for i in range(12)]
    grad_query = jnp.concatenate(blocks[:8], axis=1)
    grad_key = jnp.concatenate(blocks[8:10], axis=1)
    grad_value = jnp.concatenate(blocks[10:], axis=1)
    tail = whole[12 * D :]
    total_gain_mlp = jnp.concatenate([tail[16 * i] for i in range(D // HALF)])
    total_gain_attn = (
        jnp.sum(grad_query * w_query.astype(f32), axis=1)
        + jnp.sum(grad_key * w_key.astype(f32), axis=1)
        + jnp.sum(grad_value * w_value.astype(f32), axis=1)
    ) / gain_attn

    mine = returned[:SIDE].astype(f32)
    theirs = swap_cores(returned[SIDE:])
    chip_sum = (mine + theirs.astype(f32)).astype(bf16)
    grad_kv = chip_sum[:TOK].astype(f32)
    for behind in range(1, FAR + 1):
        if behind <= NEAR:
            piece = chip_sum[behind * TOK : (behind + 1) * TOK]
            grad_kv = grad_kv + shift_chips(piece, -behind).astype(f32)
        else:
            at = (NEAR + 1) * TOK + (behind - NEAR - 1) * SHORT
            piece = shift_chips(chip_sum[at : at + SHORT], -behind).astype(f32)
            grad_kv = grad_kv + jnp.pad(piece, ((0, LONG), (0, 0)))
    grad_kv = grad_kv.astype(bf16)
    grad_normed = grad_normed_q + mm_nt(grad_kv[:, :HD], w_key) + mm_nt(grad_kv[:, HD:], w_value)
    wide = own.astype(f32)
    scale = lax.rsqrt(jnp.mean(wide * wide, axis=-1, keepdims=True) + epsilon)
    unit = wide * scale
    scaled = grad_normed * gain_attn
    input_grad = grad_resid + scale * (
        scaled - unit * jnp.mean(scaled * unit, axis=-1, keepdims=True)
    )
    return (
        block_out[None], shared_kv[None], to_slots(input_grad)[None],
        grad_query, grad_key, grad_value, totals[3].astype(f32),
        totals[0].astype(f32), totals[1].astype(f32), totals[2].astype(f32),
        total_gain_attn, total_gain_mlp,
    )


def solution(mesh):
    fine = Mesh(mesh.devices.reshape(4, 4, 2, 4), ALL)
    rows = P("dp", SEQ, None)
    return jax.shard_map(
        shards,
        mesh=fine,
        in_specs=(rows, P("dp", None)) + (P(),) * 9 + (rows,),
        out_specs=(rows, rows, rows) + (P(),) * 9,
        check_vma=False,
    )
```

time: 761 us -> 339 us (0.45)
  waiting for transfers between devices: 281 us -> 156 us
  local copies, waits for them, and re-layouts: 106 us -> 11.1 us
  starting transfers between devices: 161 us -> 71.7 us
  blocking collectives: 74.2 us -> 15.9 us
  matrix products: 51.9 us -> 0.65 us
  Pallas kernels: 0 us -> 41.7 us
  other arithmetic: 61.6 us -> 24.2 us
    ppermute x32 -> x18, waiting for transfers between devices: 125 us -> 9.1 us  [the longest x16 9.1 us: shift_chips(): return lax.ppermute(array, CHIP, pairs)]
    ppermute x32 -> x18, starting transfers between devices: 161 us -> 48.1 us  [the longest x16 43.9 us: shift_chips(): return lax.ppermute(array, CHIP, pairs)]
    psum x1 -> x0, blocking collectives: 74.2 us -> none  [shards(): lax.psum((grad_querymat, grad_keymat, grad_valuemat, grad_projmat, grad_g...]
    dot_general x33 -> x2, matrix products: 51.9 us -> 0.65 us  [mm_nt(): lax.dot_general(left, right, (((1,), (1,)), ((), ())), preferred_element_...]
    dynamic_update_slice x22 -> x0, local copies, waits for them, and re-layouts: 44.6 us -> none  [the longest x2 23.8 us: put_window(): target = lax.dynamic_update_slice(target, pieces[0], (first, starts[0], 0))]
    pallas_call x0 -> x2, Pallas kernels: none -> 41.7 us  [the longest x1 28.1 us: run_forward(): pl.pallas_call(forward_kernel, in_specs=[SMEM] + [VMEM] * 6 + [ANY] * 9,...]
    unnamed x155 -> x47, local copies, waits for them, and re-layouts: 25.7 us -> 1.14 us
    all_to_all x0 -> x2, starting transfers between devices: none -> 23.6 us  [the longest x1 13.2 us: exchange(): return lax.all_to_all(parts, axes, 0, 0, tiled=True)]
  transfers between devices with their start and end apart: 33 -> 21, of which waited for: 33 -> 5; matrix products, arithmetic and copies ran while one was open for 1% -> 5% of each run, Pallas kernels for 0% -> 0%
where the time goes in v1:
time: 339 us; the launch traced here: 336 us
  waiting for transfers between devices  156 us (46%)
  starting transfers between devices  71.7 us (21%)
  Pallas kernels  41.7 us (12%)
  other arithmetic  24.2 us (7%)
  blocking collectives  15.9 us (5%)
  between operations  15.3 us (5%)
  local copies, waits for them, and re-layouts  11.1 us (3%)
    psum x1, waiting for transfers between devices, shards(): totals = lax.psum((g_gate, g_up, g_down, g_proj), ALL)  133 us
    ppermute x16, starting transfers between devices, shift_chips(): return lax.ppermute(array, CHIP, pairs)  43.9 us
    pallas_call x1, Pallas kernels, run_forward(): pl.pallas_call(forward_kernel, in_specs=[SMEM] + [VMEM] * 6 + [ANY] * 9,...  28.1 us
    pallas_call x1, Pallas kernels, run_backward(): pl.pallas_call(backward_kernel, in_specs=[SMEM] + [VMEM] * 11, out_specs=...  13.6 us
    all_to_all x1, waiting for transfers between devices, spread(): got = lax.all_to_all(copies, axes, 0, 0, tiled=True)  13.3 us
    all_to_all x1, starting transfers between devices, exchange(): return lax.all_to_all(parts, axes, 0, 0, tiled=True)  13.2 us
    all_to_all x1, blocking collectives, spread(): got = lax.all_to_all(copies, axes, 0, 0, tiled=True)  10.9 us
    all_to_all x1, starting transfers between devices, spread(): got = lax.all_to_all(copies, axes, 0, 0, tiled=True)  10.5 us
  transfers between devices with their start and end apart: 21, of which 5 were waited for; matrix products, arithmetic and copies ran while one was open for 5% of the time, Pallas kernels for 0%

profile of v1, /device:TPU:3, one launch (start us, length us, event | category | flops | bytes accessed | tf_op | source)
XLA Modules:
  0.0 336.4 jit_solution(8994486914277248575)
XLA Ops:
  7.2 0.9 slice_bitcast_fusion.1
  8.1 0.9 slice_bitcast_fusion
  9.7 1.1 fusion.7
  10.8 3.7 %collective-permute-start = (bf16[192,640]{1,0:T(8,128)(2,1)S(1)}, bf16[192,640]{1,0:T(8,128)(2,1)S(1)}, u32[]{:S(2)}, u32[]{:S(2)}) collective-permute-start(bf16[192,640]{1,0:T(8,128)(2,1)S(1)} %get-tuple-element.53), channel_id=1, source_target_pairs={{0,8},{8,16},{16,24},{24,32},{32,40},{40,48},{48,56},{56,64},{64,7... | collective-permute-start | bytes 737288 | tf_op jit(solution)/shard_map/ppermute | solution.py:358
  14.5 3.8 %collective-permute-start.7 = (bf16[64,640]{1,0:T(8,128)(2,1)S(1)}, bf16[64,640]{1,0:T(8,128)(2,1)S(1)}, u32[]{:S(2)}, u32[]{:S(2)}) collective-permute-start(bf16[64,640]{1,0:T(8,128)(2,1)S(1)} %slice.150), channel_id=1, source_target_pairs={{0,64},{8,72},{16,80},{24,88},{32,96},{40,104},{48,112},{56,120},{... | collective-permute-start | bytes 245768 | tf_op jit(solution)/shard_map/ppermute | solution.py:358
  18.3 2.5 collective-permute-start.6
  20.8 2.5 collective-permute-start.5
  23.2 3.5 %collective-permute-start.1 = (bf16[192,640]{1,0:T(8,128)(2,1)S(1)}, bf16[192,640]{1,0:T(8,128)(2,1)S(1)}, u32[]{:S(2)}, u32[]{:S(2)}) collective-permute-start(bf16[192,640]{1,0:T(8,128)(2,1)S(1)} %get-tuple-element.53), channel_id=1, source_target_pairs={{0,16},{8,24},{16,32},{24,40},{32,48},{40,56},{48,64},{56,72},{64,... | collective-permute-start | bytes 737288 | tf_op jit(solution)/shard_map/ppermute | solution.py:358
  26.8 2.2 collective-permute-start.2
  29.0 5.6 %collective-permute-done.1 = bf16[192,640]{1,0:T(8,128)(2,1)S(1)} collective-permute-done((bf16[192,640]{1,0:T(8,128)(2,1)S(1)}, bf16[192,640]{1,0:T(8,128)(2,1)S(1)}, u32[]{:S(2)}, u32[]{:S(2)}) %collective-permute-start.1) | collective-permute-done | bytes 245792 | tf_op jit(solution)/shard_map/ppermute | solution.py:358
  34.6 3.3 collective-permute-start.3
  38.1 4.6 %collective-permute-start.4 = (bf16[64,640]{1,0:T(8,128)(2,1)S(1)}, bf16[64,640]{1,0:T(8,128)(2,1)S(1)}, u32[]{:S(2)}, u32[]{:S(2)}) collective-permute-start(bf16[64,640]{1,0:T(8,128)(2,1)S(1)} %slice.150), channel_id=1, source_target_pairs={{0,40},{8,48},{16,56},{24,64},{32,72},{40,80},{48,88},{56,96},{64,... | collective-permute-start | bytes 245768 | tf_op jit(solution)/shard_map/ppermute | solution.py:358
  42.8 2.2 collective-permute-done.4
  45.1 2.6 collective-permute-start.8
  47.7 0.1 stack.175
  47.9 0.6 broadcast_in_dim.17.gm
  48.4 0.6 broadcast_in_dim.16.ga
  49.0 0.6 pad_add_fusion.info
  49.6 0.8 multiply_sine_fusion
  50.4 0.8 fusion.12
  51.1 1.3 constant_dynamic-update-slice_fusion.9.win_h
  52.4 28.1 %forward.1 = (bf16[768,256]{1,0:T(8,128)(2,1)}, bf16[2432,256]{1,0:T(8,128)(2,1)}, bf16[2432,256]{1,0:T(8,128)(2,1)}, bf16[768,256]{1,0:T(8,128)(2,1)}, bf16[243...) custom-call(s32[4]{0:T(128)} %pad_add_fusion.info, ...), custom_call_target="tpu_custom_call" | custom-call | flops 10000000000 | bytes 40000000 | tf_op jit(solution)/shard_map/forward/pallas_call | solution.py:310
  80.5 13.6 %backward.1 = (bf16[8192,128]{1,0:T(8,128)(2,1)}, bf16[2432,512]{1,0:T(8,128)(2,1)}, f32[192,640]{1,0:T(8,128)}) custom-call(s32[4]{0:T(128)} %pad_add_fusion.info, f32[38,128]{1,0:T(8,128)} %get-tuple-element.86.cosb, f32[38,128]{1,0:T(8,128)} %get-tuple-element.85.sinb, f32[64,128]{1,0:T(8,128)} %get-tuple-element.88.cosr, ...), custom_call_target="tpu_custom_call" | custom-call | flops 8000000000 | bytes 20000000 | tf_op jit(solution)/shard_map/backward/pallas_call | solution.py:339
  94.1 2.6 slice.119
  96.7 1.6 collective-permute-start.9
  98.3 5.0 %all_to_all.20 = bf16[2,4096,128]{2,1,0:T(8,128)(2,1)S(1)} all-to-all(bf16[2,4096,128]{2,1,0:T(8,128)(2,1)S(1)} %bitcast.86), channel_id=1, replica_groups=mesh['x'=4,'z'=4,'core'=2,'dp'=4] {'core'}, dimensions={0} | all-to-all | bytes 4194304 | tf_op jit(solution)/shard_map/all_to_all | solution.py:367
  103.3 1.6 reduce_sum.71
  104.9 13.2 %all-to-all-start.1 = ((bf16[64,64,128]{2,1,0:T(8,128)(2,1)}), bf16[64,64,128]{2,1,0:T(8,128)(2,1)S(1)}, u32[]{:S(2)}, u32[]{:S(2)}) async-start(bf16[64,64,128]{2,1,0:T(8,128)(2,1)} %bitcast.85), calls=%async_computation.1 | async-start | bytes 2097152 | tf_op jit(solution)/shard_map/all_to_all | solution.py:367
  118.2 2.0 add_convert_fusion
  120.2 0.7 fusion.15
  120.8 1.3 collective-permute-start.14
  122.1 1.3 collective-permute-start.17
  123.4 1.3 collective-permute-start.16
  124.7 0.8 fusion.16
  125.5 1.3 collective-permute-start.15
  126.8 4.3 %collective-permute-start.10 = (bf16[192,512]{1,0:T(8,128)(2,1)}, bf16[192,512]{1,0:T(8,128)(2,1)}, u32[]{:S(2)}, u32[]{:S(2)}) collective-permute-start(bf16[192,512]{1,0:T(8,128)(2,1)} %get-tuple-element.63), channel_id=1, source_target_pairs={{8,0},{16,8},{24,16},{32,24},{40,32},{48,40},{56,48},{64,56},{72,6... | collective-permute-start | bytes 589832 | tf_op jit(solution)/shard_map/ppermute | solution.py:358
  131.1 1.3 collective-permute-done.14
  132.4 4.4 %collective-permute-start.13 = (bf16[192,512]{1,0:T(8,128)(2,1)}, bf16[192,512]{1,0:T(8,128)(2,1)}, u32[]{:S(2)}, u32[]{:S(2)}) collective-permute-start(bf16[192,512]{1,0:T(8,128)(2,1)} %get-tuple-element.64), channel_id=1, source_target_pairs={{32,0},{40,8},{48,16},{56,24},{64,32},{72,40},{80,48},{88,56},{96,... | collective-permute-start | bytes 589832 | tf_op jit(solution)/shard_map/ppermute | solution.py:358
  136.9 1.9 collective-permute-start.12
  138.8 2.2 collective-permute-start.11
  141.1 0.2 reduce_sum.72
  141.3 1.2 broadcast_in_dim.40
  142.5 10.5 %all-to-all-start.2 = ((bf16[64,64,128]{2,1,0:T(8,128)(2,1)}), bf16[64,64,128]{2,1,0:T(8,128)(2,1)S(1)}, u32[]{:S(2)}, u32[]{:S(2)}) async-start(bf16[64,64,128]{2,1,0:T(8,128)(2,1)} %broadcast_in_dim.40), calls=%async_computation.2 | async-start | bytes 2097152 | tf_op jit(solution)/shard_map/all_to_all | solution.py:372
  153.0 1.4 add_convert_fusion.1
  154.5 0.3 fusion.10
  154.8 0.4 fusion.3
  155.2 0.2 fusion.6
  155.5 0.8 fusion.8
  156.3 13.3 %all-to-all-done.2 = bf16[64,64,128]{2,1,0:T(8,128)(2,1)S(1)} async-done(((bf16[64,64,128]{2,1,0:T(8,128)(2,1)}), bf16[64,64,128]{2,1,0:T(8,128)(2,1)S(1)}, u32[]{:S(2)}, u32[]{:S(2)}) %all-to-all-start.2) | async-done | bytes 1048608 | tf_op jit(solution)/shard_map/all_to_all | solution.py:372
  169.6 0.1 broadcast_in_dim.42
  169.8 10.9 %all_to_all.21 = bf16[2,4096,128]{2,1,0:T(8,128)(2,1)S(1)} all-to-all(bf16[2,4096,128]{2,1,0:T(8,128)(2,1)S(1)} %broadcast_in_dim.42), channel_id=1, replica_groups=mesh['x'=4,'z'=4,'core'=2,'dp'=4] {'core'}, dimensions={0} | all-to-all | bytes 4194304 | tf_op jit(solution)/shard_map/all_to_all | solution.py:372
  180.7 0.4 bitcast_convert_fusion
  181.5 0.1 fusion.14
  181.6 0.1 copy-done.13
  181.7 1.3 multiply_reduce_fusion.1
  183.0 0.2 copy-done.7
  183.2 0.3 multiply_reduce_fusion
  183.5 0.1 copy-done
  183.7 0.6 add_divide_fusion
  184.3 133.3 %all-reduce.7.cloned.1.call-done = (bf16[1024,640]{1,0:T(8,128)(2,1)}, bf16[640,2048]{1,0:T(8,128)(2,1)}, bf16[640,2048]{1,0:T(8,128)(2,1)}, bf16[2048,640]{1,0:T(8,128)(2,1)}) async-done(((bf16[1024,640]{1,0:T(8,128)(2,1)}, bf16[640,2048]{1,0:T(8,128)(2,1)}, bf16[640,2048]{1,0:T(8,128)(2,1)}, bf16[2048,640]{1,0:T(8,128)(2,1)}), (bf16[1024,640]{1,0:T(8,128)(2,1)}, bf16[640,2048]{1,0:T(8,128)(2,1)}, ...) | async-done | bytes 9175056 | tf_op jit(solution)/shard_map/psum | solution.py:426
  317.5 3.1 convert_element_type.90
  320.7 3.1 convert_element_type.91
  323.8 3.1 convert_element_type.92
  326.8 2.7 convert_element_type.93
  (72 shorter events, 0.9 us)
Async XLA Ops:
  10.8 37.1 %copy-start.12 = (f32[640]{0:T(1024)S(1)}, f32[640]{0:T(1024)}, u32[]{:S(2)}) copy-start(f32[640]{0:T(1024)} %param.22) | copy-start | bytes 7684
  10.8 37.6 %copy-start.10 = (f32[640]{0:T(1024)S(1)}, f32[640]{0:T(1024)}, u32[]{:S(2)}) copy-start(f32[640]{0:T(1024)} %param.21) | copy-start | bytes 7684
  10.8 16.0 %collective-permute-start = (bf16[192,640]{1,0:T(8,128)(2,1)S(1)}, bf16[192,640]{1,0:T(8,128)(2,1)S(1)}, u32[]{:S(2)}, u32[]{:S(2)}) collective-permute-start(bf16[192,640]{1,0:T(8,128)(2,1)S(1)} %get-tuple-element.53), channel_id=1, source_target_pairs={{0,8},{8,16},{16,24},{24,32},{32,40},{40,48},{48,56},{56,64},{64,7... | collective-permute-start | bytes 737288 | tf_op jit(solution)/shard_map/ppermute | solution.py:358
  14.5 30.5 %collective-permute-start.7 = (bf16[64,640]{1,0:T(8,128)(2,1)S(1)}, bf16[64,640]{1,0:T(8,128)(2,1)S(1)}, u32[]{:S(2)}, u32[]{:S(2)}) collective-permute-start(bf16[64,640]{1,0:T(8,128)(2,1)S(1)} %slice.150), channel_id=1, source_target_pairs={{0,64},{8,72},{16,80},{24,88},{32,96},{40,104},{48,112},{56,120},{... | collective-permute-start | bytes 245768 | tf_op jit(solution)/shard_map/ppermute | solution.py:358
  18.3 26.7 %collective-permute-start.6 = (bf16[64,640]{1,0:T(8,128)(2,1)S(1)}, bf16[64,640]{1,0:T(8,128)(2,1)S(1)}, u32[]{:S(2)}, u32[]{:S(2)}) collective-permute-start(bf16[64,640]{1,0:T(8,128)(2,1)S(1)} %slice.150), channel_id=1, source_target_pairs={{0,56},{8,64},{16,72},{24,80},{32,88},{40,96},{48,104},{56,112},{6... | collective-permute-start | bytes 245768 | tf_op jit(solution)/shard_map/ppermute | solution.py:358
  20.8 24.2 %collective-permute-start.5 = (bf16[64,640]{1,0:T(8,128)(2,1)S(1)}, bf16[64,640]{1,0:T(8,128)(2,1)S(1)}, u32[]{:S(2)}, u32[]{:S(2)}) collective-permute-start(bf16[64,640]{1,0:T(8,128)(2,1)S(1)} %slice.150), channel_id=1, source_target_pairs={{0,48},{8,56},{16,64},{24,72},{32,80},{40,88},{48,96},{56,104},{64... | collective-permute-start | bytes 245768 | tf_op jit(solution)/shard_map/ppermute | solution.py:358
  23.2 11.4 %collective-permute-start.1 = (bf16[192,640]{1,0:T(8,128)(2,1)S(1)}, bf16[192,640]{1,0:T(8,128)(2,1)S(1)}, u32[]{:S(2)}, u32[]{:S(2)}) collective-permute-start(bf16[192,640]{1,0:T(8,128)(2,1)S(1)} %get-tuple-element.53), channel_id=1, source_target_pairs={{0,16},{8,24},{16,32},{24,40},{32,48},{40,56},{48,64},{56,72},{64,... | collective-permute-start | bytes 737288 | tf_op jit(solution)/shard_map/ppermute | solution.py:358
  26.8 11.3 %collective-permute-start.2 = (bf16[192,640]{1,0:T(8,128)(2,1)S(1)}, bf16[192,640]{1,0:T(8,128)(2,1)S(1)}, u32[]{:S(2)}, u32[]{:S(2)}) collective-permute-start(bf16[192,640]{1,0:T(8,128)(2,1)S(1)} %get-tuple-element.53), channel_id=1, source_target_pairs={{0,24},{8,32},{16,40},{24,48},{32,56},{40,64},{48,72},{56,80},{64,... | collective-permute-start | bytes 737288 | tf_op jit(solution)/shard_map/ppermute | solution.py:358
  34.6 8.1 %collective-permute-start.3 = (bf16[192,640]{1,0:T(8,128)(2,1)S(1)}, bf16[192,640]{1,0:T(8,128)(2,1)S(1)}, u32[]{:S(2)}, u32[]{:S(2)}) collective-permute-start(bf16[192,640]{1,0:T(8,128)(2,1)S(1)} %get-tuple-element.53), channel_id=1, source_target_pairs={{0,32},{8,40},{16,48},{24,56},{32,64},{40,72},{48,80},{56,88},{64,... | collective-permute-start | bytes 737288 | tf_op jit(solution)/shard_map/ppermute | solution.py:358
  38.1 6.9 %collective-permute-start.4 = (bf16[64,640]{1,0:T(8,128)(2,1)S(1)}, bf16[64,640]{1,0:T(8,128)(2,1)S(1)}, u32[]{:S(2)}, u32[]{:S(2)}) collective-permute-start(bf16[64,640]{1,0:T(8,128)(2,1)S(1)} %slice.150), channel_id=1, source_target_pairs={{0,40},{8,48},{16,56},{24,64},{32,72},{40,80},{48,88},{56,96},{64,... | collective-permute-start | bytes 245768 | tf_op jit(solution)/shard_map/ppermute | solution.py:358
  45.1 2.6 copy-start.11
  45.1 6.0 %collective-permute-start.8 = (bf16[1216,640]{1,0:T(8,128)(2,1)S(1)}, bf16[1216,640]{1,0:T(8,128)(2,1)S(1)}, u32[]{:S(2)}, u32[]{:S(2)}) collective-permute-start(bf16[1216,640]{1,0:T(8,128)(2,1)S(1)} %get-tuple-element.77), channel_id=1, source_target_pairs={{0,4},{4,0},{1,5},{5,1},{2,6},{6,2},{3,7},{7,3},{8,12},{12,8},{9,1... | collective-permute-start | bytes 4669448 | tf_op jit(solution)/shard_map/ppermute | solution.py:362
  94.1 4.1 %copy-start.4 = (bf16[8192,128]{1,0:T(8,128)(2,1)S(1)}, bf16[8192,128]{1,0:T(8,128)(2,1)}, u32[]{:S(2)}) copy-start(bf16[8192,128]{1,0:T(8,128)(2,1)} %get-tuple-element.39) | copy-start | bytes 6291460
  96.7 21.5 %collective-permute-start.9 = (bf16[1216,512]{1,0:T(8,128)(2,1)}, bf16[1216,512]{1,0:T(8,128)(2,1)}, u32[]{:S(2)}, u32[]{:S(2)}) collective-permute-start(bf16[1216,512]{1,0:T(8,128)(2,1)} %slice.119), channel_id=1, source_target_pairs={{0,4},{4,0},{1,5},{5,1},{2,6},{6,2},{3,7},{7,3},{8,12},{12,8},{9,1... | collective-permute-start | bytes 3735560 | tf_op jit(solution)/shard_map/ppermute | solution.py:362
  104.9 36.1 %all-to-all-start.1 = ((bf16[64,64,128]{2,1,0:T(8,128)(2,1)}), bf16[64,64,128]{2,1,0:T(8,128)(2,1)S(1)}, u32[]{:S(2)}, u32[]{:S(2)}) async-start(bf16[64,64,128]{2,1,0:T(8,128)(2,1)} %bitcast.85), calls=%async_computation.1 | async-start | bytes 2097152 | tf_op jit(solution)/shard_map/all_to_all | solution.py:367
  118.1 199.4 %all-reduce.7.cloned.1.call-start = ((), (), s32[]{:S(2)}) async-start(), calls=%async_computation.4 | async-start | bytes 18350080 | tf_op jit(solution)/shard_map/psum | solution.py:426
  120.8 11.6 %collective-permute-start.14 = (bf16[64,512]{1,0:T(8,128)(2,1)S(1)}, bf16[64,512]{1,0:T(8,128)(2,1)S(1)}, u32[]{:S(2)}, u32[]{:S(2)}) collective-permute-start(bf16[64,512]{1,0:T(8,128)(2,1)S(1)} %get-tuple-element.59), channel_id=1, source_target_pairs={{40,0},{48,8},{56,16},{64,24},{72,32},{80,40},{88,48},{96,56},{104... | collective-permute-start | bytes 196616 | tf_op jit(solution)/shard_map/ppermute | solution.py:358
  122.1 14.7 %collective-permute-start.17 = (bf16[64,512]{1,0:T(8,128)(2,1)S(1)}, bf16[64,512]{1,0:T(8,128)(2,1)S(1)}, u32[]{:S(2)}, u32[]{:S(2)}) collective-permute-start(bf16[64,512]{1,0:T(8,128)(2,1)S(1)} %get-tuple-element.60), channel_id=1, source_target_pairs={{64,0},{72,8},{80,16},{88,24},{96,32},{104,40},{112,48},{120,56},{... | collective-permute-start | bytes 196616 | tf_op jit(solution)/shard_map/ppermute | solution.py:358
  123.4 15.4 %collective-permute-start.16 = (bf16[64,512]{1,0:T(8,128)(2,1)S(1)}, bf16[64,512]{1,0:T(8,128)(2,1)}, u32[]{:S(2)}, u32[]{:S(2)}) collective-permute-start(bf16[64,512]{1,0:T(8,128)(2,1)S(1)} %get-tuple-element.61), channel_id=1, source_target_pairs={{56,0},{64,8},{72,16},{80,24},{88,32},{96,40},{104,48},{112,56},{1... | collective-permute-start | bytes 196616 | tf_op jit(solution)/shard_map/ppermute | solution.py:358
  125.5 27.4 %collective-permute-start.15 = (bf16[64,512]{1,0:T(8,128)(2,1)}, bf16[64,512]{1,0:T(8,128)(2,1)}, u32[]{:S(2)}, u32[]{:S(2)}) collective-permute-start(bf16[64,512]{1,0:T(8,128)(2,1)} %get-tuple-element.62), channel_id=1, source_target_pairs={{48,0},{56,8},{64,16},{72,24},{80,32},{88,40},{96,48},{104,56},{11... | collective-permute-start | bytes 196616 | tf_op jit(solution)/shard_map/ppermute | solution.py:358
  126.8 26.2 %collective-permute-start.10 = (bf16[192,512]{1,0:T(8,128)(2,1)}, bf16[192,512]{1,0:T(8,128)(2,1)}, u32[]{:S(2)}, u32[]{:S(2)}) collective-permute-start(bf16[192,512]{1,0:T(8,128)(2,1)} %get-tuple-element.63), channel_id=1, source_target_pairs={{8,0},{16,8},{24,16},{32,24},{40,32},{48,40},{56,48},{64,56},{72,6... | collective-permute-start | bytes 589832 | tf_op jit(solution)/shard_map/ppermute | solution.py:358
  132.4 20.6 %collective-permute-start.13 = (bf16[192,512]{1,0:T(8,128)(2,1)}, bf16[192,512]{1,0:T(8,128)(2,1)}, u32[]{:S(2)}, u32[]{:S(2)}) collective-permute-start(bf16[192,512]{1,0:T(8,128)(2,1)} %get-tuple-element.64), channel_id=1, source_target_pairs={{32,0},{40,8},{48,16},{56,24},{64,32},{72,40},{80,48},{88,56},{96,... | collective-permute-start | bytes 589832 | tf_op jit(solution)/shard_map/ppermute | solution.py:358
  136.9 16.1 %collective-permute-start.12 = (bf16[192,512]{1,0:T(8,128)(2,1)}, bf16[192,512]{1,0:T(8,128)(2,1)}, u32[]{:S(2)}, u32[]{:S(2)}) collective-permute-start(bf16[192,512]{1,0:T(8,128)(2,1)} %get-tuple-element.65), channel_id=1, source_target_pairs={{24,0},{32,8},{40,16},{48,24},{56,32},{64,40},{72,48},{80,56},{88,... | collective-permute-start | bytes 589832 | tf_op jit(solution)/shard_map/ppermute | solution.py:358
  138.8 14.2 %collective-permute-start.11 = (bf16[192,512]{1,0:T(8,128)(2,1)S(1)}, bf16[192,512]{1,0:T(8,128)(2,1)}, u32[]{:S(2)}, u32[]{:S(2)}) collective-permute-start(bf16[192,512]{1,0:T(8,128)(2,1)S(1)} %get-tuple-element.66), channel_id=1, source_target_pairs={{16,0},{24,8},{32,16},{40,24},{48,32},{56,40},{64,48},{72,56},{80,... | collective-permute-start | bytes 589832 | tf_op jit(solution)/shard_map/ppermute | solution.py:358
  141.0 13.4 %copy-start.5 = (bf16[640,256]{1,0:T(8,128)(2,1)S(1)}, bf16[640,256]{1,0:T(8,128)(2,1)}, u32[]{:S(2)}) copy-start(bf16[640,256]{1,0:T(8,128)(2,1)} %wk_h.1) | copy-start | bytes 983044
  141.2 13.5 %copy-start.6 = (bf16[640,256]{1,0:T(8,128)(2,1)S(1)}, bf16[640,256]{1,0:T(8,128)(2,1)}, u32[]{:S(2)}) copy-start(bf16[640,256]{1,0:T(8,128)(2,1)} %wv_h.1) | copy-start | bytes 983044
  142.5 27.1 %all-to-all-start.2 = ((bf16[64,64,128]{2,1,0:T(8,128)(2,1)}), bf16[64,64,128]{2,1,0:T(8,128)(2,1)S(1)}, u32[]{:S(2)}, u32[]{:S(2)}) async-start(bf16[64,64,128]{2,1,0:T(8,128)(2,1)} %broadcast_in_dim.40), calls=%async_computation.2 | async-start | bytes 2097152 | tf_op jit(solution)/shard_map/all_to_all | solution.py:372
  153.0 1.8 copy-start.8
  153.0 2.2 copy-start.9
  181.1 0.6 copy-start.13
  181.5 1.7 copy-start.7
  181.7 1.9 copy-start
  317.5 3.1 copy-start.3
  320.7 3.1 copy-start.2
  323.7 3.1 copy-start.1
Sparse Core Ops, SparseCore 0:
  141.2 176.3 all-reduce.6

commit v2 on v1

v2 whole, which is shorter than its diff:
```python
import jax
import jax.numpy as jnp
import numpy as np
from jax import lax
from jax.experimental import pallas as pl
from jax.experimental.pallas import tpu as pltpu
from jax.sharding import Mesh, PartitionSpec as P

WINDOW = 1024
SHORT_LEN = 2048
D = 640
HEADS = 4
HD = 256
HALF = 128
FF = 2048
TOK = 192
SHORT = 64
LONG = 128
CHIPS = 16
NEAR = 4
FAR = 8
SIDE = (NEAR + 1) * TOK + (FAR - NEAR) * SHORT
GROUPS = SIDE // SHORT
KEYS_SHORT = 2 * (FAR + 1) * SHORT
KEYS_LONG = 2 * (NEAR + 1) * LONG
KEYS = KEYS_SHORT + KEYS_LONG
FF_CHUNK = 512

epsilon = 1e-06
theta_base = 10000.0
masked_score = -1e30

SEQ = ("x", "z", "core")
CHIP = ("x", "z")
ALL = ("x", "z", "core", "dp")
HALF_FF = FF // 2
AT_GATE, AT_UP, AT_MIXED, AT_NORMED, AT_OUT, AT_BRANCH = 1024, 2048, 3072, 3584, 4224, 4864
ACTS = 5504
A_GATE, A_UP, A_DOWN, A_PROJ, A_GAIN, A_ROWS = 0, 5120, 10240, 15360, 17920, 18432
B_QUERY, B_KV, B_GAIN, B_ROWS = 0, 2560, 3840, 4096
DP = 4
A_DP = 6144
A_XZ = A_ROWS - A_DP
A_DP_PIECE, B_PIECE, A_XZ_PIECE = A_DP // DP, B_ROWS // DP, A_XZ // CHIPS
A_DP_BLOCK, B_BLOCK, A_XZ_BLOCK = A_DP_PIECE // CHIPS, B_PIECE // CHIPS, A_XZ_PIECE // DP
BLOCK = A_DP_BLOCK + B_BLOCK + A_XZ_BLOCK
XZ_FIRST = 208
JOINED = XZ_FIRST - A_DP_BLOCK - B_BLOCK
DP_FIRST = A_XZ_BLOCK - JOINED

bf16 = jnp.bfloat16
f32 = jnp.float32


def mm(left, right):
    return jnp.dot(left, right, preferred_element_type=f32)


def mm_tn(left, right):
    return lax.dot_general(left, right, (((0,), (0,)), ((), ())), preferred_element_type=f32)


def mm_nt(left, right):
    return lax.dot_general(left, right, (((1,), (1,)), ((), ())), preferred_element_type=f32)


def window_groups():
    groups = []
    for behind in range(NEAR + 1):
        groups += [(behind, "short", 0), (behind, "long", 0), (behind, "long", 1)]
    groups += [(behind, "short", 0) for behind in range(NEAR + 1, FAR + 1)]
    return groups


def key_row(side, group):
    behind, kind, part = group
    if kind == "short":
        return side * (KEYS_SHORT // 2) + behind * SHORT
    return KEYS_SHORT + side * (KEYS_LONG // 2) + behind * LONG + part * SHORT


def mask_bias(kind, chip, core):
    rows, width, first_key = (SHORT, KEYS_SHORT, 0) if kind == "short" else (LONG, KEYS_LONG, 0)
    half = width // 2
    column = lax.broadcasted_iota(jnp.int32, (1, width), 1)
    other = (column >= half).astype(jnp.int32)
    inner = column - other * half
    shift = 6 if kind == "short" else 7
    behind = lax.shift_right_logical(inner, shift)
    rest = inner & (rows - 1)
    key_core = core + other * (1 - 2 * core)
    key_position = (2 * (chip - behind) + key_core) * rows + rest
    query_position = (2 * chip + core) * rows + lax.broadcasted_iota(jnp.int32, (rows, 1), 0)
    distance = query_position - key_position
    allowed = (key_position >= 0) & (distance >= 0) & (distance < WINDOW)
    return jnp.where(allowed, 0.0, masked_score).astype(f32)


def group_tables(tables, chip, core, side, group):
    behind, kind, part = group
    piece = 2 * (chip - behind) + (core if side == 0 else 1 - core)
    at = jnp.maximum(piece if kind == "short" else 2 * piece + part, 0)
    cb, sb = tables[0, pl.ds(at, 1), :], tables[1, pl.ds(at, 1), :]
    cr, sr = tables[2], tables[3]
    return cb * cr - sb * sr, sb * cr + cb * sr


def rotary_tables():
    frequency = theta_base ** (-(np.arange(HALF) * 2.0 / HD))
    far = np.arange(SHORT)[:, None] * SHORT * frequency[None, :]
    near = np.arange(SHORT)[:, None] * frequency[None, :]
    return np.stack([np.cos(far), np.sin(far), np.cos(near), np.sin(near)]).astype(np.float32)


def place():
    return lax.axis_index("x") * 4 + lax.axis_index("z"), lax.axis_index("core")


def starts(lengths):
    short_first = (lengths[0, 0] == SHORT_LEN).astype(jnp.int32)
    return pl.multiple_of((1 - short_first) * LONG, SHORT), pl.multiple_of(short_first * SHORT, SHORT)


KINDS = (
    ("short", SHORT, 0, KEYS_SHORT, 0, 0),
    ("long", LONG, KEYS_SHORT, KEYS_LONG, HEADS * SHORT, SHORT),
)


def copies_of(pairs, sems, first=0):
    copies = [
        pltpu.make_async_copy(source, target, sems.at[first + number])
        for number, (source, target) in enumerate(pairs)
    ]
    for copy in copies:
        copy.start()
    return copies


class Stores:
    def __init__(self, sems):
        self.sems, self.copies = sems, []

    def start(self, source, target):
        self.copies += copies_of([(source, target)], self.sems, len(self.copies))

    def wait(self):
        for copy in self.copies:
            copy.wait()


def forward_kernel(
    lengths, tables, ga, gm, w0_h, w1_h, w2_h, w3_h, w4_h, w5_h, w6_h, w7_h, og_h, wq_h, wk_h, wv_h, wo_h, wg_h, wu_h, wd_h,
    ggain_o, q_h, k_h, v_h, gmix_h, norm_h, gres_h, bo_h, skv_h, keep_h, send_h,
    win, og, wq, wk, wv, wo, wg, wu, wd, norm, q, k, v, kv, scores_all, probs_all, mixed, gmix, gres,
    bo, skv, acts, bias_s, bias_l, win_sem, sems, out_sem,
):
    chip, core = place()
    short_at, long_at = starts(lengths)
    window_loads = []
    for side, (known, *rounds) in enumerate(((w0_h, w1_h, w2_h, w3_h), (w4_h, w5_h, w6_h, w7_h))):
        base = side * SIDE
        for source, first, behind in [(known, 0, 0), (known, TOK, NEAR)] + [(r, 0, n + 1) for n, r in enumerate(rounds)]:
            at = base + behind * TOK
            window_loads += [
                (source.at[pl.ds(first + short_at, SHORT)], win.at[pl.ds(at, SHORT)]),
                (source.at[pl.ds(first + long_at, LONG)], win.at[pl.ds(at + SHORT, LONG)]),
            ]
        for source, first, behind in [(known, 2 * TOK, FAR)] + [(r, TOK, NEAR + 1 + n) for n, r in enumerate(rounds)]:
            at = base + (NEAR + 1) * TOK + (behind - NEAR - 1) * SHORT
            window_loads.append((source.at[pl.ds(first, SHORT)], win.at[pl.ds(at, SHORT)]))
    window_loads = copies_of(window_loads, win_sem)
    names = ("wk", "wv", "wq", "wo", "ogs", "ogl", "wg", "wu", "wd")
    loads = dict(zip(names, copies_of((
        (wk_h, wk), (wv_h, wv), (wq_h, wq), (wo_h, wo),
        (og_h.at[pl.ds(short_at, SHORT)], og.at[pl.ds(0, SHORT)]),
        (og_h.at[pl.ds(long_at, LONG)], og.at[pl.ds(SHORT, LONG)]),
        (wg_h, wg), (wu_h, wu), (wd_h, wd),
    ), sems)))
    stores = Stores(out_sem)
    bias_s[...] = mask_bias("short", chip, core)
    bias_l[...] = mask_bias("long", chip, core)
    gain_a = ga[...].reshape(1, D)
    gain_m = gm[...].reshape(1, D)
    for copy in window_loads:
        copy.wait()

    def normalise(step, carry):
        rows = pl.ds(pl.multiple_of(step * SHORT, SHORT), SHORT)
        x = win[rows, :].astype(f32)
        scale = lax.rsqrt(jnp.mean(x * x, axis=-1, keepdims=True) + epsilon)
        norm[rows, :] = (x * scale * gain_a).astype(bf16)
        return carry

    lax.fori_loop(0, 2 * GROUPS, normalise, 0, unroll=2)
    stores.start(norm, norm_h)
    loads["wk"].wait()
    loads["wv"].wait()
    for side in range(2):
        normed = norm[side * SIDE : (side + 1) * SIDE, :]
        kv[:, :HD] = mm(normed, wk[...])
        kv[:, HD:] = mm(normed, wv[...])
        for number, group in enumerate(window_groups()):
            rows = slice(number * SHORT, (number + 1) * SHORT)
            cos, sin = group_tables(tables, chip, core, side, group)
            low_half, high_half = kv[rows, :HALF], kv[rows, HALF:HD]
            at = key_row(side, group)
            k[at : at + SHORT, :HALF] = (low_half * cos - high_half * sin).astype(bf16)
            k[at : at + SHORT, HALF:] = (high_half * cos + low_half * sin).astype(bf16)
            v[at : at + SHORT, :] = kv[rows, HD:].astype(bf16)
            if side == 0 and number < 3:
                skv[rows, :HD] = k[at : at + SHORT, :]
                skv[rows, HD:] = v[at : at + SHORT, :]
    stores.start(k, k_h)
    stores.start(v, v_h)
    stores.start(skv.at[pl.ds(0, SHORT)], skv_h.at[pl.ds(short_at, SHORT)])
    stores.start(skv.at[pl.ds(SHORT, LONG)], skv_h.at[pl.ds(long_at, LONG)])

    loads["wq"].wait()
    query_raw = mm(norm[:TOK, :], wq[...])
    for number in range(3):
        rows = slice(number * SHORT, (number + 1) * SHORT)
        cos, sin = group_tables(tables, chip, core, 0, window_groups()[number])
        for head in range(HEADS):
            low_half = query_raw[rows, head * HD : head * HD + HALF]
            high_half = query_raw[rows, head * HD + HALF : (head + 1) * HD]
            at = head * SHORT if number == 0 else HEADS * SHORT + head * LONG + (number - 1) * SHORT
            q[at : at + SHORT, :HALF] = (low_half * cos - high_half * sin).astype(bf16) * bf16(HD**-0.5)
            q[at : at + SHORT, HALF:] = (high_half * cos + low_half * sin).astype(bf16) * bf16(HD**-0.5)
    stores.start(q, q_h)

    for kind, rows, key_at, width, query_at, row_at in KINDS:
        bias = bias_s if kind == "short" else bias_l
        count = HEADS * rows
        scores_all[:count, :width] = mm_nt(q[query_at : query_at + count, :], k[key_at : key_at + width, :])
        for head in range(HEADS):
            here = slice(head * rows, (head + 1) * rows)
            scores = scores_all[here, :width] + bias[...]
            exponent = jnp.exp(scores - jnp.max(scores, axis=-1, keepdims=True))
            share = 1.0 / jnp.sum(exponent, axis=-1, keepdims=True)
            probs_all[here, :width] = (exponent * share).astype(bf16)
        mixed_all = mm(probs_all[:count, :width], v[key_at : key_at + width, :]).astype(bf16)
        for head in range(HEADS):
            mixed[row_at : row_at + rows, head * HD : (head + 1) * HD] = mixed_all[
                head * rows : (head + 1) * rows, :
            ]

    loads["wo"].wait()
    resid = win[:TOK, :].astype(f32) + mm(mixed[...], wo[...])
    scale = lax.rsqrt(jnp.mean(resid * resid, axis=-1, keepdims=True) + epsilon)
    unit = resid * scale
    normed_mlp = (unit * gain_m).astype(bf16)
    for name in ("ogs", "ogl", "wg", "wu", "wd"):
        loads[name].wait()
    grad_out = og[...]
    for half in range(2):
        acts[half, :, AT_MIXED:AT_NORMED] = mixed[:, half * 2 * HD : (half + 1) * 2 * HD]
        acts[half, :, AT_NORMED:AT_OUT] = normed_mlp
        acts[half, :, AT_OUT:AT_BRANCH] = grad_out
    block_out = resid
    grad_normed = jnp.zeros((TOK, D), f32)
    for chunk in range(FF // FF_CHUNK):
        cols = slice(chunk * FF_CHUNK, (chunk + 1) * FF_CHUNK)
        gate = mm(normed_mlp, wg[:, cols])
        up = mm(normed_mlp, wu[:, cols])
        sig = jax.nn.sigmoid(gate)
        silu = gate * sig
        act = (silu * up).astype(bf16)
        grad_act = mm_nt(grad_out, wd[cols, :])
        grad_gate = (grad_act * up * sig * (1.0 + gate * (1.0 - sig))).astype(bf16)
        grad_up = (grad_act * silu).astype(bf16)
        block_out = block_out + mm(act, wd[cols, :])
        grad_normed = grad_normed + mm_nt(grad_gate, wg[:, cols]) + mm_nt(grad_up, wu[:, cols])
        half, at = chunk // 2, (chunk % 2) * FF_CHUNK
        acts[half, :, at : at + FF_CHUNK] = act
        acts[half, :, AT_GATE + at : AT_GATE + at + FF_CHUNK] = grad_gate
        acts[half, :, AT_UP + at : AT_UP + at + FF_CHUNK] = grad_up
    stores.start(acts.at[1 - core, :, pl.ds(0, AT_BRANCH)], send_h.at[:, pl.ds(0, AT_BRANCH)])
    stores.start(acts.at[core, :, pl.ds(0, AT_BRANCH)], keep_h.at[:, pl.ds(0, AT_BRANCH)])
    ggain_o[...] = jnp.sum(grad_normed * unit, axis=0, keepdims=True)
    scaled = grad_normed * gain_m
    grad_resid = grad_out.astype(f32) + scale * (
        scaled - unit * jnp.mean(scaled * unit, axis=-1, keepdims=True)
    )
    grad_branch = grad_resid.astype(bf16)
    for half in range(2):
        acts[half, :, AT_BRANCH:] = grad_branch
    rest = pl.ds(AT_BRANCH, ACTS - AT_BRANCH)
    stores.start(acts.at[1 - core, :, rest], send_h.at[:, rest])
    stores.start(acts.at[core, :, rest], keep_h.at[:, rest])
    gres[...] = grad_resid
    stores.start(gres, gres_h)
    bo[...] = block_out.astype(bf16)
    stores.start(bo.at[pl.ds(0, SHORT)], bo_h.at[pl.ds(short_at, SHORT)])
    stores.start(bo.at[pl.ds(SHORT, LONG)], bo_h.at[pl.ds(long_at, LONG)])
    grad_mixed = mm_nt(grad_branch, wo[...]).astype(bf16)
    for head in range(HEADS):
        cols = slice(head * HD, (head + 1) * HD)
        gmix[head * SHORT : (head + 1) * SHORT, :] = grad_mixed[:SHORT, cols]
        at = HEADS * SHORT + head * LONG
        gmix[at : at + LONG, :] = grad_mixed[SHORT:, cols]
    stores.start(gmix, gmix_h)
    stores.wait()


def backward_kernel(
    tables, ga, q_h, k_h, v_h, gmix_h, norm_h, wq_h, wk_h, wv_h,
    gain_o, mine_h, other_h, gq_h, gnq_h,
    q, k, v, gmix, norm, wq, wk, wv, scores_all, gp_all, probs_all, gs_all, ret, gq, gnq, bias_s, bias_l,
    sems, out_sem,
):
    chip, core = place()
    loads = copies_of((
        (q_h, q), (k_h, k), (gmix_h, gmix), (v_h, v), (norm_h, norm), (wq_h, wq), (wk_h, wk), (wv_h, wv),
    ), sems)
    stores = Stores(out_sem)
    bias_s[...] = mask_bias("short", chip, core)
    bias_l[...] = mask_bias("long", chip, core)
    for copy in loads[:4]:
        copy.wait()
    for kind, rows, key_at, width, query_at, row_at in KINDS:
        bias = bias_s if kind == "short" else bias_l
        keys = k[key_at : key_at + width, :]
        count = HEADS * rows
        stack = slice(query_at, query_at + count)
        scores_all[:count, :width] = mm_nt(q[stack, :], keys)
        gp_all[:count, :width] = mm_nt(gmix[stack, :], v[key_at : key_at + width, :])
        for head in range(HEADS):
            here = slice(head * rows, (head + 1) * rows)
            scores = scores_all[here, :width] + bias[...]
            exponent = jnp.exp(scores - jnp.max(scores, axis=-1, keepdims=True))
            probs = exponent * (1.0 / jnp.sum(exponent, axis=-1, keepdims=True))
            probs_all[here, :width] = probs.astype(bf16)
            grad_probs = gp_all[here, :width]
            inner = jnp.sum(probs * grad_probs, axis=-1, keepdims=True)
            gs_all[here, :width] = (probs * (grad_probs - inner)).astype(bf16)
        grad_queries = mm(gs_all[:count, :width], keys) * (HD**-0.5)
        for head in range(HEADS):
            for part in range(rows // SHORT):
                number = 0 if kind == "short" else 1 + part
                cos, sin = group_tables(tables, chip, core, 0, window_groups()[number])
                at = head * rows + part * SHORT
                low_half = grad_queries[at : at + SHORT, :HALF]
                high_half = grad_queries[at : at + SHORT, HALF:]
                to = slice(row_at + part * SHORT, row_at + (part + 1) * SHORT)
                gq[to, head * HD : head * HD + HALF] = (low_half * cos + high_half * sin).astype(bf16)
                gq[to, head * HD + HALF : (head + 1) * HD] = (high_half * cos - low_half * sin).astype(bf16)
        grad_keys = mm_tn(gs_all[:count, :width], q[stack, :])
        grad_values = mm_tn(probs_all[:count, :width], gmix[stack, :])
        for side in range(2):
            for number, group in enumerate(window_groups()):
                if group[1] != kind:
                    continue
                at = key_row(side, group) - key_at
                cos, sin = group_tables(tables, chip, core, side, group)
                low_half = grad_keys[at : at + SHORT, :HALF]
                high_half = grad_keys[at : at + SHORT, HALF:]
                to = slice(number * SHORT, (number + 1) * SHORT)
                ret[side, to, :HALF] = (low_half * cos + high_half * sin).astype(bf16)
                ret[side, to, HALF:HD] = (high_half * cos - low_half * sin).astype(bf16)
                ret[side, to, HD:] = grad_values[at : at + SHORT, :].astype(bf16)
    stores.start(ret.at[0], mine_h)
    stores.start(ret.at[1], other_h)
    stores.start(gq, gq_h)
    for copy in loads[4:]:
        copy.wait()
    gnq[...] = mm_nt(gq[...], wq[...])
    stores.start(gnq, gnq_h)
    grad_gain = jnp.sum(gnq[...] * norm[:TOK, :].astype(f32), axis=0, keepdims=True)
    for step in range(8):
        side, first = step // 4, step % 4 * (SIDE // 4)
        rows = slice(first, first + SIDE // 4)
        grad_normed = mm_nt(ret[side, rows, :HD], wk[...]) + mm_nt(ret[side, rows, HD:], wv[...])
        here = norm[side * SIDE + first : side * SIDE + first + SIDE // 4, :].astype(f32)
        grad_gain = grad_gain + jnp.sum(grad_normed * here, axis=0, keepdims=True)
    gain_o[...] = grad_gain / ga[...].reshape(1, D)
    stores.wait()


def project_kernel(gain, norm_h, mine_h, other_h, gq_h, keep_h, send_h, norm, ret, gq, b, sems, out_sem):
    core = lax.axis_index("core")
    loads = copies_of((
        (norm_h.at[pl.ds(0, SIDE)], norm.at[0]), (gq_h, gq), (mine_h, ret.at[0]),
        (norm_h.at[pl.ds(SIDE, SIDE)], norm.at[1]), (other_h, ret.at[1]),
    ), sems)
    stores = Stores(out_sem)

    def put(half, at, block):
        for part in range(block.shape[1] // HALF):
            row = at + part * D
            b[half, row : row + D, :] = block[:, part * HALF : (part + 1) * HALF].astype(bf16)

    b[0, B_GAIN:, :] = jnp.zeros((B_ROWS - B_GAIN, HALF), bf16)
    b[1, B_GAIN:, :] = jnp.zeros((B_ROWS - B_GAIN, HALF), bf16)
    for part in range(D // HALF):
        b[0, B_GAIN + 16 * part : B_GAIN + 16 * part + 16, :] = jnp.broadcast_to(
            gain[:, part * HALF : (part + 1) * HALF], (16, HALF)
        ).astype(bf16)
    for copy in loads[:2]:
        copy.wait()
    for half in range(2):
        put(half, B_QUERY, mm_tn(norm[0, :TOK, :], gq[:, half * 2 * HD : (half + 1) * 2 * HD]))
    for copy in loads[2:]:
        copy.wait()
    both = mm_tn(norm[0], ret[0]) + mm_tn(norm[1], ret[1])
    for half in range(2):
        put(half, B_KV, both[:, half * HD : (half + 1) * HD])
    stores.start(b.at[1 - core], send_h)
    stores.start(b.at[core], keep_h)
    stores.wait()


def pieces_out(stores, pieces, outs):
    me = lax.axis_index("dp")
    for step, out in enumerate(outs):
        stores.start(pieces.at[lax.rem(me + step, DP)], out)


def halves_kernel(ggain, keep_h, recv_h, p0_h, p1_h, p2_h, p3_h, xz_h, x, pieces, xz, sems, out_sem):
    copies = copies_of(((keep_h, x.at[pl.ds(0, TOK)]), (recv_h, x.at[pl.ds(TOK, TOK)])), sems)
    stores = Stores(out_sem)
    for copy in copies:
        copy.wait()

    def write(at, values):
        done, rows = 0, values.shape[0]
        while done < rows:
            row = at + done
            if row < A_DP:
                piece, inner = row // A_DP_PIECE, row % A_DP_PIECE
                size = min(rows - done, A_DP_PIECE - inner)
                pieces[piece, inner : inner + size, :] = values[done : done + size, :]
            else:
                piece, inner = (row - A_DP) // A_XZ_PIECE, (row - A_DP) % A_XZ_PIECE
                size = min(rows - done, A_XZ_PIECE - inner)
                xz[piece, inner : inner + size, :] = values[done : done + size, :]
            done += size

    def put(at, block):
        rows = block.shape[0]
        for part in range(block.shape[1] // HALF):
            write(at + part * rows, block[:, part * HALF : (part + 1) * HALF].astype(bf16))

    normed = x[:, AT_NORMED:AT_OUT]
    for chunk in range(2):
        cols = slice(AT_GATE + chunk * FF_CHUNK, AT_GATE + (chunk + 1) * FF_CHUNK)
        put(A_GATE + chunk * 4 * D, mm_tn(normed, x[:, cols]))
    for chunk in range(2):
        cols = slice(AT_UP + chunk * FF_CHUNK, AT_UP + (chunk + 1) * FF_CHUNK)
        put(A_UP + chunk * 4 * D, mm_tn(normed, x[:, cols]))
        if chunk == 0:
            pieces_out(stores, pieces, (p0_h, p1_h, p2_h, p3_h))
    put(A_DOWN, mm_tn(x[:, :AT_GATE], x[:, AT_OUT:AT_BRANCH]))
    put(A_PROJ, mm_tn(x[:, AT_MIXED:AT_NORMED], x[:, AT_BRANCH:]))
    for part in range(D // HALF):
        write(A_GAIN + 16 * part, jnp.broadcast_to(
            ggain[:, part * HALF : (part + 1) * HALF], (16, HALF)
        ).astype(bf16))
    end = A_GAIN + 16 * (D // HALF)
    write(end, jnp.zeros((A_ROWS - end, HALF), bf16))
    stores.start(xz, xz_h)
    stores.wait()


def chip_sum_kernel(keep, recv, p0_h, p1_h, p2_h, p3_h, pieces, out_sem):
    stores = Stores(out_sem)
    for piece in range(DP):
        rows = slice(piece * B_PIECE, (piece + 1) * B_PIECE)
        pieces[piece] = (keep[rows, :].astype(f32) + recv[rows, :].astype(f32)).astype(bf16)
    pieces_out(stores, pieces, (p0_h, p1_h, p2_h, p3_h))
    stores.wait()


def first_sum_kernel(
    a0, a1, a2, a3, b0, b1, b2, b3, xz, out_xz, p0_h, p1_h, p2_h, p3_h, pieces, out_sem
):
    stores = Stores(out_sem)
    for piece in range(DP):
        rows = slice(piece * A_XZ_BLOCK, (piece + 1) * A_XZ_BLOCK)
        total = xz[0, rows, :].astype(f32)
        for chip in range(1, CHIPS):
            total = total + xz[chip, rows, :].astype(f32)
        pieces[piece] = total.astype(bf16)
    pieces_out(stores, pieces, (p0_h, p1_h, p2_h, p3_h))
    for chip in range(CHIPS):
        for at, size, parts in ((0, A_DP_BLOCK, (a0, a1, a2, a3)), (A_DP_BLOCK, B_BLOCK, (b0, b1, b2, b3))):
            rows = slice(chip * size, (chip + 1) * size)
            total = (parts[0][rows, :].astype(f32) + parts[1][rows, :].astype(f32)) + (
                parts[2][rows, :].astype(f32) + parts[3][rows, :].astype(f32)
            )
            out_xz[chip, at : at + size, :] = total.astype(bf16)
    stores.wait()


def second_sum_kernel(xz, c0, c1, c2, c3, copies_h, own, total, out_sem):
    stores = Stores(out_sem)
    rest = (
        (c0[...].astype(f32) + c1[...].astype(f32)) + (c2[...].astype(f32) + c3[...].astype(f32))
    ).astype(bf16)
    own[...] = rest[JOINED:, :]
    value = xz[0].astype(f32)
    for chip in range(1, CHIPS):
        value = value + xz[chip].astype(f32)
    total[: XZ_FIRST - JOINED, :] = value.astype(bf16)
    total[XZ_FIRST - JOINED :, :] = rest[:JOINED, :]
    for chip in range(CHIPS):
        stores.start(total, copies_h.at[chip])
    stores.wait()


def spread_kernel(d0, d1, d2, d3, copies_h, rows, out_sem):
    stores = Stores(out_sem)
    me = lax.axis_index("dp")
    for step, part in enumerate((d0, d1, d2, d3)):
        rows[lax.rem(me + DP - step, DP)] = part[...]
    for chip in range(CHIPS):
        stores.start(rows, copies_h.at[chip])
    stores.wait()


def unpack_kernel(
    e0_h, e1_h, e2_h, e3_h, f_h, o0_h, o1_h, o2_h, o3_h, p_h,
    gain_a_o, gain_m_o, gate_h, up_h, down_h, proj_h, query_h, key_h, value_h,
    a_dp, a_xz, b, gate, up, down, proj, query, key, value, sems, out_sem,
):
    mine, me = lax.axis_index("core"), lax.axis_index("dp")
    sides = ((mine, (e0_h, e1_h, e2_h, e3_h), f_h), (1 - mine, (o0_h, o1_h, o2_h, o3_h), p_h))
    firsts, seconds, thirds = [], [], []
    for side, parts, xz_h in sides:
        for step, part in enumerate(parts):
            dp = lax.rem(me + DP - step, DP)
            firsts.append((part.at[:, pl.ds(0, A_DP_BLOCK)], a_dp.at[side, dp]))
            seconds.append((part.at[:, pl.ds(A_DP_BLOCK, B_BLOCK)], b.at[side, dp]))
            thirds.append((part.at[:, pl.ds(XZ_FIRST - JOINED, JOINED)], a_xz.at[side, :, dp, pl.ds(0, JOINED)]))
        thirds.append((xz_h, a_xz.at[side, :, :, pl.ds(JOINED, DP_FIRST)]))
    loads = copies_of(firsts + seconds + thirds, sems)
    stores = Stores(out_sem)

    def pieces_of(core, at, rows, in_b):
        done = 0
        while done < rows:
            row = at + done
            if in_b:
                source, size = b, B_BLOCK
                index = (core, row // B_PIECE, row % B_PIECE // B_BLOCK)
            elif row < A_DP:
                source, size = a_dp, A_DP_BLOCK
                index = (core, row // A_DP_PIECE, row % A_DP_PIECE // A_DP_BLOCK)
            else:
                row = row - A_DP
                source, size = a_xz, A_XZ_BLOCK
                index = (core, row // A_XZ_PIECE, row % A_XZ_PIECE // A_XZ_BLOCK)
            inner = row % size
            size = min(rows - done, size - inner)
            yield done, size, source[index + (slice(inner, inner + size), slice(None))].astype(f32)
            done += size

    def unpack(target, at, rows, in_b, place_of, count, cores=(0, 1)):
        for core in cores:
            for part in range(count):
                row, col = place_of(core, part)
                for done, size, values in pieces_of(core, at + part * rows, rows, in_b):
                    target[row + done : row + done + size, col : col + HALF] = values

    for copy in loads[: 2 * DP]:
        copy.wait()
    unpack(gate, A_GATE, D, False, lambda core, part: (0, core * HALF_FF + part * HALF), HALF_FF // HALF)
    stores.start(gate, gate_h)
    for copy in loads[2 * DP : 4 * DP]:
        copy.wait()
    unpack(query, B_QUERY, D, True, lambda core, part: (0, core * 2 * HD + part * HALF), 4)
    stores.start(query, query_h)
    unpack(key, B_KV, D, True, lambda core, part: (0, part * HALF), 2, (0,))
    stores.start(key, key_h)
    unpack(value, B_KV, D, True, lambda core, part: (0, part * HALF), 2, (1,))
    stores.start(value, value_h)
    for copy in loads[4 * DP :]:
        copy.wait()
    unpack(up, A_UP, D, False, lambda core, part: (0, core * HALF_FF + part * HALF), HALF_FF // HALF)
    stores.start(up, up_h)
    unpack(down, A_DOWN, HALF_FF, False, lambda core, part: (core * HALF_FF, part * HALF), D // HALF)
    stores.start(down, down_h)
    unpack(proj, A_PROJ, 2 * HD, False, lambda core, part: (core * 2 * HD, part * HALF), D // HALF)
    stores.start(proj, proj_h)
    for out, at, in_b in ((gain_a_o, B_GAIN, True), (gain_m_o, A_GAIN, False)):
        for part in range(D // HALF):
            (_, _, first), = pieces_of(0, at + 16 * part, 1, in_b)
            (_, _, second), = pieces_of(1, at + 16 * part, 1, in_b)
            out[part * HALF : (part + 1) * HALF] = (first + second).reshape(HALF)
    stores.wait()


VMEM = pl.BlockSpec(memory_space=pltpu.VMEM)
SMEM = pl.BlockSpec(memory_space=pltpu.SMEM)
ANY = pl.BlockSpec(memory_space=pl.ANY)


def shape(dims, kind=bf16):
    return jax.ShapeDtypeStruct(dims, kind)


def limit(mib):
    return pltpu.CompilerParams(vmem_limit_bytes=mib * 2**20)


def cost(flops, moved):
    return pl.CostEstimate(flops=flops, bytes_accessed=moved, transcendentals=0)


def scratch(*dims, kind=bf16):
    return pltpu.VMEM(dims, kind)


def semaphores(count):
    return pltpu.SemaphoreType.DMA((count,))


def run_forward(*operands):
    return pl.pallas_call(
        forward_kernel,
        in_specs=[SMEM] + [VMEM] * 3 + [ANY] * 16,
        out_specs=[VMEM] + [ANY] * 10,
        out_shape=[
            shape((1, D), f32),
            shape((HEADS * TOK, HD)), shape((KEYS, HD)), shape((KEYS, HD)), shape((HEADS * TOK, HD)),
            shape((2 * SIDE, D)), shape((TOK, D), f32),
            shape((TOK, D)), shape((TOK, 2 * HD)), shape((TOK, ACTS)), shape((TOK, ACTS)),
        ],
        scratch_shapes=[
            scratch(2 * SIDE, D), scratch(TOK, D), scratch(D, HEADS * HD), scratch(D, HD), scratch(D, HD),
            scratch(HEADS * HD, D), scratch(D, FF), scratch(D, FF), scratch(FF, D),
            scratch(2 * SIDE, D), scratch(HEADS * TOK, HD), scratch(KEYS, HD), scratch(KEYS, HD),
            scratch(SIDE, 2 * HD, kind=f32), scratch(HEADS * LONG, KEYS_LONG, kind=f32),
            scratch(HEADS * LONG, KEYS_LONG), scratch(TOK, HEADS * HD), scratch(HEADS * TOK, HD),
            scratch(TOK, D, kind=f32), scratch(TOK, D), scratch(TOK, 2 * HD), scratch(2, TOK, ACTS),
            scratch(SHORT, KEYS_SHORT, kind=f32), scratch(LONG, KEYS_LONG, kind=f32),
            semaphores(28), semaphores(9), semaphores(14),
        ],
        compiler_params=limit(58),
        cost_estimate=cost(8 * 10**9, 3 * 10**7),
        name="forward",
    )(*operands)


def run_backward(*operands):
    return pl.pallas_call(
        backward_kernel,
        in_specs=[VMEM] * 2 + [ANY] * 8,
        out_specs=[VMEM] + [ANY] * 4,
        out_shape=[
            shape((1, D), f32), shape((SIDE, 2 * HD)), shape((SIDE, 2 * HD)), shape((TOK, HEADS * HD)),
            shape((TOK, D), f32),
        ],
        scratch_shapes=[
            scratch(HEADS * TOK, HD), scratch(KEYS, HD), scratch(KEYS, HD), scratch(HEADS * TOK, HD),
            scratch(2 * SIDE, D), scratch(D, HEADS * HD), scratch(D, HD), scratch(D, HD),
            scratch(HEADS * LONG, KEYS_LONG, kind=f32), scratch(HEADS * LONG, KEYS_LONG, kind=f32),
            scratch(HEADS * LONG, KEYS_LONG), scratch(HEADS * LONG, KEYS_LONG),
            scratch(2, SIDE, 2 * HD), scratch(TOK, HEADS * HD), scratch(TOK, D, kind=f32),
            scratch(SHORT, KEYS_SHORT, kind=f32), scratch(LONG, KEYS_LONG, kind=f32),
            semaphores(8), semaphores(4),
        ],
        compiler_params=limit(54),
        cost_estimate=cost(10**12, 10**9),
        name="backward",
    )(*operands)


def run_project(*operands):
    return pl.pallas_call(
        project_kernel,
        in_specs=[VMEM] + [ANY] * 4,
        out_specs=[ANY] * 2,
        out_shape=[shape((B_ROWS, HALF)), shape((B_ROWS, HALF))],
        scratch_shapes=[
            scratch(2, SIDE, D), scratch(2, SIDE, 2 * HD), scratch(TOK, HEADS * HD),
            scratch(2, B_ROWS, HALF), semaphores(5), semaphores(2),
        ],
        compiler_params=limit(54),
        cost_estimate=cost(10**12, 10**9),
        name="project",
    )(*operands)


def run_halves(*operands):
    return pl.pallas_call(
        halves_kernel,
        in_specs=[VMEM, ANY, ANY],
        out_specs=[ANY] * 5,
        out_shape=[shape((A_DP_PIECE, HALF))] * 4 + [shape((CHIPS, A_XZ_PIECE, HALF))],
        scratch_shapes=[
            scratch(2 * TOK, ACTS), scratch(DP, A_DP_PIECE, HALF), scratch(CHIPS, A_XZ_PIECE, HALF),
            semaphores(2), semaphores(5),
        ],
        compiler_params=limit(20),
        cost_estimate=cost(2 * 10**9, 10**7),
        name="halves",
    )(*operands)


def run_chip_sum(*operands):
    return pl.pallas_call(
        chip_sum_kernel,
        in_specs=[VMEM] * 2,
        out_specs=[ANY] * 4,
        out_shape=[shape((B_PIECE, HALF))] * 4,
        scratch_shapes=[scratch(DP, B_PIECE, HALF), semaphores(4)],
        compiler_params=limit(8),
        cost_estimate=cost(10**6, 4 * 10**6),
        name="chip_sum",
    )(*operands)


def run_first_sum(*operands):
    return pl.pallas_call(
        first_sum_kernel,
        in_specs=[VMEM] * 9,
        out_specs=[VMEM] + [ANY] * 4,
        out_shape=[shape((CHIPS, A_DP_BLOCK + B_BLOCK, HALF))] + [shape((A_XZ_BLOCK, HALF))] * 4,
        scratch_shapes=[scratch(DP, A_XZ_BLOCK, HALF), semaphores(4)],
        compiler_params=limit(12),
        cost_estimate=cost(10**6, 8 * 10**6),
        name="first_sum",
    )(*operands)


def run_second_sum(*operands):
    return pl.pallas_call(
        second_sum_kernel,
        in_specs=[VMEM] * 5,
        out_specs=[ANY, VMEM],
        out_shape=[shape((CHIPS, XZ_FIRST, HALF)), shape((DP_FIRST, HALF))],
        scratch_shapes=[scratch(XZ_FIRST, HALF), semaphores(CHIPS)],
        compiler_params=limit(4),
        cost_estimate=cost(10**6, 10**6),
        name="second_sum",
    )(*operands)


def run_spread(*operands):
    return pl.pallas_call(
        spread_kernel,
        in_specs=[VMEM] * 4,
        out_specs=ANY,
        out_shape=shape((CHIPS, DP, DP_FIRST, HALF)),
        scratch_shapes=[scratch(DP, DP_FIRST, HALF), semaphores(CHIPS)],
        compiler_params=limit(4),
        cost_estimate=cost(0, 10**6),
        name="spread",
    )(*operands)


def run_unpack(*operands):
    return pl.pallas_call(
        unpack_kernel,
        in_specs=[ANY] * 10,
        out_specs=[VMEM] * 2 + [ANY] * 7,
        out_shape=[
            shape((D,), f32), shape((D,), f32), shape((D, FF), f32), shape((D, FF), f32),
            shape((FF, D), f32), shape((HEADS * HD, D), f32), shape((D, HEADS * HD), f32),
            shape((D, HD), f32), shape((D, HD), f32),
        ],
        scratch_shapes=[
            scratch(2, DP, CHIPS, A_DP_BLOCK, HALF), scratch(2, CHIPS, DP, A_XZ_BLOCK, HALF),
            scratch(2, DP, CHIPS, B_BLOCK, HALF),
            scratch(D, FF, kind=f32), scratch(D, FF, kind=f32), scratch(FF, D, kind=f32),
            scratch(HEADS * HD, D, kind=f32), scratch(D, HEADS * HD, kind=f32), scratch(D, HD, kind=f32),
            scratch(D, HD, kind=f32), semaphores(26), semaphores(7),
        ],
        compiler_params=limit(40),
        cost_estimate=cost(0, 3 * 10**7),
        name="unpack",
    )(*operands)


def swap_cores(array):
    return lax.ppermute(array, "core", [(0, 1), (1, 0)])


def gather_dp(pieces):
    got = [pieces[0]]
    for step in range(1, DP):
        got.append(lax.ppermute(pieces[step], "dp", [(i, (i + step) % DP) for i in range(DP)]))
    return got


def shards(
    tokens, lengths, w_query, w_key, w_value, w_output, w_gate, w_up, w_down, gain_attn, gain_mlp, out_grad
):
    short_first = lengths[0, 0] == SHORT_LEN

    def to_slots(rows):
        return jnp.where(
            short_first, rows, jnp.concatenate([rows[SHORT:], rows[:SHORT]], axis=0)
        )

    slots = tokens[0]
    short_at = jnp.where(short_first, 0, LONG)

    def short_of(rows):
        return lax.dynamic_slice_in_dim(rows, short_at, SHORT, 0)

    own_short = short_of(slots)
    back = lax.ppermute(slots, "x", [(i, i + 1) for i in range(3)])
    back_short = lax.ppermute(own_short, "x", [(i, i + 2) for i in range(2)])
    here = jnp.concatenate([slots, short_of(back)], axis=0)
    there = jnp.concatenate([back, back_short], axis=0)
    ahead = lax.axis_index("z")
    rounds = [
        lax.ppermute(
            jnp.where(ahead + step < 4, here, there), "z", [(i, (i + step) % 4) for i in range(4)]
        )
        for step in range(1, 4)
    ]
    known = jnp.concatenate([slots, there], axis=0)
    window = [known, *rounds, *[swap_cores(part) for part in (known, *rounds)]]
    tables = jnp.asarray(rotary_tables())
    (
        grad_gain_mlp, q, k, v, gmix, norm, grad_resid, block_out, shared_kv, kept, sent,
    ) = run_forward(
        lengths, tables, gain_attn, gain_mlp, *window, out_grad[0],
        w_query, w_key, w_value, w_output, w_gate, w_up, w_down,
    )
    *a_pieces, a_xz = run_halves(grad_gain_mlp, kept, swap_cores(sent))
    q, a_xz = lax.optimization_barrier((q, a_xz))
    a_xz = lax.all_to_all(a_xz, CHIP, 0, 0, tiled=True)
    a_got = gather_dp(a_pieces)
    gain_part, mine, other, gq, grad_normed_q = run_backward(
        tables, gain_attn, q, k, v, gmix, norm, w_query, w_key, w_value
    )
    gq, *a_got = lax.optimization_barrier((gq, *a_got))
    b_kept, b_sent = run_project(gain_part, norm, mine, other, gq)
    b_got = gather_dp(run_chip_sum(b_kept, swap_cores(b_sent)))

    chip_sum = (mine.astype(f32) + swap_cores(other).astype(f32)).astype(bf16)
    def near(behind):
        return chip_sum[behind * TOK : (behind + 1) * TOK]

    def far(behind):
        at = (NEAR + 1) * TOK + (behind - NEAR - 1) * SHORT
        return chip_sum[at : at + SHORT]

    def padded(short):
        return jnp.pad(short, ((0, LONG), (0, 0)))

    grad_kv = near(0).astype(f32)
    for_back = near(NEAR).astype(f32)
    for_far_back = far(FAR).astype(f32)
    for step in range(1, 4):
        sent_back = jnp.concatenate([near(step), far(NEAR + step)], axis=0)
        came = lax.ppermute(sent_back, "z", [(i, (i - step) % 4) for i in range(4)]).astype(f32)
        same = ahead + step < 4
        came_near, came_far = came[:TOK], came[TOK:]
        grad_kv = grad_kv + jnp.where(same, came_near, 0.0)
        for_back = for_back + jnp.where(same, padded(came_far), came_near)
        for_far_back = for_far_back + jnp.where(same, 0.0, came_far)
    for_back, for_far_back = for_back.astype(bf16), for_far_back.astype(bf16)
    first, *c_pieces = run_first_sum(*a_got, *b_got, a_xz)
    c_got = gather_dp(c_pieces)
    first = lax.all_to_all(first, CHIP, 0, 0, tiled=True)
    copies, own_xz = run_second_sum(first, *c_got)
    copies, grad_kv, for_back, for_far_back = lax.optimization_barrier((copies, grad_kv, for_back, for_far_back))
    from_back = lax.ppermute(for_back, "x", [(i + 1, i) for i in range(3)])
    from_far_back = lax.ppermute(for_far_back, "x", [(i + 2, i) for i in range(2)])

    dp_part = lax.all_to_all(copies, CHIP, 0, 0, tiled=True)
    xz_copies = run_spread(*gather_dp([own_xz] * DP))
    dp_part, xz_copies, from_back, from_far_back = lax.optimization_barrier(
        (dp_part, xz_copies, from_back, from_far_back)
    )
    dp_parts = gather_dp([dp_part] * DP)
    xz_parts = lax.all_to_all(xz_copies, CHIP, 0, 0, tiled=True)
    parts = [*dp_parts, xz_parts]
    parts = list(lax.optimization_barrier(tuple(parts)))
    (
        total_gain_attn, total_gain_mlp, grad_gate, grad_up, grad_down, grad_proj, grad_query, grad_key, grad_value,
    ) = run_unpack(*parts, *[swap_cores(part) for part in parts])

    grad_kv = grad_kv + from_back.astype(f32) + padded(from_far_back.astype(f32))
    grad_kv = grad_kv.astype(bf16)
    grad_normed = grad_normed_q + mm_nt(grad_kv[:, :HD], w_key) + mm_nt(grad_kv[:, HD:], w_value)
    own = jnp.where(short_first, slots, jnp.concatenate([slots[LONG:], slots[:LONG]], axis=0))
    wide = own.astype(f32)
    scale = lax.rsqrt(jnp.mean(wide * wide, axis=-1, keepdims=True) + epsilon)
    unit = wide * scale
    scaled = grad_normed * gain_attn
    input_grad = to_slots(
        grad_resid + scale * (scaled - unit * jnp.mean(scaled * unit, axis=-1, keepdims=True))
    )

    return (
        block_out[None], shared_kv[None], input_grad[None],
        grad_query, grad_key, grad_value, grad_proj, grad_gate, grad_up, grad_down,
        total_gain_attn, total_gain_mlp,
    )


def solution(mesh):
    fine = Mesh(mesh.devices.reshape(4, 4, 2, 4), ALL)
    rows = P("dp", SEQ, None)
    return jax.shard_map(
        shards,
        mesh=fine,
        in_specs=(rows, P("dp", None)) + (P(),) * 9 + (rows,),
        out_specs=(rows, rows, rows) + (P(),) * 9,
        check_vma=False,
    )
```

time: 339 us -> 245 us (0.72)
  waiting for transfers between devices: 156 us -> 78.4 us
  Pallas kernels: 41.7 us -> 62.6 us
  blocking collectives: 15.9 us -> 0 us
  other arithmetic: 24.2 us -> 9.74 us
  between operations: 15.3 us -> 1.99 us
  starting transfers between devices: 71.7 us -> 79.5 us
  local copies, waits for them, and re-layouts: 11.1 us -> 7.28 us
    psum x1 -> x0, waiting for transfers between devices: 133 us -> none  [shards(): totals = lax.psum((g_gate, g_up, g_down, g_proj), ALL)]
    ppermute x16 -> x25, waiting for transfers between devices: 9.1 us -> 68.8 us  [the longest x15 56.4 us: gather_dp(): lax.ppermute(pieces[step], 'dp', [(i, (i + step) % DP) for i in range(DP)])]
    pallas_call x2 -> x9, Pallas kernels: 41.7 us -> 62.6 us  [the longest x1 22.1 us: run_forward(): pl.pallas_call(forward_kernel, in_specs=[SMEM] + [VMEM] * 3 + [ANY] * 16,...]
    all_to_all x2 -> x0, blocking collectives: 15.9 us -> none  [the longest x1 10.9 us: spread(): got = lax.all_to_all(copies, axes, 0, 0, tiled=True)]
    ppermute x2 -> x12, starting transfers between devices: 4.17 us -> 18 us  [swap_cores(): return lax.ppermute(array, 'core', [(0, 1), (1, 0)])]
    all_to_all x2 -> x4, waiting for transfers between devices: 13.3 us -> 0.01 us  [the longest x1 0.01 us: shards(): first = lax.all_to_all(first, CHIP, 0, 0, tiled=True)]
    convert_element_type x7 -> x6, other arithmetic: 14.4 us -> 3.82 us  [the longest x1 1.63 us: shards(): chip_sum = (mine.astype(f32) + swap_cores(other).astype(f32)).astype(bf16)]
    ppermute x2 -> x12, waiting for transfers between devices: 0.01 us -> 9.54 us  [swap_cores(): return lax.ppermute(array, 'core', [(0, 1), (1, 0)])]
  transfers between devices with their start and end apart: 21 -> 41, of which waited for: 5 -> 21; matrix products, arithmetic and copies ran while one was open for 5% -> 5% of each run, Pallas kernels for 0% -> 10%
where the time goes in v2:
time: 245 us; the launch traced here: 241 us
  starting transfers between devices  79.5 us (32%)
  waiting for transfers between devices  78.4 us (32%)
  Pallas kernels  62.6 us (26%)
  other arithmetic  9.74 us (4%)
  local copies, waits for them, and re-layouts  7.28 us (3%)
    ppermute x15, waiting for transfers between devices, gather_dp(): lax.ppermute(pieces[step], 'dp', [(i, (i + step) % DP) for i in range(DP)])  56.4 us
    pallas_call x1, Pallas kernels, run_forward(): pl.pallas_call(forward_kernel, in_specs=[SMEM] + [VMEM] * 3 + [ANY] * 16,...  22.1 us
    ppermute x12, starting transfers between devices, swap_cores(): return lax.ppermute(array, 'core', [(0, 1), (1, 0)])  18 us
    ppermute x15, starting transfers between devices, gather_dp(): lax.ppermute(pieces[step], 'dp', [(i, (i + step) % DP) for i in range(DP)])  17.4 us
    pallas_call x1, Pallas kernels, run_backward(): pl.pallas_call(backward_kernel, in_specs=[VMEM] * 2 + [ANY] * 8, out_spec...  11 us
    pallas_call x1, Pallas kernels, run_unpack(): pl.pallas_call(unpack_kernel, in_specs=[ANY] * 10, out_specs=[VMEM] * 2 +...  10.3 us
    ppermute x12, waiting for transfers between devices, swap_cores(): return lax.ppermute(array, 'core', [(0, 1), (1, 0)])  9.54 us
    all_to_all x1, starting transfers between devices, shards(): a_xz = lax.all_to_all(a_xz, CHIP, 0, 0, tiled=True)  7.55 us
  transfers between devices with their start and end apart: 41, of which 21 were waited for; matrix products, arithmetic and copies ran while one was open for 5% of the time, Pallas kernels for 10%

profile of v2, /device:TPU:3, one launch (start us, length us, event | category | flops | bytes accessed | tf_op | source)
XLA Modules:
  0.0 241.0 jit_solution(7609171320393585821)
XLA Ops:
  0.7 3.3 %collective-permute-start = (bf16[192,640]{1,0:T(8,128)(2,1)}, bf16[192,640]{1,0:T(8,128)(2,1)S(1)}, u32[]{:S(2)}, u32[]{:S(2)}) collective-permute-start(bf16[192,640]{1,0:T(8,128)(2,1)} %bitcast.18), channel_id=1, source_target_pairs={{0,32},{32,64},{64,96},{1,33},{33,65},{65,97},{2,34},{34,66},{66,9... | collective-permute-start | bytes 737288 | tf_op jit(solution)/shard_map/ppermute | solution.py:804
  4.6 1.6 slice_bitcast_fusion.1
  6.1 1.9 collective-permute-start.1
  8.1 1.6 collective-permute-done
  9.8 1.1 broadcast_select_fusion
  10.9 3.8 %collective-permute-start.4 = (bf16[256,640]{1,0:T(8,128)(2,1)S(1)}, bf16[256,640]{1,0:T(8,128)(2,1)S(1)}, u32[]{:S(2)}, u32[]{:S(2)}) collective-permute-start(bf16[256,640]{1,0:T(8,128)(2,1)S(1)} %get-tuple-element.150), channel_id=1, source_target_pairs={{0,24},{8,0},{16,8},{24,16},{1,25},{9,1},{17,9},{25,17},{2,26},{10... | collective-permute-start | bytes 983048 | tf_op jit(solution)/shard_map/ppermute | solution.py:810
  15.5 2.5 %collective-permute-start.5 = (bf16[448,640]{1,0:T(8,128)(2,1)S(1)}, bf16[448,640]{1,0:T(8,128)(2,1)S(1)}, u32[]{:S(2)}, u32[]{:S(2)}) collective-permute-start(bf16[448,640]{1,0:T(8,128)(2,1)S(1)} %pad_maximum_fusion.w0_h), channel_id=1, source_target_pairs={{0,4},{4,0},{1,5},{5,1},{2,6},{6,2},{3,7},{7,3},{8,12},{12,8},{9,1... | collective-permute-start | bytes 1720328 | tf_op jit(solution)/shard_map/ppermute | solution.py:777
  18.0 3.9 %collective-permute-done.4.w3_h = bf16[256,640]{1,0:T(8,128)(2,1)S(1)} collective-permute-done((bf16[256,640]{1,0:T(8,128)(2,1)S(1)}, bf16[256,640]{1,0:T(8,128)(2,1)S(1)}, u32[]{:S(2)}, u32[]{:S(2)}) %collective-permute-start.4) | collective-permute-done | bytes 327712 | tf_op jit(solution)/shard_map/ppermute | solution.py:810
  21.9 7.8 %collective-permute-start.8 = (bf16[256,640]{1,0:T(8,128)(2,1)S(1)}, bf16[256,640]{1,0:T(8,128)(2,1)S(1)}, u32[]{:S(2)}, u32[]{:S(2)}) collective-permute-start(bf16[256,640]{1,0:T(8,128)(2,1)S(1)} %collective-permute-done.4.w3_h), channel_id=1, source_target_pairs={{0,4},{4,0},{1,5},{5,1},{2,6},{6,2},{3,7},{7,3},{8,12},{12,8},{9,1... | collective-permute-start | bytes 983048 | tf_op jit(solution)/shard_map/ppermute | solution.py:777
  29.8 2.5 %collective-permute-done.2.w1_h = bf16[256,640]{1,0:T(8,128)(2,1)S(1)} collective-permute-done((bf16[256,640]{1,0:T(8,128)(2,1)S(1)}, bf16[256,640]{1,0:T(8,128)(2,1)S(1)}, u32[]{:S(2)}, u32[]{:S(2)}) %collective-permute-start.2) | collective-permute-done | bytes 327712 | tf_op jit(solution)/shard_map/ppermute | solution.py:810
  32.2 1.0 collective-permute-start.6
  33.3 1.2 collective-permute-done.6.w5_h
  35.3 22.1 %forward.1 = (f32[1,640]{1,0:T(1,128)}, bf16[768,256]{1,0:T(8,128)(2,1)}, bf16[2432,256]{1,0:T(8,128)(2,1)}, bf16[2432,256]{1,0:T(8,128)(2,1)}, bf16[768,256]{1,...) custom-call(s32[1,2]{1,0:T(1,128)} %lengths.1, ...), custom_call_target="tpu_custom_call" | custom-call | flops 8000000000 | bytes 30000000 | tf_op jit(solution)/shard_map/forward/pallas_call | solution.py:619
  58.0 4.0 %collective-permute-done.9.recv_h = bf16[192,5504]{1,0:T(8,128)(2,1)S(1)} collective-permute-done((bf16[192,5504]{1,0:T(8,128)(2,1)}, bf16[192,5504]{1,0:T(8,128)(2,1)S(1)}, u32[]{:S(2)}, u32[]{:S(2)}) %collective-permute-start.9) | collective-permute-done | bytes 2113568 | tf_op jit(solution)/shard_map/ppermute | solution.py:777
  62.0 1.6 copy-done.5
  64.3 5.4 %halves.1 = (bf16[1536,128]{1,0:T(8,128)(2,1)S(1)}, bf16[1536,128]{1,0:T(8,128)(2,1)}, bf16[1536,128]{1,0:T(8,128)(2,1)}, bf16[1536,128]{1,0:T(8,128)(2,1)}, bf16[16,768,128]{2,1,0:T(8,128)(2,1)}) custom-call(f32[1,640]{1,0:T(1,128)S(1)} %copy-done.6, bf16[192,5504]{1,0:T(8,128)(2,1)S(1)} %copy-done.5, bf16[192,5504]{1,0:T(8,128)(2,1)S(1)} %collective-permute-done.9.recv_h), custom_call_target="tpu_custom_call" | custom-call | flops 2000000000 | bytes 10000000 | tf_op jit(solution)/shard_map/halves/pallas_call | solution.py:686
  69.7 7.5 %all-to-all-start = ((bf16[16,768,128]{2,1,0:T(8,128)(2,1)}), bf16[16,768,128]{2,1,0:T(8,128)(2,1)}, u32[]{:S(2)}, u32[]{:S(2)}) async-start(bf16[16,768,128]{2,1,0:T(8,128)(2,1)} %get-tuple-element.108), calls=%async_computation | async-start | bytes 6291456 | tf_op jit(solution)/shard_map/all_to_all | solution.py:826
  77.2 1.3 collective-permute-start.10
  78.6 2.6 %collective-permute-start.11 = (bf16[1536,128]{1,0:T(8,128)(2,1)}, bf16[1536,128]{1,0:T(8,128)(2,1)}, u32[]{:S(2)}, u32[]{:S(2)}) collective-permute-start(bf16[1536,128]{1,0:T(8,128)(2,1)} %get-tuple-element.92), channel_id=1, source_target_pairs={{0,2},{1,3},{2,0},{3,1},{4,6},{5,7},{6,4},{7,5},{8,10},{9,11},{10,... | collective-permute-start | bytes 1179656 | tf_op jit(solution)/shard_map/ppermute | solution.py:783
  81.2 1.1 collective-permute-start.12
  82.3 11.0 %backward.1 = (f32[1,640]{1,0:T(1,128)}, bf16[1216,512]{1,0:T(8,128)(2,1)}, bf16[1216,512]{1,0:T(8,128)(2,1)}, bf16[192,1024]{1,0:T(8,128)(2,1)}, f32[192,640]{1,0:T(8,128)}) custom-call(f32[4,64,128]{2,1,0:T(8,128)} %constant.36.clone.tables, f32[640]{0:T(1024)} %ga.3, bf16[768,256]{1,0:T(8,128)(2,1)} %get-tuple-element.83.q_h, ...), custom_call_target="tpu_custom_call" | custom-call | flops 999999995904 | bytes 1000000000 | tf_op jit(solution)/shard_map/backward/pallas_call | solution.py:646
  93.2 2.2 collective-permute-start.20
  95.5 2.7 %collective-permute-done.11.a2 = bf16[1536,128]{1,0:T(8,128)(2,1)} collective-permute-done((bf16[1536,128]{1,0:T(8,128)(2,1)}, bf16[1536,128]{1,0:T(8,128)(2,1)}, u32[]{:S(2)}, u32[]{:S(2)}) %collective-permute-start.11) | collective-permute-done | bytes 393248 | tf_op jit(solution)/shard_map/ppermute | solution.py:783
  98.2 6.8 %project.1 = (bf16[4096,128]{1,0:T(8,128)(2,1)}, bf16[4096,128]{1,0:T(8,128)(2,1)}) custom-call(f32[1,640]{1,0:T(1,128)} %get-tuple-element.98.gain, bf16[2432,640]{1,0:T(8,128)(2,1)} %get-tuple-element.87.norm_h, bf16[1216,512]{1,0:T(8,128)(2,1)} %get-tuple-element.99.mine_h, bf16[1216,512]{1,0:T(8,128)(2,1)} %get-tuple-element.100.other_h, ...), custom_call_target="tpu_custom_call" | custom-call | flops 999999995904 | bytes 1000000000 | tf_op jit(solution)/shard_map/project/pallas_call | solution.py:670
  105.0 1.9 collective-permute-start.13
  106.9 1.6 add_convert_fusion
  108.6 0.8 collective-permute-done.13.recv
  109.7 1.0 collective-permute-start.14
  110.8 0.7 pad_maximum_fusion.3
  111.5 2.7 %collective-permute-start.22 = (bf16[256,512]{1,0:T(8,128)(2,1)}, bf16[256,512]{1,0:T(8,128)(2,1)S(1)}, u32[]{:S(2)}, u32[]{:S(2)}) collective-permute-start(bf16[256,512]{1,0:T(8,128)(2,1)} %pad_maximum_fusion.3), channel_id=1, source_target_pairs={{0,16},{8,24},{16,0},{24,8},{1,17},{9,25},{17,1},{25,9},{2,18},{10... | collective-permute-start | bytes 786440 | tf_op jit(solution)/shard_map/ppermute | solution.py:851
  115.2 2.1 collective-permute-start.15
  117.3 1.3 collective-permute-start.16
  119.3 2.4 collective-permute-start.21
  121.7 2.2 collective-permute-done.15.b2
  123.9 4.9 %collective-permute-done.16.b3 = bf16[1024,128]{1,0:T(8,128)(2,1)S(1)} collective-permute-done((bf16[1024,128]{1,0:T(8,128)(2,1)S(1)}, bf16[1024,128]{1,0:T(8,128)(2,1)S(1)}, u32[]{:S(2)}, u32[]{:S(2)}) %collective-permute-start.16) | collective-permute-done | bytes 262176 | tf_op jit(solution)/shard_map/ppermute | solution.py:783
  128.8 4.1 %first_sum.1 = (bf16[16,160,128]{2,1,0:T(8,128)(2,1)}, bf16[192,128]{1,0:T(8,128)(2,1)S(1)}, bf16[192,128]{1,0:T(8,128)(2,1)S(1)}, bf16[192,128]{1,0:T(8,128)(2,1)S(1)}, bf16[192,128]{1,0:T(8,128)(2,1)S(1)}) custom-call(bf16[1536,128]{1,0:T(8,128)(2,1)S(1)} %get-tuple-element.94.a0, bf16[1536,128]{1,0:T(8,128)(2,1)} %collective-permute-done.10.a1, ...), custom_call_target="tpu_custom_call" | custom-call | flops 1000000 | bytes 8000000 | tf_op jit(solution)/shard_map/first_sum/pallas_call | solution.py:715
  133.0 6.4 %all-to-all-start.1 = ((bf16[16,160,128]{2,1,0:T(8,128)(2,1)}), bf16[16,160,128]{2,1,0:T(8,128)(2,1)S(1)}, u32[]{:S(2)}, u32[]{:S(2)}) async-start(bf16[16,160,128]{2,1,0:T(8,128)(2,1)} %get-tuple-element.109), calls=%async_computation.1 | async-start | bytes 1310720 | tf_op jit(solution)/shard_map/all_to_all | solution.py:860
  139.5 0.9 slice.107
  140.4 1.0 convert_element_type.53
  141.4 1.0 add_convert_fusion.2
  142.4 2.4 collective-permute-start.17
  144.8 2.3 collective-permute-start.18
  147.7 1.8 collective-permute-done.18.c2
  149.6 1.3 collective-permute-done.19.c3
  150.9 1.1 second_sum.1
  152.0 6.7 %all-to-all-start.2 = ((bf16[16,208,128]{2,1,0:T(8,128)(2,1)}), bf16[16,208,128]{2,1,0:T(8,128)(2,1)S(1)}, u32[]{:S(2)}, u32[]{:S(2)}) async-start(bf16[16,208,128]{2,1,0:T(8,128)(2,1)} %get-tuple-element.116), calls=%async_computation.2 | async-start | bytes 1703936 | tf_op jit(solution)/shard_map/all_to_all | solution.py:866
  158.7 2.0 collective-permute-start.27
  160.7 1.3 collective-permute-start.28
  162.0 0.9 collective-permute-start.26
  163.6 1.5 collective-permute-done.26.d3
  165.1 2.3 collective-permute-done.25.d2
  167.9 1.5 spread.1
  169.5 4.3 %collective-permute-done.28 = bf16[64,512]{1,0:T(8,128)(2,1)S(1)} collective-permute-done((bf16[64,512]{1,0:T(8,128)(2,1)S(1)}, bf16[64,512]{1,0:T(8,128)(2,1)S(1)}, u32[]{:S(2)}, u32[]{:S(2)}) %collective-permute-start.28) | collective-permute-done | bytes 65568 | tf_op jit(solution)/shard_map/ppermute | solution.py:864
  174.5 5.2 %all-to-all-start.3 = ((bf16[16,4,144,128]{3,2,1,0:T(8,128)(2,1)}), bf16[16,4,144,128]{3,2,1,0:T(8,128)(2,1)S(1)}, u32[]{:S(2)}, u32[]{:S(2)}) async-start(bf16[16,4,144,128]{3,2,1,0:T(8,128)(2,1)} %spread.1), calls=%async_computation.3 | async-start | bytes 4718592 | tf_op jit(solution)/shard_map/all_to_all | solution.py:872
  181.2 14.3 %collective-permute-done.31.e3_h = bf16[16,208,128]{2,1,0:T(8,128)(2,1)S(1)} collective-permute-done((bf16[16,208,128]{2,1,0:T(8,128)(2,1)S(1)}, bf16[16,208,128]{2,1,0:T(8,128)(2,1)S(1)}, u32[]{:S(2)}, u32[]{:S(2)}) %collective-permute-start.31) | collective-permute-done | bytes 852000 | tf_op jit(solution)/shard_map/ppermute | solution.py:783
  195.5 1.8 collective-permute-done.30.e2_h
  197.2 0.9 copy-done.3
  198.1 22.7 %collective-permute-done.29.e1_h = bf16[16,208,128]{2,1,0:T(8,128)(2,1)} collective-permute-done((bf16[16,208,128]{2,1,0:T(8,128)(2,1)S(1)}, bf16[16,208,128]{2,1,0:T(8,128)(2,1)}, u32[]{:S(2)}, u32[]{:S(2)}) %collective-permute-start.29) | collective-permute-done | bytes 852000 | tf_op jit(solution)/shard_map/ppermute | solution.py:783
  221.7 1.2 add_convert_fusion.1
  222.8 1.3 fusion.8
  226.2 0.8 fusion.7
  227.0 2.5 %collective-permute-done.33.o1_h = bf16[16,208,128]{2,1,0:T(8,128)(2,1)S(1)} collective-permute-done((bf16[16,208,128]{2,1,0:T(8,128)(2,1)}, bf16[16,208,128]{2,1,0:T(8,128)(2,1)S(1)}, u32[]{:S(2)}, u32[]{:S(2)}) %collective-permute-start.33) | collective-permute-done | bytes 852000 | tf_op jit(solution)/shard_map/ppermute | solution.py:777
  229.5 1.0 collective-permute-done.35.o3_h
  230.5 10.3 %unpack.1 = (f32[640]{0:T(1024)}, f32[640]{0:T(1024)}, f32[640,2048]{1,0:T(8,128)}, f32[640,2048]{1,0:T(8,128)}, f32[2048,640]{1,0:T(8,128)}, /*index=5*/f32[102...) custom-call(bf16[16,208,128]{2,1,0:T(8,128)(2,1)S(1)} %all-to-all-done.2.e0_h, ...), custom_call_target="tpu_custom_call" | custom-call | bytes 30000000 | tf_op jit(solution)/shard_map/unpack/pallas_call | solution.py:754
  (109 shorter events, 12.1 us)
Async XLA Ops:
  0.6 14.8 %copy-start.7 = (bf16[1,192,640]{2,1,0:T(8,128)(2,1)S(1)}, bf16[1,192,640]{2,1,0:T(8,128)(2,1)}, u32[]{:S(2)}) copy-start(bf16[1,192,640]{2,1,0:T(8,128)(2,1)} %param.13) | copy-start | bytes 737284
  0.7 9.1 %collective-permute-start = (bf16[192,640]{1,0:T(8,128)(2,1)}, bf16[192,640]{1,0:T(8,128)(2,1)S(1)}, u32[]{:S(2)}, u32[]{:S(2)}) collective-permute-start(bf16[192,640]{1,0:T(8,128)(2,1)} %bitcast.18), channel_id=1, source_target_pairs={{0,32},{32,64},{64,96},{1,33},{33,65},{65,97},{2,34},{34,66},{66,9... | collective-permute-start | bytes 737288 | tf_op jit(solution)/shard_map/ppermute | solution.py:804
  6.1 3.6 %collective-permute-start.1 = (bf16[64,640]{1,0:T(8,128)(2,1)S(1)}, bf16[64,640]{1,0:T(8,128)(2,1)S(1)}, u32[]{:S(2)}, u32[]{:S(2)}) collective-permute-start(bf16[64,640]{1,0:T(8,128)(2,1)S(1)} %get-tuple-element.154), channel_id=1, source_target_pairs={{0,64},{32,96},{1,65},{33,97},{2,66},{34,98},{3,67},{35,99},{4,68}... | collective-permute-start | bytes 245768 | tf_op jit(solution)/shard_map/ppermute | solution.py:805
  10.9 11.0 %collective-permute-start.4 = (bf16[256,640]{1,0:T(8,128)(2,1)S(1)}, bf16[256,640]{1,0:T(8,128)(2,1)S(1)}, u32[]{:S(2)}, u32[]{:S(2)}) collective-permute-start(bf16[256,640]{1,0:T(8,128)(2,1)S(1)} %get-tuple-element.150), channel_id=1, source_target_pairs={{0,24},{8,0},{16,8},{24,16},{1,25},{9,1},{17,9},{25,17},{2,26},{10... | collective-permute-start | bytes 983048 | tf_op jit(solution)/shard_map/ppermute | solution.py:810
  14.7 15.0 %collective-permute-start.3 = (bf16[256,640]{1,0:T(8,128)(2,1)S(1)}, bf16[256,640]{1,0:T(8,128)(2,1)S(1)}, u32[]{:S(2)}, u32[]{:S(2)}) collective-permute-start(bf16[256,640]{1,0:T(8,128)(2,1)S(1)} %get-tuple-element.151), channel_id=1, source_target_pairs={{0,16},{8,24},{16,0},{24,8},{1,17},{9,25},{17,1},{25,9},{2,18},{10... | collective-permute-start | bytes 983048 | tf_op jit(solution)/shard_map/ppermute | solution.py:810
  14.7 17.5 %collective-permute-start.2 = (bf16[256,640]{1,0:T(8,128)(2,1)S(1)}, bf16[256,640]{1,0:T(8,128)(2,1)S(1)}, u32[]{:S(2)}, u32[]{:S(2)}) collective-permute-start(bf16[256,640]{1,0:T(8,128)(2,1)S(1)} %get-tuple-element.152), channel_id=1, source_target_pairs={{0,8},{8,16},{16,24},{24,0},{1,9},{9,17},{17,25},{25,1},{2,10},{10... | collective-permute-start | bytes 983048 | tf_op jit(solution)/shard_map/ppermute | solution.py:810
  15.5 19.0 %copy-start.10 = (bf16[448,640]{1,0:T(8,128)(2,1)}, bf16[448,640]{1,0:T(8,128)(2,1)S(1)}, u32[]{:S(2)}) copy-start(bf16[448,640]{1,0:T(8,128)(2,1)S(1)} %pad_maximum_fusion.w0_h) | copy-start | bytes 1720324
  15.5 17.7 %collective-permute-start.5 = (bf16[448,640]{1,0:T(8,128)(2,1)S(1)}, bf16[448,640]{1,0:T(8,128)(2,1)S(1)}, u32[]{:S(2)}, u32[]{:S(2)}) collective-permute-start(bf16[448,640]{1,0:T(8,128)(2,1)S(1)} %pad_maximum_fusion.w0_h), channel_id=1, source_target_pairs={{0,4},{4,0},{1,5},{5,1},{2,6},{6,2},{3,7},{7,3},{8,12},{12,8},{9,1... | collective-permute-start | bytes 1720328 | tf_op jit(solution)/shard_map/ppermute | solution.py:777
  21.9 12.6 %copy-start.19 = (bf16[256,640]{1,0:T(8,128)(2,1)}, bf16[256,640]{1,0:T(8,128)(2,1)S(1)}, u32[]{:S(2)}) copy-start(bf16[256,640]{1,0:T(8,128)(2,1)S(1)} %collective-permute-done.4.w3_h) | copy-start | bytes 983044
  21.9 11.3 %collective-permute-start.8 = (bf16[256,640]{1,0:T(8,128)(2,1)S(1)}, bf16[256,640]{1,0:T(8,128)(2,1)S(1)}, u32[]{:S(2)}, u32[]{:S(2)}) collective-permute-start(bf16[256,640]{1,0:T(8,128)(2,1)S(1)} %collective-permute-done.4.w3_h), channel_id=1, source_target_pairs={{0,4},{4,0},{1,5},{5,1},{2,6},{6,2},{3,7},{7,3},{8,12},{12,8},{9,1... | collective-permute-start | bytes 983048 | tf_op jit(solution)/shard_map/ppermute | solution.py:777
  29.7 4.8 %copy-start.20 = (bf16[256,640]{1,0:T(8,128)(2,1)}, bf16[256,640]{1,0:T(8,128)(2,1)S(1)}, u32[]{:S(2)}) copy-start(bf16[256,640]{1,0:T(8,128)(2,1)S(1)} %collective-permute-done.3.w2_h) | copy-start | bytes 983044
  29.7 3.6 %collective-permute-start.7 = (bf16[256,640]{1,0:T(8,128)(2,1)S(1)}, bf16[256,640]{1,0:T(8,128)(2,1)S(1)}, u32[]{:S(2)}, u32[]{:S(2)}) collective-permute-start(bf16[256,640]{1,0:T(8,128)(2,1)S(1)} %collective-permute-done.3.w2_h), channel_id=1, source_target_pairs={{0,4},{4,0},{1,5},{5,1},{2,6},{6,2},{3,7},{7,3},{8,12},{12,8},{9,1... | collective-permute-start | bytes 983048 | tf_op jit(solution)/shard_map/ppermute | solution.py:777
  32.2 2.3 copy-start.21
  32.2 2.3 collective-permute-start.6
  33.2 1.3 copy-start.18
  33.3 1.3 copy-start.22
  33.3 1.3 copy-start.23
  34.5 0.8 copy-start.24
  57.3 4.7 %collective-permute-start.9 = (bf16[192,5504]{1,0:T(8,128)(2,1)}, bf16[192,5504]{1,0:T(8,128)(2,1)S(1)}, u32[]{:S(2)}, u32[]{:S(2)}) collective-permute-start(bf16[192,5504]{1,0:T(8,128)(2,1)} %get-tuple-element.81), channel_id=1, source_target_pairs={{0,4},{4,0},{1,5},{5,1},{2,6},{6,2},{3,7},{7,3},{8,12},{12,8},{9,1... | collective-permute-start | bytes 6340616 | tf_op jit(solution)/shard_map/ppermute | solution.py:777
  62.0 1.6 copy-start.5
  69.7 59.2 %all-to-all-start = ((bf16[16,768,128]{2,1,0:T(8,128)(2,1)}), bf16[16,768,128]{2,1,0:T(8,128)(2,1)}, u32[]{:S(2)}, u32[]{:S(2)}) async-start(bf16[16,768,128]{2,1,0:T(8,128)(2,1)} %get-tuple-element.108), calls=%async_computation | async-start | bytes 6291456 | tf_op jit(solution)/shard_map/all_to_all | solution.py:826
  77.2 18.2 %collective-permute-start.10 = (bf16[1536,128]{1,0:T(8,128)(2,1)}, bf16[1536,128]{1,0:T(8,128)(2,1)}, u32[]{:S(2)}, u32[]{:S(2)}) collective-permute-start(bf16[1536,128]{1,0:T(8,128)(2,1)} %get-tuple-element.91), channel_id=1, source_target_pairs={{0,1},{1,2},{2,3},{3,0},{4,5},{5,6},{6,7},{7,4},{8,9},{9,10},{10,1... | collective-permute-start | bytes 1179656 | tf_op jit(solution)/shard_map/ppermute | solution.py:783
  78.6 19.6 %collective-permute-start.11 = (bf16[1536,128]{1,0:T(8,128)(2,1)}, bf16[1536,128]{1,0:T(8,128)(2,1)}, u32[]{:S(2)}, u32[]{:S(2)}) collective-permute-start(bf16[1536,128]{1,0:T(8,128)(2,1)} %get-tuple-element.92), channel_id=1, source_target_pairs={{0,2},{1,3},{2,0},{3,1},{4,6},{5,7},{6,4},{7,5},{8,10},{9,11},{10,... | collective-permute-start | bytes 1179656 | tf_op jit(solution)/shard_map/ppermute | solution.py:783
  81.2 17.0 %collective-permute-start.12 = (bf16[1536,128]{1,0:T(8,128)(2,1)}, bf16[1536,128]{1,0:T(8,128)(2,1)}, u32[]{:S(2)}, u32[]{:S(2)}) collective-permute-start(bf16[1536,128]{1,0:T(8,128)(2,1)} %get-tuple-element.93), channel_id=1, source_target_pairs={{0,3},{1,0},{2,1},{3,2},{4,7},{5,4},{6,5},{7,6},{8,11},{9,8},{10,9... | collective-permute-start | bytes 1179656 | tf_op jit(solution)/shard_map/ppermute | solution.py:783
  93.2 13.7 %collective-permute-start.20 = (bf16[1216,512]{1,0:T(8,128)(2,1)}, bf16[1216,512]{1,0:T(8,128)(2,1)}, u32[]{:S(2)}, u32[]{:S(2)}) collective-permute-start(bf16[1216,512]{1,0:T(8,128)(2,1)} %get-tuple-element.100.other_h), channel_id=1, source_target_pairs={{0,4},{4,0},{1,5},{5,1},{2,6},{6,2},{3,7},{7,3},{8,12},{12,8},{9,1... | collective-permute-start | bytes 3735560 | tf_op jit(solution)/shard_map/ppermute | solution.py:777
  98.2 8.7 %copy-start.9 = (bf16[1216,512]{1,0:T(8,128)(2,1)S(1)}, bf16[1216,512]{1,0:T(8,128)(2,1)}, u32[]{:S(2)}) copy-start(bf16[1216,512]{1,0:T(8,128)(2,1)} %get-tuple-element.99.mine_h) | copy-start | bytes 3735556
  105.0 4.4 %copy-start = (bf16[4096,128]{1,0:T(8,128)(2,1)S(1)}, bf16[4096,128]{1,0:T(8,128)(2,1)}, u32[]{:S(2)}) copy-start(bf16[4096,128]{1,0:T(8,128)(2,1)} %get-tuple-element.102.keep) | copy-start | bytes 3145732
  105.0 4.4 %collective-permute-start.13 = (bf16[4096,128]{1,0:T(8,128)(2,1)}, bf16[4096,128]{1,0:T(8,128)(2,1)S(1)}, u32[]{:S(2)}, u32[]{:S(2)}) collective-permute-start(bf16[4096,128]{1,0:T(8,128)(2,1)} %get-tuple-element.103), channel_id=1, source_target_pairs={{0,4},{4,0},{1,5},{5,1},{2,6},{6,2},{3,7},{7,3},{8,12},{12,8},{9,1... | collective-permute-start | bytes 3145736 | tf_op jit(solution)/shard_map/ppermute | solution.py:777
  109.7 9.6 %collective-permute-start.14 = (bf16[1024,128]{1,0:T(8,128)(2,1)S(1)}, bf16[1024,128]{1,0:T(8,128)(2,1)S(1)}, u32[]{:S(2)}, u32[]{:S(2)}) collective-permute-start(bf16[1024,128]{1,0:T(8,128)(2,1)S(1)} %get-tuple-element.105), channel_id=1, source_target_pairs={{0,1},{1,2},{2,3},{3,0},{4,5},{5,6},{6,7},{7,4},{8,9},{9,10},{10,1... | collective-permute-start | bytes 786440 | tf_op jit(solution)/shard_map/ppermute | solution.py:783
  111.5 27.9 %collective-permute-start.22 = (bf16[256,512]{1,0:T(8,128)(2,1)}, bf16[256,512]{1,0:T(8,128)(2,1)S(1)}, u32[]{:S(2)}, u32[]{:S(2)}) collective-permute-start(bf16[256,512]{1,0:T(8,128)(2,1)} %pad_maximum_fusion.3), channel_id=1, source_target_pairs={{0,16},{8,24},{16,0},{24,8},{1,17},{9,25},{17,1},{25,9},{2,18},{10... | collective-permute-start | bytes 786440 | tf_op jit(solution)/shard_map/ppermute | solution.py:851
  114.9 24.6 %collective-permute-start.23 = (bf16[256,512]{1,0:T(8,128)(2,1)}, bf16[256,512]{1,0:T(8,128)(2,1)S(1)}, u32[]{:S(2)}, u32[]{:S(2)}) collective-permute-start(bf16[256,512]{1,0:T(8,128)(2,1)} %pad_maximum_fusion.4), channel_id=1, source_target_pairs={{0,8},{8,16},{16,24},{24,0},{1,9},{9,17},{17,25},{25,1},{2,10},{10... | collective-permute-start | bytes 786440 | tf_op jit(solution)/shard_map/ppermute | solution.py:851
  115.2 8.8 %collective-permute-start.15 = (bf16[1024,128]{1,0:T(8,128)(2,1)S(1)}, bf16[1024,128]{1,0:T(8,128)(2,1)S(1)}, u32[]{:S(2)}, u32[]{:S(2)}) collective-permute-start(bf16[1024,128]{1,0:T(8,128)(2,1)S(1)} %get-tuple-element.106), channel_id=1, source_target_pairs={{0,2},{1,3},{2,0},{3,1},{4,6},{5,7},{6,4},{7,5},{8,10},{9,11},{10,... | collective-permute-start | bytes 786440 | tf_op jit(solution)/shard_map/ppermute | solution.py:783
  117.3 11.6 %collective-permute-start.16 = (bf16[1024,128]{1,0:T(8,128)(2,1)S(1)}, bf16[1024,128]{1,0:T(8,128)(2,1)S(1)}, u32[]{:S(2)}, u32[]{:S(2)}) collective-permute-start(bf16[1024,128]{1,0:T(8,128)(2,1)S(1)} %get-tuple-element.107), channel_id=1, source_target_pairs={{0,3},{1,0},{2,1},{3,2},{4,7},{5,4},{6,5},{7,6},{8,11},{9,8},{10,9... | collective-permute-start | bytes 786440 | tf_op jit(solution)/shard_map/ppermute | solution.py:783
  119.3 20.2 %collective-permute-start.21 = (bf16[256,512]{1,0:T(8,128)(2,1)}, bf16[256,512]{1,0:T(8,128)(2,1)}, u32[]{:S(2)}, u32[]{:S(2)}) collective-permute-start(bf16[256,512]{1,0:T(8,128)(2,1)} %pad_maximum_fusion.2), channel_id=1, source_target_pairs={{0,24},{8,0},{16,8},{24,16},{1,25},{9,1},{17,9},{25,17},{2,26},{10... | collective-permute-start | bytes 786440 | tf_op jit(solution)/shard_map/ppermute | solution.py:851
  133.0 17.9 %all-to-all-start.1 = ((bf16[16,160,128]{2,1,0:T(8,128)(2,1)}), bf16[16,160,128]{2,1,0:T(8,128)(2,1)S(1)}, u32[]{:S(2)}, u32[]{:S(2)}) async-start(bf16[16,160,128]{2,1,0:T(8,128)(2,1)} %get-tuple-element.109), calls=%async_computation.1 | async-start | bytes 1310720 | tf_op jit(solution)/shard_map/all_to_all | solution.py:860
  142.4 5.3 %collective-permute-start.17 = (bf16[192,128]{1,0:T(8,128)(2,1)S(1)}, bf16[192,128]{1,0:T(8,128)(2,1)S(1)}, u32[]{:S(2)}, u32[]{:S(2)}) collective-permute-start(bf16[192,128]{1,0:T(8,128)(2,1)S(1)} %get-tuple-element.111), channel_id=1, source_target_pairs={{0,1},{1,2},{2,3},{3,0},{4,5},{5,6},{6,7},{7,4},{8,9},{9,10},{10,1... | collective-permute-start | bytes 147464 | tf_op jit(solution)/shard_map/ppermute | solution.py:783
  144.8 4.7 %collective-permute-start.18 = (bf16[192,128]{1,0:T(8,128)(2,1)S(1)}, bf16[192,128]{1,0:T(8,128)(2,1)S(1)}, u32[]{:S(2)}, u32[]{:S(2)}) collective-permute-start(bf16[192,128]{1,0:T(8,128)(2,1)S(1)} %get-tuple-element.112), channel_id=1, source_target_pairs={{0,2},{1,3},{2,0},{3,1},{4,6},{5,7},{6,4},{7,5},{8,10},{9,11},{10,... | collective-permute-start | bytes 147464 | tf_op jit(solution)/shard_map/ppermute | solution.py:783
  147.1 3.7 %collective-permute-start.19 = (bf16[192,128]{1,0:T(8,128)(2,1)S(1)}, bf16[192,128]{1,0:T(8,128)(2,1)S(1)}, u32[]{:S(2)}, u32[]{:S(2)}) collective-permute-start(bf16[192,128]{1,0:T(8,128)(2,1)S(1)} %get-tuple-element.113), channel_id=1, source_target_pairs={{0,3},{1,0},{2,1},{3,2},{4,7},{5,4},{6,5},{7,6},{8,11},{9,8},{10,9... | collective-permute-start | bytes 147464 | tf_op jit(solution)/shard_map/ppermute | solution.py:783
  152.0 21.8 %all-to-all-start.2 = ((bf16[16,208,128]{2,1,0:T(8,128)(2,1)}), bf16[16,208,128]{2,1,0:T(8,128)(2,1)S(1)}, u32[]{:S(2)}, u32[]{:S(2)}) async-start(bf16[16,208,128]{2,1,0:T(8,128)(2,1)} %get-tuple-element.116), calls=%async_computation.2 | async-start | bytes 1703936 | tf_op jit(solution)/shard_map/all_to_all | solution.py:866
  158.7 15.1 %collective-permute-start.27 = (bf16[192,512]{1,0:T(8,128)(2,1)}, bf16[192,512]{1,0:T(8,128)(2,1)S(1)}, u32[]{:S(2)}, u32[]{:S(2)}) collective-permute-start(bf16[192,512]{1,0:T(8,128)(2,1)} %get-tuple-element.118), channel_id=1, source_target_pairs={{32,0},{64,32},{96,64},{33,1},{65,33},{97,65},{34,2},{66,34},{98,6... | collective-permute-start | bytes 589832 | tf_op jit(solution)/shard_map/ppermute | solution.py:863
  160.7 13.1 %collective-permute-start.28 = (bf16[64,512]{1,0:T(8,128)(2,1)S(1)}, bf16[64,512]{1,0:T(8,128)(2,1)S(1)}, u32[]{:S(2)}, u32[]{:S(2)}) collective-permute-start(bf16[64,512]{1,0:T(8,128)(2,1)S(1)} %add_convert_fusion.3), channel_id=1, source_target_pairs={{64,0},{96,32},{65,1},{97,33},{66,2},{98,34},{67,3},{99,35},{68,4}... | collective-permute-start | bytes 196616 | tf_op jit(solution)/shard_map/ppermute | solution.py:864
  162.0 3.2 %collective-permute-start.26 = (bf16[144,128]{1,0:T(8,128)(2,1)S(1)}, bf16[144,128]{1,0:T(8,128)(2,1)S(1)}, u32[]{:S(2)}, u32[]{:S(2)}) collective-permute-start(bf16[144,128]{1,0:T(8,128)(2,1)S(1)} %get-tuple-element.117.d0), channel_id=1, source_target_pairs={{0,3},{1,0},{2,1},{3,2},{4,7},{5,4},{6,5},{7,6},{8,11},{9,8},{10,9... | collective-permute-start | bytes 110600 | tf_op jit(solution)/shard_map/ppermute | solution.py:783
  162.9 4.6 %collective-permute-start.25 = (bf16[144,128]{1,0:T(8,128)(2,1)S(1)}, bf16[144,128]{1,0:T(8,128)(2,1)S(1)}, u32[]{:S(2)}, u32[]{:S(2)}) collective-permute-start(bf16[144,128]{1,0:T(8,128)(2,1)S(1)} %get-tuple-element.117.d0), channel_id=1, source_target_pairs={{0,2},{1,3},{2,0},{3,1},{4,6},{5,7},{6,4},{7,5},{8,10},{9,11},{10,... | collective-permute-start | bytes 110600 | tf_op jit(solution)/shard_map/ppermute | solution.py:783
  163.3 4.6 %collective-permute-start.24 = (bf16[144,128]{1,0:T(8,128)(2,1)S(1)}, bf16[144,128]{1,0:T(8,128)(2,1)S(1)}, u32[]{:S(2)}, u32[]{:S(2)}) collective-permute-start(bf16[144,128]{1,0:T(8,128)(2,1)S(1)} %get-tuple-element.117.d0), channel_id=1, source_target_pairs={{0,1},{1,2},{2,3},{3,0},{4,5},{5,6},{6,7},{7,4},{8,9},{9,10},{10,1... | collective-permute-start | bytes 110600 | tf_op jit(solution)/shard_map/ppermute | solution.py:783
  169.4 52.0 %copy-start.8 = (bf16[1,192,640]{2,1,0:T(8,128)(2,1)S(1)}, bf16[1,192,640]{2,1,0:T(8,128)(2,1)}, u32[]{:S(2)}) copy-start(bf16[1,192,640]{2,1,0:T(8,128)(2,1)} %param.13) | copy-start | bytes 737284
  169.4 52.0 %copy-start.14 = (bf16[64,640]{1,0:T(8,128)(2,1)S(1)}, bf16[64,640]{1,0:T(8,128)(2,1)}, u32[]{:S(2)}) copy-start(bf16[64,640]{1,0:T(8,128)(2,1)} %get-tuple-element.153) | copy-start | bytes 245764
  173.8 0.7 copy-start.15
  174.5 46.4 %all-to-all-start.3 = ((bf16[16,4,144,128]{3,2,1,0:T(8,128)(2,1)}), bf16[16,4,144,128]{3,2,1,0:T(8,128)(2,1)S(1)}, u32[]{:S(2)}, u32[]{:S(2)}) async-start(bf16[16,4,144,128]{3,2,1,0:T(8,128)(2,1)} %spread.1), calls=%async_computation.3 | async-start | bytes 4718592 | tf_op jit(solution)/shard_map/all_to_all | solution.py:872
  179.6 46.0 %copy-start.17 = (f32[640]{0:T(1024)S(1)}, f32[640]{0:T(1024)}, u32[]{:S(2)}) copy-start(f32[640]{0:T(1024)} %ga.3) | copy-start | bytes 7684
  179.6 15.8 %collective-permute-start.31 = (bf16[16,208,128]{2,1,0:T(8,128)(2,1)S(1)}, bf16[16,208,128]{2,1,0:T(8,128)(2,1)S(1)}, u32[]{:S(2)}, u32[]{:S(2)}) collective-permute-start(bf16[16,208,128]{2,1,0:T(8,128)(2,1)S(1)} %all-to-all-done.2.e0_h), channel_id=1, source_target_pairs={{0,3},{1,0},{2,1},{3,2},{4,7},{5,4},{6,5},{7,6},{8,11},{9,8},{10,9... | collective-permute-start | bytes 2555912 | tf_op jit(solution)/shard_map/ppermute | solution.py:783
  180.1 17.1 %collective-permute-start.30 = (bf16[16,208,128]{2,1,0:T(8,128)(2,1)S(1)}, bf16[16,208,128]{2,1,0:T(8,128)(2,1)S(1)}, u32[]{:S(2)}, u32[]{:S(2)}) collective-permute-start(bf16[16,208,128]{2,1,0:T(8,128)(2,1)S(1)} %all-to-all-done.2.e0_h), channel_id=1, source_target_pairs={{0,2},{1,3},{2,0},{3,1},{4,6},{5,7},{6,4},{7,5},{8,10},{9,11},{10,... | collective-permute-start | bytes 2555912 | tf_op jit(solution)/shard_map/ppermute | solution.py:783
  180.6 40.2 %collective-permute-start.29 = (bf16[16,208,128]{2,1,0:T(8,128)(2,1)S(1)}, bf16[16,208,128]{2,1,0:T(8,128)(2,1)}, u32[]{:S(2)}, u32[]{:S(2)}) collective-permute-start(bf16[16,208,128]{2,1,0:T(8,128)(2,1)S(1)} %all-to-all-done.2.e0_h), channel_id=1, source_target_pairs={{0,1},{1,2},{2,3},{3,0},{4,5},{5,6},{6,7},{7,4},{8,9},{9,10},{10,1... | collective-permute-start | bytes 2555912 | tf_op jit(solution)/shard_map/ppermute | solution.py:783
  195.5 1.8 copy-start.1
  197.2 0.9 copy-start.3
  220.9 3.3 %copy-start.13 = (bf16[640,256]{1,0:T(8,128)(2,1)S(1)}, bf16[640,256]{1,0:T(8,128)(2,1)}, u32[]{:S(2)}) copy-start(bf16[640,256]{1,0:T(8,128)(2,1)} %wk_h.3) | copy-start | bytes 983044
  220.9 4.2 %copy-start.4 = (bf16[16,208,128]{2,1,0:T(8,128)(2,1)S(1)}, bf16[16,208,128]{2,1,0:T(8,128)(2,1)}, u32[]{:S(2)}) copy-start(bf16[16,208,128]{2,1,0:T(8,128)(2,1)} %copy-done.3) | copy-start | bytes 2555908
  220.9 4.5 %copy-start.2 = (bf16[16,208,128]{2,1,0:T(8,128)(2,1)S(1)}, bf16[16,208,128]{2,1,0:T(8,128)(2,1)}, u32[]{:S(2)}) copy-start(bf16[16,208,128]{2,1,0:T(8,128)(2,1)} %copy-done.1) | copy-start | bytes 2555908
  220.9 4.8 %copy-start.11 = (f32[192,640]{1,0:T(8,128)S(1)}, f32[192,640]{1,0:T(8,128)}, u32[]{:S(2)}) copy-start(f32[192,640]{1,0:T(8,128)} %get-tuple-element.88) | copy-start | bytes 1474564
  220.9 9.7 %collective-permute-start.36 = (bf16[16,4,144,128]{3,2,1,0:T(8,128)(2,1)S(1)}, bf16[16,4,144,128]{3,2,1,0:T(8,128)(2,1)S(1)}, u32[]{:S(2)}, u32[]{:S(2)}) collective-permute-start(bf16[16,4,144,128]{3,2,1,0:T(8,128)(2,1)S(1)} %all-to-all-done.3.f_h), channel_id=1, source_target_pairs={{0,4},{4,0},{1,5},{5,1},{2,6},{6,2},{3,7},{7,3},{8,12},{12,8},{9,1... | collective-permute-start | bytes 7077896 | tf_op jit(solution)/shard_map/ppermute | solution.py:777
  222.8 3.1 %copy-start.12 = (f32[192,640]{1,0:T(8,128)S(1)}, f32[192,640]{1,0:T(8,128)}, u32[]{:S(2)}) copy-start(f32[192,640]{1,0:T(8,128)} %get-tuple-element.77) | copy-start | bytes 1474564
  224.4 2.6 %collective-permute-start.32 = (bf16[16,208,128]{2,1,0:T(8,128)(2,1)S(1)}, bf16[16,208,128]{2,1,0:T(8,128)(2,1)S(1)}, u32[]{:S(2)}, u32[]{:S(2)}) collective-permute-start(bf16[16,208,128]{2,1,0:T(8,128)(2,1)S(1)} %all-to-all-done.2.e0_h), channel_id=1, source_target_pairs={{0,4},{4,0},{1,5},{5,1},{2,6},{6,2},{3,7},{7,3},{8,12},{12,8},{9,1... | collective-permute-start | bytes 2555912 | tf_op jit(solution)/shard_map/ppermute | solution.py:777
  224.7 4.8 %collective-permute-start.33 = (bf16[16,208,128]{2,1,0:T(8,128)(2,1)}, bf16[16,208,128]{2,1,0:T(8,128)(2,1)S(1)}, u32[]{:S(2)}, u32[]{:S(2)}) collective-permute-start(bf16[16,208,128]{2,1,0:T(8,128)(2,1)} %collective-permute-done.29.e1_h), channel_id=1, source_target_pairs={{0,4},{4,0},{1,5},{5,1},{2,6},{6,2},{3,7},{7,3},{8,12},{12,8},{9,1... | collective-permute-start | bytes 2555912 | tf_op jit(solution)/shard_map/ppermute | solution.py:777
  225.0 4.5 %collective-permute-start.34 = (bf16[16,208,128]{2,1,0:T(8,128)(2,1)S(1)}, bf16[16,208,128]{2,1,0:T(8,128)(2,1)S(1)}, u32[]{:S(2)}, u32[]{:S(2)}) collective-permute-start(bf16[16,208,128]{2,1,0:T(8,128)(2,1)S(1)} %copy-done.4), channel_id=1, source_target_pairs={{0,4},{4,0},{1,5},{5,1},{2,6},{6,2},{3,7},{7,3},{8,12},{12,8},{9,1... | collective-permute-start | bytes 2555912 | tf_op jit(solution)/shard_map/ppermute | solution.py:777
  225.4 5.2 %collective-permute-start.35 = (bf16[16,208,128]{2,1,0:T(8,128)(2,1)S(1)}, bf16[16,208,128]{2,1,0:T(8,128)(2,1)S(1)}, u32[]{:S(2)}, u32[]{:S(2)}) collective-permute-start(bf16[16,208,128]{2,1,0:T(8,128)(2,1)S(1)} %copy-done.2), channel_id=1, source_target_pairs={{0,4},{4,0},{1,5},{5,1},{2,6},{6,2},{3,7},{7,3},{8,12},{12,8},{9,1... | collective-permute-start | bytes 2555912 | tf_op jit(solution)/shard_map/ppermute | solution.py:777
  (2 other events, 1.3 us)
